TPU v7x, 512 devices: a whole 4x8x8 slice. The times are simulated.
512 devices in a mesh: row: 8 (over x, core), col: 8 (over z), rep: 8 (over y).
Axes of the slice: x: 4, y: 8, z: 8, core: 2. Of those that a mesh axis runs over, the one named last changes fastest.
Arguments:
- m_tensor: bfloat16 [512, 256, 256], P('row', ('col', 'rep')), may hold values from -1 to 1
- green: bfloat16 [2, 256, 256], P(None, ('row', 'col')), may hold values from -0.375 to 0.375
- tile_mask: int32 [4, 2, 2], replicated, may hold values 0 or 1
- green_mask: int32 [2, 2, 2], replicated, may hold values 0 or 1
Outputs:
- chi_cyclic: float32 [512, 512], P('row', ('col', 'rep'))
All inputs are finite; a program needn't handle non-finite values.
Results may differ from a plain program's by a relative error of at most 0.0041.
Values may be sent and summed in bfloat16 or wider, within the bound.
No kernel may reach another device: no remote copies, remote signals or barrier semaphores. Data moves between devices by JAX's collectives and lax.ppermute only.
A program may use at most 64 MiB of HBM per device.

v0:
```python
import jax
import jax.numpy as jnp
from jax import lax
from jax.sharding import PartitionSpec as P

TILE = 128


def spread(value, axis, source):
    kept = jnp.where(lax.axis_index(axis) == source, value, 0).astype(value.dtype)
    return lax.psum(kept, axis)


def body(m_tensor, green, tile_mask, green_mask):
    row_count, mu_block, ao_count = m_tensor.shape
    groups = lax.axis_size(("col", "rep"))
    whole_green = lax.all_gather(green, ("row", "col"), axis=1, tiled=True)
    green_keep = jnp.repeat(jnp.repeat(green_mask.astype(jnp.bfloat16), TILE, axis=1), TILE, axis=2)
    whole_green = whole_green * green_keep
    occupied = whole_green[0]
    virtual = whole_green[1]
    tile_count = tile_mask.shape[0]
    ao_tiles = tile_mask.shape[1]
    row_ids = lax.axis_index("row") * row_count + jnp.arange(row_count, dtype=jnp.int32)
    row_hot = (row_ids[:, None] // TILE == jnp.arange(tile_count, dtype=jnp.int32)[None, :]).astype(
        jnp.float32
    )
    mu_ids = lax.axis_index(("col", "rep")) * mu_block + jnp.arange(mu_block, dtype=jnp.int32)
    mu_hot = (mu_ids[:, None] // TILE == jnp.arange(ao_tiles, dtype=jnp.int32)[None, :]).astype(
        jnp.float32
    )
    selected = jnp.einsum("pt,tab,ma->pmb", row_hot, tile_mask.astype(jnp.float32), mu_hot)
    keep = jnp.repeat(selected.astype(jnp.bfloat16), TILE, axis=2)
    masked = m_tensor * keep
    per_group = row_count // groups
    grouped = masked.reshape(groups, per_group, mu_block, ao_count)
    halfway = jnp.einsum(
        "airn,ns->airs",
        lax.all_to_all(grouped, ("col", "rep"), split_axis=0, concat_axis=2, tiled=True),
        virtual,
        preferred_element_type=jnp.float32,
    ).astype(jnp.bfloat16)
    product = jnp.einsum(
        "rl,airs->ails", occupied, halfway, preferred_element_type=jnp.float32
    ).astype(jnp.bfloat16)
    contracted = lax.all_to_all(product, ("col", "rep"), split_axis=2, concat_axis=0, tiled=True)
    y_flat = contracted.reshape(row_count, mu_block * ao_count)
    m_flat = masked.reshape(row_count, mu_block * ao_count)
    pair_dims = (((1,), (1,)), ((), ()))
    y_cols, m_cols = (
        lax.all_gather(y_flat, "col", axis=1, tiled=True),
        lax.all_gather(m_flat, "col", axis=1, tiled=True),
    )
    m_owner = spread(m_cols, "row", lax.axis_index("col"))
    partial_sum = lax.dot_general(y_cols, m_owner, pair_dims, preferred_element_type=jnp.float32)
    summed = lax.psum_scatter(partial_sum, "rep", scatter_dimension=1, tiled=True)
    result = lax.all_to_all(summed, "row", split_axis=0, concat_axis=0, tiled=True)
    return result


def solution(mesh):
    return jax.shard_map(
        body,
        mesh=mesh,
        in_specs=(P("row", ("col", "rep"), None), P(None, ("row", "col"), None), P(), P()),
        out_specs=P("row", ("col", "rep")),
        check_vma=False,
    )
```

profile of v0, /device:TPU:1, one launch (start us, length us, event | category | flops | bytes accessed | tf_op | source)
XLA Modules:
  0.0 256.8 jit_solution(4057546812954407058)
XLA Ops:
  6.5 0.0 all-gather.5.cloned.1.call-start
  6.6 0.0 copy-start.2
  6.6 0.7 copy-done.2
  7.2 0.2 fusion.1
  7.5 0.1 copy.15
  7.6 0.3 broadcast_in_dim.17
  8.0 0.0 copy-start
  8.0 0.1 reshape.111
  8.1 0.8 copy-done
  8.9 0.7 mul.18
  9.6 1.6 copy.21
  11.2 0.0 all-gather.5.cloned.1.call-update
  11.2 0.0 copy-start.1
  11.2 17.1 %all-to-all-start = ((bf16[64,1,4,256]{3,2,1,0:T(4,128)(2,1)}), bf16[64,1,4,256]{3,2,1,0:T(4,128)(2,1)S(1)}, u32[]{:S(2)}, u32[]{:S(2)}) async-start(bf16[64,1,4,256]{3,2,1,0:T(4,128)(2,1)} %bitcast.4), calls=%async_computation | async-start | bytes 262144 | tf_op jit(solution)/shard_map/all_to_all | solution.py:39
  28.4 0.0 copy-done.1
  28.4 0.0 copy-start.3
  28.4 44.9 %all_gather.9 = bf16[2,256,256]{2,0,1:T(2,128)(2,1)S(1)} all-gather(bf16[2,4,256]{2,0,1:T(2,128)(2,1)S(1)} %copy.16), channel_id=1, replica_groups=mesh['row'=8,'col'=8,'rep'=8] {'row','col'}, dimensions={1}, use_global_device_ids=true | all-gather | bytes 266240 | tf_op jit(solution)/shard_map/all_gather | solution.py:17
  73.3 0.0 copy-done.3
  73.3 0.6 broadcast_in_dim.19
  73.9 0.2 reshape.115
  74.1 0.0 all-to-all-done
  74.2 0.4 fusion
  74.6 0.2 copy.18
  74.8 0.5 broadcast.95
  75.3 1.4 reduce.2
  76.7 0.7 reshape.122
  77.5 10.4 %all-to-all-start.1 = ((bf16[64,2,512]{2,1,0:T(2,128)(2,1)}), bf16[64,2,512]{2,1,0:T(2,128)(2,1)S(1)}, u32[]{:S(2)}, u32[]{:S(2)}) async-start(bf16[64,2,512]{2,1,0:T(2,128)(2,1)} %reshape.122), calls=%async_computation.1 | async-start | bytes 262144 | tf_op jit(solution)/shard_map/all_to_all | solution.py:46
  87.8 0.0 all-gather.3.cloned.1.call-start
  87.9 11.5 %all-to-all-done.1 = bf16[64,2,512]{2,1,0:T(2,128)(2,1)S(1)} async-done(((bf16[64,2,512]{2,1,0:T(2,128)(2,1)}), bf16[64,2,512]{2,1,0:T(2,128)(2,1)S(1)}, u32[]{:S(2)}, u32[]{:S(2)}) %all-to-all-start.1) | async-done | bytes 131104 | tf_op jit(solution)/shard_map/all_to_all | solution.py:46
  99.4 0.1 reshape.123
  99.5 0.7 bitcast_reduce_fusion
  100.2 0.7 reshape.116
  101.0 0.0 all-gather.3.cloned.1.call-update
  101.0 0.0 all-reduce.3.cloned.1.call-start
  101.0 0.0 all-gather.5.cloned.1.call-done
  101.1 1.1 broadcast_select_fusion
  102.1 0.0 all-reduce.3.cloned.1.call-update
  102.2 1.3 dynamic-slice
  104.1 27.8 %all-gather.3.cloned.1.call-done = bf16[64,8192]{1,0:T(8,128)(2,1)} async-done(((bf16[64,1024]{1,0:T(8,128)(2,1)}), bf16[64,8192]{1,0:T(8,128)(2,1)}) %all-gather.3.cloned.1.call-update) | async-done | bytes 1048592 | tf_op jit(solution)/shard_map/all_gather | solution.py:51
  131.8 76.6 %all-reduce.3.cloned.1.call-done = bf16[64,8192]{1,0:T(8,128)(2,1)} async-done(((bf16[64,8192]{1,0:T(8,128)(2,1)}), bf16[64,8192]{1,0:T(8,128)(2,1)}) %all-reduce.3.cloned.1.call-update) | async-done | bytes 1048592 | tf_op jit(solution)/shard_map/psum | solution.py:11
  208.5 2.0 fusion.13
  210.5 22.0 %all-reduce = f32[64,64]{0,1:T(8,128)S(1)} all-reduce(f32[64,64]{0,1:T(8,128)S(1)} %fusion.13), channel_id=2, replica_groups=mesh['row'=8,'col'=8,'rep'=8] {'rep'}, use_global_device_ids=true, to_apply=%region_1.2.clone | all-reduce | flops 4096 | bytes 32768
  232.5 0.1 all_to_all.24
  232.6 17.0 %all_to_all.30 = f32[8,8,8]{1,2,0:T(8,128)S(1)} all-to-all(f32[8,8,8]{1,2,0:T(8,128)S(1)} %copy.19), channel_id=1, replica_groups=mesh['row'=8,'col'=8,'rep'=8] {'row'}, dimensions={0} | all-to-all | bytes 4096 | tf_op jit(solution)/shard_map/all_to_all | solution.py:57
  249.6 0.7 all_to_all.26
  (11 shorter events, 0.1 us)
Async XLA Ops:
  6.5 94.5 %all-gather.5.cloned.1.call-start = ((), (), s32[]{:S(2)}) async-start(), calls=%async_computation.4 | async-start | bytes 1179648 | tf_op jit(solution)/shard_map/all_gather | solution.py:52
  6.6 0.7 copy-start.2
  8.0 0.9 copy-start
  11.2 17.2 %copy-start.1 = (bf16[2,4,256]{2,1,0:T(4,128)(2,1)S(1)}, bf16[2,4,256]{2,1,0:T(4,128)(2,1)}, u32[]{:S(2)}) copy-start(bf16[2,4,256]{2,1,0:T(4,128)(2,1)} %param.5) | copy-start | bytes 12292
  11.2 62.9 %all-to-all-start = ((bf16[64,1,4,256]{3,2,1,0:T(4,128)(2,1)}), bf16[64,1,4,256]{3,2,1,0:T(4,128)(2,1)S(1)}, u32[]{:S(2)}, u32[]{:S(2)}) async-start(bf16[64,1,4,256]{3,2,1,0:T(4,128)(2,1)} %bitcast.4), calls=%async_computation | async-start | bytes 262144 | tf_op jit(solution)/shard_map/all_to_all | solution.py:39
  28.4 44.9 %copy-start.3 = (s32[2,2,2]{2,1,0:T(2,128)S(1)}, s32[2,2,2]{2,1,0:T(2,128)}, u32[]{:S(2)}) copy-start(s32[2,2,2]{2,1,0:T(2,128)} %param.7) | copy-start | bytes 100
  77.5 21.9 %all-to-all-start.1 = ((bf16[64,2,512]{2,1,0:T(2,128)(2,1)}), bf16[64,2,512]{2,1,0:T(2,128)(2,1)S(1)}, u32[]{:S(2)}, u32[]{:S(2)}) async-start(bf16[64,2,512]{2,1,0:T(2,128)(2,1)} %reshape.122), calls=%async_computation.1 | async-start | bytes 262144 | tf_op jit(solution)/shard_map/all_to_all | solution.py:46
  87.8 44.0 %all-gather.3.cloned.1.call-start = ((), (), s32[]{:S(2)}) async-start(), calls=%async_computation.3 | async-start | bytes 1179648 | tf_op jit(solution)/shard_map/all_gather | solution.py:51
  101.0 107.5 %all-reduce.3.cloned.1.call-start = ((), (), s32[]{:S(2)}) async-start(), calls=%async_computation.5 | async-start | bytes 2097152 | tf_op jit(solution)/shard_map/psum | solution.py:11
Sparse Core Ops, SparseCore 0:
  11.3 44.4 all-gather.4
  101.1 30.7 all-gather.2
  134.2 74.2 all-reduce.2
where the time goes:
time: 257 us
  waiting for transfers between devices  116 us (45%)
  blocking collectives  83.9 us (33%)
  starting transfers between devices  27.6 us (11%)
  between operations  14 us (5%)
  local copies, waits for them, and re-layouts  9.48 us (4%)
  other arithmetic  3.26 us (1%)
  matrix products  2.63 us (1%)
    psum x1, waiting for transfers between devices, spread(): return lax.psum(kept, axis)  76.6 us
    all_gather x1, blocking collectives, body(): whole_green = lax.all_gather(green, ('row', 'col'), axis=1, tiled=True)  44.9 us
    all_gather x1, waiting for transfers between devices, body(): lax.all_gather(y_flat, 'col', axis=1, tiled=True)  27.8 us
    unnamed x1, blocking collectives  22 us
    all_to_all x1, starting transfers between devices, body(): lax.all_to_all(grouped, ('col', 'rep'), split_axis=0, concat_axis=2, tile...  17.1 us
    all_to_all x1, blocking collectives, body(): lax.all_to_all(summed, 'row', split_axis=0, concat_axis=0, tiled=True)  17 us
    all_to_all x1, waiting for transfers between devices, body(): lax.all_to_all(product, ('col', 'rep'), split_axis=2, concat_axis=0, tile...  11.5 us
    all_to_all x1, starting transfers between devices, body(): lax.all_to_all(product, ('col', 'rep'), split_axis=2, concat_axis=0, tile...  10.4 us
  transfers between devices with their start and end apart: 5, of which 3 were waited for; matrix products, arithmetic and copies ran while one was open for 3% of the time, Pallas kernels for 0%

commit v1 on v0

v1 whole, which is shorter than its diff:
```python
import jax
import jax.numpy as jnp
from jax import lax
from jax.sharding import PartitionSpec as P

TILE = 128
GRID = ("col", "rep")


def body(m_tensor, green, tile_mask, green_mask):
    row_count, mu_block, ao_count = m_tensor.shape
    groups = lax.axis_size(GRID)
    rows = lax.axis_size("row")
    cells = lax.axis_size(("row", "col"))
    sent = jnp.broadcast_to(green[None], (cells,) + green.shape)
    whole = lax.all_to_all(sent, ("row", "col"), 0, 0, tiled=True)
    whole = whole.transpose(1, 0, 2, 3).reshape(2, ao_count, ao_count)
    green_keep = jnp.repeat(jnp.repeat(green_mask.astype(jnp.bfloat16), TILE, axis=1), TILE, axis=2)
    whole = whole * green_keep
    occupied, virtual = whole[0], whole[1]
    keep_two = tile_mask[
        lax.axis_index("row") * row_count // TILE, lax.axis_index(GRID) * mu_block // TILE
    ]
    keep = jnp.repeat(keep_two.astype(jnp.bfloat16), TILE)
    masked = m_tensor * keep[None, None, :]
    m_all = lax.all_gather(masked.reshape(row_count, mu_block * ao_count), "row", axis=0, tiled=True)
    mine = lax.all_to_all(masked, GRID, 0, 0, tiled=True).reshape(ao_count, ao_count)
    halfway = jnp.dot(mine, virtual, preferred_element_type=jnp.float32).astype(jnp.bfloat16)
    product = lax.dot_general(
        occupied, halfway, (((0,), (0,)), ((), ())), preferred_element_type=jnp.float32
    ).astype(jnp.bfloat16)
    contracted = lax.all_to_all(
        product.reshape(groups, mu_block, ao_count), GRID, 0, 0, tiled=True
    ).reshape(row_count, mu_block * ao_count)
    partial = lax.dot_general(
        m_all, contracted, (((1,), (1,)), ((), ())), preferred_element_type=jnp.float32
    )
    width = partial.shape[0] // groups
    pieces = lax.all_to_all(partial.reshape(groups, width, row_count), GRID, 0, 0, tiled=True)
    summed = jnp.sum(pieces, axis=0)
    blocks = summed.reshape(width, rows, row_count // rows).transpose(1, 2, 0)
    result = lax.all_to_all(blocks, "row", 0, 0, tiled=True)
    return result.reshape(row_count, width)


def solution(mesh):
    return jax.shard_map(
        body,
        mesh=mesh,
        in_specs=(P("row", ("col", "rep"), None), P(None, ("row", "col"), None), P(), P()),
        out_specs=P("row", ("col", "rep")),
        check_vma=False,
    )
```

time: 257 us -> 116 us (0.45)
  waiting for transfers between devices: 116 us -> 22.6 us
  blocking collectives: 83.9 us -> 42.9 us
  local copies, waits for them, and re-layouts: 9.48 us -> 6.11 us
  starting transfers between devices: 27.6 us -> 24.8 us
    psum x1 -> x0, waiting for transfers between devices: 76.6 us -> none  [spread(): return lax.psum(kept, axis)]
    all_gather x1 -> x0, blocking collectives: 44.9 us -> none  [body(): whole_green = lax.all_gather(green, ('row', 'col'), axis=1, tiled=True)]
    all_gather x2 -> x1, waiting for transfers between devices: 27.8 us -> 0.02 us  [body(): lax.all_gather(masked.reshape(row_count, mu_block * ao_count), 'row', axi...]
    all_to_all x1 -> x3, blocking collectives: 17 us -> 42.9 us  [the longest x1 16.2 us: body(): lax.all_to_all(product.reshape(groups, mu_block, ao_count), GRID, 0, 0, t...]
    unnamed x1 -> x0, blocking collectives: 22 us -> none
    all_to_all x2, waiting for transfers between devices: 11.5 us -> 22.6 us  [the longest x1 11.5 us: body(): lax.all_to_all(masked, GRID, 0, 0, tiled=True).reshape(ao_count, ao_count)]
    unnamed x15 -> x10, local copies, waits for them, and re-layouts: 5.67 us -> 2.56 us
    all_to_all x2, starting transfers between devices: 27.5 us -> 24.8 us  [the longest x1 17.1 us: body(): lax.all_to_all(masked, GRID, 0, 0, tiled=True).reshape(ao_count, ao_count)]
  transfers between devices with their start and end apart: 5 -> 3, of which waited for: 3 -> 2; matrix products, arithmetic and copies ran while one was open for 3% -> 3% of each run, Pallas kernels for 0% -> 0%
where the time goes in v1:
time: 116 us; the launch traced here: 115 us
  blocking collectives  42.9 us (37%)
  starting transfers between devices  24.8 us (21%)
  waiting for transfers between devices  22.6 us (19%)
  between operations  13.5 us (12%)
  local copies, waits for them, and re-layouts  6.11 us (5%)
  other arithmetic  3.12 us (3%)
  matrix products  2.04 us (2%)
    all_to_all x1, starting transfers between devices, body(): lax.all_to_all(masked, GRID, 0, 0, tiled=True).reshape(ao_count, ao_count)  17.1 us
    all_to_all x1, blocking collectives, body(): lax.all_to_all(product.reshape(groups, mu_block, ao_count), GRID, 0, 0, t...  16.2 us
    all_to_all x1, blocking collectives, body(): lax.all_to_all(partial.reshape(groups, width, row_count), GRID, 0, 0, til...  15.4 us
    all_to_all x1, waiting for transfers between devices, body(): lax.all_to_all(masked, GRID, 0, 0, tiled=True).reshape(ao_count, ao_count)  11.5 us
    all_to_all x1, blocking collectives, body(): result = lax.all_to_all(blocks, 'row', 0, 0, tiled=True)  11.2 us
    all_to_all x1, waiting for transfers between devices, body(): whole = lax.all_to_all(sent, ('row', 'col'), 0, 0, tiled=True)  11.1 us
    all_to_all x1, starting transfers between devices, body(): whole = lax.all_to_all(sent, ('row', 'col'), 0, 0, tiled=True)  7.62 us
    unnamed x10, local copies, waits for them, and re-layouts  2.56 us
  transfers between devices with their start and end apart: 3, of which 2 were waited for; matrix products, arithmetic and copies ran while one was open for 3% of the time, Pallas kernels for 0%

profile of v1, /device:TPU:1, one launch (start us, length us, event | category | flops | bytes accessed | tf_op | source)
XLA Modules:
  0.0 115.1 jit_solution(1499436031635489606)
XLA Ops:
  6.5 0.0 all-gather.2.cloned.1.call-start
  6.5 0.0 copy-start.2
  6.5 0.7 copy-done.2
  7.2 0.2 fusion.8
  7.4 0.1 broadcast_bitcast_fusion
  7.5 1.6 %broadcast_multiply_fusion = bf16[64,4,256]{2,1,0:T(4,128)(2,1)} fusion(bf16[64,4,256]{2,1,0:T(4,128)(2,1)} %param.4, bf16[256]{0:T(256)(128)(2,1)S(1)} %broadcast_bitcast_fusion), kind=kLoop, calls=%fused_computation.9 | loop fusion | flops 65536 | bytes 262656 | tf_op jit(solution)/shard_map/mul | solution.py:25
  9.1 1.6 %copy.17 = bf16[8,8,4,256]{3,1,2,0:T(8,128)(2,1)} copy(bf16[8,8,4,256]{3,2,1,0:T(4,128)(2,1)} %bitcast.9) | data formatting | bytes 262144
  10.7 0.0 all-gather.2.cloned.1.call-update
  10.7 0.0 copy-start
  10.7 17.1 %all-to-all-start.1 = ((bf16[64,4,256]{2,1,0:T(4,128)(2,1)}), bf16[64,4,256]{2,1,0:T(4,128)(2,1)S(1)}, u32[]{:S(2)}, u32[]{:S(2)}) async-start(bf16[64,4,256]{2,1,0:T(4,128)(2,1)} %broadcast_multiply_fusion), calls=%async_computation.1 | async-start | bytes 262144 | tf_op jit(solution)/shard_map/all_to_all | solution.py:27
  27.9 0.0 copy-done
  27.9 11.5 %all-to-all-done.1 = bf16[64,4,256]{2,1,0:T(4,128)(2,1)S(1)} async-done(((bf16[64,4,256]{2,1,0:T(4,128)(2,1)}), bf16[64,4,256]{2,1,0:T(4,128)(2,1)S(1)}, u32[]{:S(2)}, u32[]{:S(2)}) %all-to-all-start.1) | async-done | bytes 131104 | tf_op jit(solution)/shard_map/all_to_all | solution.py:27
  39.4 0.8 broadcast_in_dim.16
  40.3 0.0 copy-start.1
  40.3 7.6 %all-to-all-start = ((bf16[64,2,4,256]{3,1,2,0:T(2,128)(2,1)}), bf16[64,2,4,256]{3,1,2,0:T(2,128)(2,1)S(1)}, u32[]{:S(2)}, u32[]{:S(2)}) async-start(bf16[64,2,4,256]{3,1,2,0:T(2,128)(2,1)} %broadcast_in_dim.16), calls=%async_computation | async-start | bytes 524288 | tf_op jit(solution)/shard_map/all_to_all | solution.py:16
  47.9 0.0 copy-done.1
  47.9 0.1 broadcast_in_dim.17
  48.0 0.6 broadcast_in_dim.18
  48.6 0.2 reshape.35
  48.8 11.1 %all-to-all-done = bf16[64,2,4,256]{3,1,2,0:T(2,128)(2,1)S(1)} async-done(((bf16[64,2,4,256]{3,1,2,0:T(2,128)(2,1)}), bf16[64,2,4,256]{3,1,2,0:T(2,128)(2,1)S(1)}, u32[]{:S(2)}, u32[]{:S(2)}) %all-to-all-start) | async-done | bytes 262176 | tf_op jit(solution)/shard_map/all_to_all | solution.py:16
  59.9 0.3 bitcast_multiply_fusion
  60.2 0.4 fusion.9
  60.6 0.4 convolution_convert_fusion
  61.0 16.2 %all_to_all.25 = bf16[64,4,256]{2,1,0:T(4,128)(2,1)S(1)} all-to-all(bf16[64,4,256]{2,1,0:T(4,128)(2,1)S(1)} %reshape.37), channel_id=1, replica_groups=mesh['row'=8,'col'=8,'rep'=8] {'col','rep'}, dimensions={0} | all-to-all | bytes 262144 | tf_op jit(solution)/shard_map/all_to_all | solution.py:32
  77.3 0.1 reshape.41
  77.3 0.0 all-gather.2.cloned.1.call-done
  77.4 1.6 %fusion = f32[64,8,64]{2,1,0:T(8,128)S(1)} fusion(bf16[64,1024,1]{1,0,2:T(8,128)(2,1)S(1)} %reshape.41, bf16[512,1024]{1,0:T(8,128)(2,1)} %all-gather.2.cloned.1.call-done), kind=kOutput, calls=%fused_computation.2 | convolution fusion | flops 67108864 | bytes 1310720 | tf_op jit(solution)/shard_map/dot_general | solution.py:35
  79.0 0.2 reshape.44
  79.2 15.4 %all_to_all.26 = f32[64,1,512]{2,1,0:T(1,128)S(1)} all-to-all(f32[64,1,512]{2,1,0:T(1,128)S(1)} %reshape.44), channel_id=1, replica_groups=mesh['row'=8,'col'=8,'rep'=8] {'col','rep'}, dimensions={0} | all-to-all | bytes 262144 | tf_op jit(solution)/shard_map/all_to_all | solution.py:39
  94.6 0.5 broadcast.4
  95.1 0.9 reduce.2
  96.1 0.1 reshape.45
  96.2 0.1 reduce_sum.9
  96.2 0.1 reshape.39
  96.3 11.2 %all_to_all.27 = f32[8,8,8]{1,2,0:T(8,128)S(1)} all-to-all(f32[8,8,8]{1,2,0:T(8,128)S(1)} %copy.13), channel_id=1, replica_groups=mesh['row'=8,'col'=8,'rep'=8] {'row'}, dimensions={0} | all-to-all | bytes 4096 | tf_op jit(solution)/shard_map/all_to_all | solution.py:42
  107.6 0.7 reshape.40
  (7 shorter events, 0.1 us)
Async XLA Ops:
  6.5 70.8 %all-gather.2.cloned.1.call-start = ((), (), s32[]{:S(2)}) async-start(), calls=%async_computation.5 | async-start | bytes 1179648 | tf_op jit(solution)/shard_map/all_gather | solution.py:26
  6.5 0.7 copy-start.2
  10.7 17.2 %copy-start = (bf16[2,4,256]{2,1,0:T(4,128)(2,1)S(1)}, bf16[2,4,256]{2,1,0:T(4,128)(2,1)}, u32[]{:S(2)}) copy-start(bf16[2,4,256]{2,1,0:T(4,128)(2,1)} %param.5) | copy-start | bytes 12292
  10.7 28.7 %all-to-all-start.1 = ((bf16[64,4,256]{2,1,0:T(4,128)(2,1)}), bf16[64,4,256]{2,1,0:T(4,128)(2,1)S(1)}, u32[]{:S(2)}, u32[]{:S(2)}) async-start(bf16[64,4,256]{2,1,0:T(4,128)(2,1)} %broadcast_multiply_fusion), calls=%async_computation.1 | async-start | bytes 262144 | tf_op jit(solution)/shard_map/all_to_all | solution.py:27
  40.3 7.6 %copy-start.1 = (s32[2,2,2]{2,1,0:T(2,128)S(1)}, s32[2,2,2]{2,1,0:T(2,128)}, u32[]{:S(2)}) copy-start(s32[2,2,2]{2,1,0:T(2,128)} %param.7) | copy-start | bytes 100
  40.3 19.7 %all-to-all-start = ((bf16[64,2,4,256]{3,1,2,0:T(2,128)(2,1)}), bf16[64,2,4,256]{3,1,2,0:T(2,128)(2,1)S(1)}, u32[]{:S(2)}, u32[]{:S(2)}) async-start(bf16[64,2,4,256]{3,1,2,0:T(2,128)(2,1)} %broadcast_in_dim.16), calls=%async_computation | async-start | bytes 524288 | tf_op jit(solution)/shard_map/all_to_all | solution.py:16
Sparse Core Ops, SparseCore 0:
  10.8 34.5 all-gather.1

commit v2 on v1

v2 whole, which is shorter than its diff:
```python
import jax
import jax.numpy as jnp
from jax import lax
from jax.sharding import PartitionSpec as P

TILE = 128
GRID = ("col", "rep")


def swap_pairs(size):
    return [(a * size + b, b * size + a) for a in range(size) for b in range(size)]


def body(m_tensor, green, tile_mask, green_mask):
    row_count, mu_block, ao_count = m_tensor.shape
    groups = lax.axis_size(GRID)
    rows = lax.axis_size("row")
    chips = rows // 2
    halves = ao_count // TILE
    row, col = lax.axis_index("row"), lax.axis_index("col")

    own = m_tensor.reshape(row_count, mu_block, halves, TILE).transpose(0, 2, 1, 3)
    own = own.reshape(row_count, halves * mu_block, TILE)
    green_own = green.reshape(2, mu_block, halves, TILE).transpose(0, 2, 1, 3)
    green_own = green_own.reshape(2 * halves * mu_block, TILE)
    m_turned = lax.ppermute(own, ("row", "col"), swap_pairs(rows))
    green_turned = lax.ppermute(green_own, ("col", "rep"), swap_pairs(rows))

    mu_tile = lax.axis_index(GRID) * mu_block // TILE
    keep_own = jnp.repeat(tile_mask[row * row_count // TILE, mu_tile].astype(jnp.bfloat16), TILE)
    right = (m_tensor * keep_own[None, None, :]).reshape(row_count, mu_block * ao_count)
    pieces = [right]
    for step in range(1, chips):
        pairs = [(r, (r + 2 * step) % rows) for r in range(rows)]
        pieces.append(lax.ppermute(right, "row", pairs))
    near = jnp.concatenate(pieces, axis=0)
    far = lax.ppermute(near, "row", [(r, r ^ 1) for r in range(rows)])

    sent = jnp.concatenate(
        [own_part for own_part in (m_turned, jnp.broadcast_to(green_turned[None], (groups,) + green_turned.shape))],
        axis=1,
    )
    got = lax.all_to_all(sent, ("row", "rep"), 0, 0, tiled=True)
    got = got.reshape(groups, 3, halves, mu_block, TILE).transpose(1, 0, 3, 2, 4)
    got = got.reshape(3, ao_count, ao_count)
    tile_keep = jnp.repeat(jnp.repeat(tile_mask[col * row_count // TILE].astype(jnp.bfloat16), TILE, axis=0), TILE, axis=1)
    green_keep = jnp.repeat(jnp.repeat(green_mask.astype(jnp.bfloat16), TILE, axis=1), TILE, axis=2)
    mine = got[0] * tile_keep
    occupied = got[1] * green_keep[0]
    virtual = got[2] * green_keep[1]
    halfway = jnp.dot(mine, virtual, preferred_element_type=jnp.float32).astype(jnp.bfloat16)
    product = lax.dot_general(
        occupied, halfway, (((0,), (0,)), ((), ())), preferred_element_type=jnp.float32
    ).astype(jnp.bfloat16)
    contracted = lax.all_to_all(
        product.reshape(groups, mu_block, ao_count), GRID, 0, 0, tiled=True
    ).reshape(row_count, mu_block * ao_count)

    pair_dims = (((1,), (1,)), ((), ()))
    width = rows * row_count // groups
    partial = jnp.zeros((rows, row_count, row_count), jnp.float32)
    for held, core in ((near, row % 2), (far, 1 - row % 2)):
        part = lax.dot_general(held, contracted, pair_dims, preferred_element_type=jnp.float32)
        part = part.reshape(chips, row_count, row_count)
        for step in range(chips):
            block = (row // 2 - step + chips) % chips * 2 + core
            partial = lax.dynamic_update_slice(partial, part[step][None], (block, 0, 0))
    slices = lax.all_to_all(partial.reshape(groups, width, row_count), GRID, 0, 0, tiled=True)
    return jnp.sum(slices, axis=0).T


def solution(mesh):
    return jax.shard_map(
        body,
        mesh=mesh,
        in_specs=(P("row", ("col", "rep"), None), P(None, ("row", "col"), None), P(), P()),
        out_specs=P("row", ("col", "rep")),
        check_vma=False,
    )
```

time: 116 us -> 97.8 us (0.84)
  the two profiles are of different devices: /device:TPU:1 before, /device:TPU:2 now
where the time goes in v2:
time: 97.8 us; the launch traced here: 97.3 us
  starting transfers between devices  45.4 us (46%)
  waiting for transfers between devices  25.2 us (26%)
  blocking collectives  16.6 us (17%)
  local copies, waits for them, and re-layouts  5.74 us (6%)
  other arithmetic  2.82 us (3%)
    all_to_all x1, blocking collectives, body(): lax.all_to_all(partial.reshape(groups, width, row_count), GRID, 0, 0, til...  16.6 us
    ppermute x3, starting transfers between devices, body(): pieces.append(lax.ppermute(right, 'row', pairs))  15.3 us
    all_to_all x1, waiting for transfers between devices, body(): lax.all_to_all(product.reshape(groups, mu_block, ao_count), GRID, 0, 0, t...  12.7 us
    all_to_all x1, starting transfers between devices, body(): got = lax.all_to_all(sent, ('row', 'rep'), 0, 0, tiled=True)  12.6 us
    all_to_all x1, waiting for transfers between devices, body(): got = lax.all_to_all(sent, ('row', 'rep'), 0, 0, tiled=True)  12.5 us
    all_to_all x1, starting transfers between devices, body(): lax.all_to_all(product.reshape(groups, mu_block, ao_count), GRID, 0, 0, t...  8.62 us
    ppermute x1, starting transfers between devices, body(): m_turned = lax.ppermute(own, ('row', 'col'), swap_pairs(rows))  6.19 us
    ppermute x1, starting transfers between devices, body(): far = lax.ppermute(near, 'row', [(r, r ^ 1) for r in range(rows)])  2.08 us
  transfers between devices with their start and end apart: 8, of which 2 were waited for; matrix products, arithmetic and copies ran while one was open for 4% of the time, Pallas kernels for 0%

profile of v2, /device:TPU:2, one launch (start us, length us, event | category | flops | bytes accessed | tf_op | source)
XLA Modules:
  0.0 97.3 jit_solution(5223109312085218019)
XLA Ops:
  0.0 1.0 reshape.86
  1.0 6.2 %collective-permute-start.3 = (bf16[64,8,128]{2,0,1:T(8,128)(2,1)S(1)}, bf16[64,8,128]{2,0,1:T(8,128)(2,1)S(1)}, u32[]{:S(2)}, u32[]{:S(2)}) collective-permute-start(bf16[64,8,128]{2,0,1:T(8,128)(2,1)S(1)} %bitcast.85), channel_id=1, source_target_pairs={{0,0},{8,64},{16,128},{24,192},{32,256},{40,320},{48,384},{56,448}... | collective-permute-start | bytes 393224 | tf_op jit(solution)/shard_map/ppermute | solution.py:26
  7.2 0.7 collective-permute-start.4
  7.9 0.7 copy-done.1
  8.6 0.2 fusion.13
  9.0 8.2 %collective-permute-start = (bf16[64,1024]{1,0:T(8,128)(2,1)S(1)}, bf16[64,1024]{1,0:T(8,128)(2,1)S(1)}, u32[]{:S(2)}, u32[]{:S(2)}) collective-permute-start(bf16[64,1024]{1,0:T(8,128)(2,1)S(1)} %bitcast.77), channel_id=1, source_target_pairs={{0,128},{64,192},{128,256},{192,320},{256,384},{320,448},{384,0},{... | collective-permute-start | bytes 393224 | tf_op jit(solution)/shard_map/ppermute | solution.py:35
  17.2 2.5 %collective-permute-start.1 = (bf16[64,1024]{1,0:T(8,128)(2,1)S(1)}, bf16[64,1024]{1,0:T(8,128)(2,1)S(1)}, u32[]{:S(2)}, u32[]{:S(2)}) collective-permute-start(bf16[64,1024]{1,0:T(8,128)(2,1)S(1)} %bitcast.78), channel_id=1, source_target_pairs={{0,256},{64,320},{128,384},{192,448},{256,0},{320,64},{384,128},{4... | collective-permute-start | bytes 393224 | tf_op jit(solution)/shard_map/ppermute | solution.py:35
  19.7 4.5 %collective-permute-start.2 = (bf16[64,1024]{1,0:T(8,128)(2,1)S(1)}, bf16[64,1024]{1,0:T(8,128)(2,1)S(1)}, u32[]{:S(2)}, u32[]{:S(2)}) collective-permute-start(bf16[64,1024]{1,0:T(8,128)(2,1)S(1)} %bitcast.79), channel_id=1, source_target_pairs={{0,384},{64,448},{128,0},{192,64},{256,128},{320,192},{384,256},{4... | collective-permute-start | bytes 393224 | tf_op jit(solution)/shard_map/ppermute | solution.py:35
  24.3 0.1 copy.42
  24.5 0.8 pad_maximum_fusion
  25.2 12.6 %all-to-all-start = ((bf16[64,24,128]{2,1,0:T(8,128)(2,1)}), bf16[64,24,128]{2,1,0:T(8,128)(2,1)S(1)}, u32[]{:S(2)}, u32[]{:S(2)}) async-start(bf16[64,24,128]{2,1,0:T(8,128)(2,1)} %pad_maximum_fusion), calls=%async_computation | async-start | bytes 786432 | tf_op jit(solution)/shard_map/all_to_all | solution.py:43
  37.9 0.1 fusion.11
  38.0 0.1 copy.59
  38.1 0.1 broadcast_in_dim.43
  38.2 0.1 broadcast_in_dim.44
  38.3 0.1 copy.47
  38.4 0.1 broadcast_in_dim.46
  38.5 0.1 broadcast_in_dim.47
  38.6 2.1 %collective-permute-start.5 = (bf16[256,1024]{1,0:T(8,128)(2,1)S(1)}, bf16[256,1024]{1,0:T(8,128)(2,1)S(1)}, u32[]{:S(2)}, u32[]{:S(2)}) collective-permute-start(bf16[256,1024]{1,0:T(8,128)(2,1)S(1)} %constant_dynamic-update-slice_fusion), channel_id=1, source_target_pairs={{0,64},{64,0},{128,192},{192,128},{256,320},{320,256},{384,448},{4... | collective-permute-start | bytes 1572872 | tf_op jit(solution)/shard_map/ppermute | solution.py:37
  40.7 12.5 %all-to-all-done = bf16[64,24,128]{2,1,0:T(8,128)(2,1)S(1)} async-done(((bf16[64,24,128]{2,1,0:T(8,128)(2,1)}), bf16[64,24,128]{2,1,0:T(8,128)(2,1)S(1)}, u32[]{:S(2)}, u32[]{:S(2)}) %all-to-all-start) | async-done | bytes 393248 | tf_op jit(solution)/shard_map/all_to_all | solution.py:43
  53.2 0.1 copy.43
  53.3 0.1 fusion.14
  53.4 0.1 copy.44
  53.6 0.1 copy.46
  53.7 0.1 copy.48
  53.9 0.3 broadcast_in_dim.41
  54.2 0.4 convolution_convert_fusion
  54.6 0.7 reshape.83
  55.3 8.6 %all-to-all-start.1 = ((bf16[64,4,256]{2,1,0:T(4,128)(2,1)}), bf16[64,4,256]{2,1,0:T(4,128)(2,1)S(1)}, u32[]{:S(2)}, u32[]{:S(2)}) async-start(bf16[64,4,256]{2,1,0:T(4,128)(2,1)} %reshape.83), calls=%async_computation.1 | async-start | bytes 262144 | tf_op jit(solution)/shard_map/all_to_all | solution.py:55
  64.1 12.7 %all-to-all-done.1 = bf16[64,4,256]{2,1,0:T(4,128)(2,1)S(1)} async-done(((bf16[64,4,256]{2,1,0:T(4,128)(2,1)}), bf16[64,4,256]{2,1,0:T(4,128)(2,1)S(1)}, u32[]{:S(2)}, u32[]{:S(2)}) %all-to-all-start.1) | async-done | bytes 131104 | tf_op jit(solution)/shard_map/all_to_all | solution.py:55
  76.7 0.3 fusion.15
  77.0 0.3 fusion.16
  77.3 0.1 slice_bitcast_fusion
  77.4 0.1 copy.53
  77.5 0.1 slice_bitcast_fusion.4
  77.6 0.1 copy.49
  77.7 0.1 copy.50
  77.7 0.1 copy.51
  77.8 0.1 copy.52
  77.9 0.1 copy.54
  78.0 0.1 copy.55
  78.1 0.1 copy.56
  78.3 0.2 reshape.88
  78.5 16.6 %all_to_all.15 = f32[64,1,512]{2,1,0:T(1,128)S(1)} all-to-all(f32[64,1,512]{2,1,0:T(1,128)S(1)} %reshape.88), channel_id=1, replica_groups=mesh['row'=8,'col'=8,'rep'=8] {'col','rep'}, dimensions={0} | all-to-all | bytes 262144 | tf_op jit(solution)/shard_map/all_to_all | solution.py:68
  95.1 0.5 broadcast.30
  95.6 0.9 reduce.2
  96.6 0.1 reshape.89
  96.7 0.7 reduce_sum.9
  (35 shorter events, 0.4 us)
Async XLA Ops:
  1.0 6.3 %copy-start.3 = (bf16[2,4,256]{2,1,0:T(4,128)(2,1)S(1)}, bf16[2,4,256]{2,1,0:T(4,128)(2,1)}, u32[]{:S(2)}) copy-start(bf16[2,4,256]{2,1,0:T(4,128)(2,1)} %param.5) | copy-start | bytes 12292
  1.0 7.9 %copy-start = (bf16[64,4,256]{2,1,0:T(4,128)(2,1)S(1)}, bf16[64,4,256]{2,1,0:T(4,128)(2,1)}, u32[]{:S(2)}) copy-start(bf16[64,4,256]{2,1,0:T(4,128)(2,1)} %param.4) | copy-start | bytes 393220
  1.0 23.3 %collective-permute-start.3 = (bf16[64,8,128]{2,0,1:T(8,128)(2,1)S(1)}, bf16[64,8,128]{2,0,1:T(8,128)(2,1)S(1)}, u32[]{:S(2)}, u32[]{:S(2)}) collective-permute-start(bf16[64,8,128]{2,0,1:T(8,128)(2,1)S(1)} %bitcast.85), channel_id=1, source_target_pairs={{0,0},{8,64},{16,128},{24,192},{32,256},{40,320},{48,384},{56,448}... | collective-permute-start | bytes 393224 | tf_op jit(solution)/shard_map/ppermute | solution.py:26
  7.2 17.2 %collective-permute-start.4 = (bf16[16,128]{1,0:T(8,128)(2,1)S(1)}, bf16[16,128]{1,0:T(8,128)(2,1)S(1)}, u32[]{:S(2)}, u32[]{:S(2)}) collective-permute-start(bf16[16,128]{1,0:T(8,128)(2,1)S(1)} %bitcast.89), channel_id=1, source_target_pairs={{0,0},{1,8},{2,16},{3,24},{4,32},{5,40},{6,48},{7,56},{8,1},{9,9},... | collective-permute-start | bytes 12296 | tf_op jit(solution)/shard_map/ppermute | solution.py:27
  7.9 0.7 copy-start.1
  8.9 15.3 %copy-start.2 = (s32[2,2,2]{2,1,0:T(2,128)S(1)}, s32[2,2,2]{2,1,0:T(2,128)}, u32[]{:S(2)}) copy-start(s32[2,2,2]{2,1,0:T(2,128)} %param.7) | copy-start | bytes 100
  9.0 29.6 %collective-permute-start = (bf16[64,1024]{1,0:T(8,128)(2,1)S(1)}, bf16[64,1024]{1,0:T(8,128)(2,1)S(1)}, u32[]{:S(2)}, u32[]{:S(2)}) collective-permute-start(bf16[64,1024]{1,0:T(8,128)(2,1)S(1)} %bitcast.77), channel_id=1, source_target_pairs={{0,128},{64,192},{128,256},{192,320},{256,384},{320,448},{384,0},{... | collective-permute-start | bytes 393224 | tf_op jit(solution)/shard_map/ppermute | solution.py:35
  17.2 21.4 %collective-permute-start.1 = (bf16[64,1024]{1,0:T(8,128)(2,1)S(1)}, bf16[64,1024]{1,0:T(8,128)(2,1)S(1)}, u32[]{:S(2)}, u32[]{:S(2)}) collective-permute-start(bf16[64,1024]{1,0:T(8,128)(2,1)S(1)} %bitcast.78), channel_id=1, source_target_pairs={{0,256},{64,320},{128,384},{192,448},{256,0},{320,64},{384,128},{4... | collective-permute-start | bytes 393224 | tf_op jit(solution)/shard_map/ppermute | solution.py:35
  19.7 18.9 %collective-permute-start.2 = (bf16[64,1024]{1,0:T(8,128)(2,1)S(1)}, bf16[64,1024]{1,0:T(8,128)(2,1)S(1)}, u32[]{:S(2)}, u32[]{:S(2)}) collective-permute-start(bf16[64,1024]{1,0:T(8,128)(2,1)S(1)} %bitcast.79), channel_id=1, source_target_pairs={{0,384},{64,448},{128,0},{192,64},{256,128},{320,192},{384,256},{4... | collective-permute-start | bytes 393224 | tf_op jit(solution)/shard_map/ppermute | solution.py:35
  25.2 28.0 %all-to-all-start = ((bf16[64,24,128]{2,1,0:T(8,128)(2,1)}), bf16[64,24,128]{2,1,0:T(8,128)(2,1)S(1)}, u32[]{:S(2)}, u32[]{:S(2)}) async-start(bf16[64,24,128]{2,1,0:T(8,128)(2,1)} %pad_maximum_fusion), calls=%async_computation | async-start | bytes 786432 | tf_op jit(solution)/shard_map/all_to_all | solution.py:43
  38.6 38.4 %collective-permute-start.5 = (bf16[256,1024]{1,0:T(8,128)(2,1)S(1)}, bf16[256,1024]{1,0:T(8,128)(2,1)S(1)}, u32[]{:S(2)}, u32[]{:S(2)}) collective-permute-start(bf16[256,1024]{1,0:T(8,128)(2,1)S(1)} %constant_dynamic-update-slice_fusion), channel_id=1, source_target_pairs={{0,64},{64,0},{128,192},{192,128},{256,320},{320,256},{384,448},{4... | collective-permute-start | bytes 1572872 | tf_op jit(solution)/shard_map/ppermute | solution.py:37
  55.3 21.4 %all-to-all-start.1 = ((bf16[64,4,256]{2,1,0:T(4,128)(2,1)}), bf16[64,4,256]{2,1,0:T(4,128)(2,1)S(1)}, u32[]{:S(2)}, u32[]{:S(2)}) async-start(bf16[64,4,256]{2,1,0:T(4,128)(2,1)} %reshape.83), calls=%async_computation.1 | async-start | bytes 262144 | tf_op jit(solution)/shard_map/all_to_all | solution.py:55

commit v3 on v2

v3 whole, which is shorter than its diff:
```python
import jax
import jax.numpy as jnp
from jax import lax
from jax.sharding import PartitionSpec as P

TILE = 128
GRID = ("col", "rep")


def body(m_tensor, green, tile_mask, green_mask):
    row_count, mu_block, ao_count = m_tensor.shape
    groups = lax.axis_size(GRID)
    rows = lax.axis_size("row")
    chips = rows // 2
    halves = ao_count // TILE
    line = halves * mu_block
    row, col, rep = lax.axis_index("row"), lax.axis_index("col"), lax.axis_index("rep")

    own = m_tensor.reshape(row_count, mu_block, halves, TILE).transpose(0, 2, 1, 3)
    own = own.reshape(rows, row_count // rows * line, TILE)
    green_own = green.reshape(2, mu_block, halves, TILE).transpose(0, 2, 1, 3)
    green_own = green_own.reshape(1, 2 * line, TILE)
    first = jnp.concatenate([own, jnp.broadcast_to(green_own, (rows, 2 * line, TILE))], axis=1)
    first = lax.all_to_all(first, "row", 0, 0, tiled=True)
    cyclic = first[:, : row_count // rows * line].reshape(groups, line, TILE)
    shard = lax.dynamic_slice_in_dim(first[:, row_count // rows * line :], rep, 1, axis=0)
    sent = jnp.concatenate([cyclic, jnp.broadcast_to(shard, (groups, 2 * line, TILE))], axis=1)

    mu_tile = lax.axis_index(GRID) * mu_block // TILE
    keep_own = jnp.repeat(tile_mask[row * row_count // TILE, mu_tile].astype(jnp.bfloat16), TILE)
    right = (m_tensor * keep_own[None, None, :]).reshape(row_count, mu_block * ao_count)

    def along(step):
        return lax.ppermute(right, "row", [(r, (r + 2 * step) % rows) for r in range(rows)])

    right, sent = lax.optimization_barrier((right, sent))
    got = lax.all_to_all(sent, GRID, 0, 0, tiled=True)
    got = got.reshape(groups, 3, halves, mu_block, TILE)
    mine = got[:, 0].transpose(0, 2, 1, 3).reshape(ao_count, ao_count)
    whole = got[:, 1:].reshape(groups // rows, rows, 2, halves, mu_block, TILE)
    whole = whole.transpose(2, 1, 0, 4, 3, 5).reshape(2, ao_count, ao_count)
    tile_keep = jnp.repeat(jnp.repeat(tile_mask[col * row_count // TILE].astype(jnp.bfloat16), TILE, axis=0), TILE, axis=1)
    green_keep = jnp.repeat(jnp.repeat(green_mask.astype(jnp.bfloat16), TILE, axis=1), TILE, axis=2)
    mine = mine * tile_keep
    whole = whole * green_keep
    halfway = jnp.dot(mine, whole[1], preferred_element_type=jnp.float32).astype(jnp.bfloat16)
    product = lax.dot_general(
        whole[0], halfway, (((0,), (0,)), ((), ())), preferred_element_type=jnp.float32
    ).astype(jnp.bfloat16)
    near = jnp.concatenate([right] + [along(step) for step in (1, 2, 3)], axis=0)
    near, product = lax.optimization_barrier((near, product))
    far = lax.ppermute(near, "row", [(r, r ^ 1) for r in range(rows)])
    contracted = lax.all_to_all(
        product.reshape(groups, mu_block, ao_count), GRID, 0, 0, tiled=True
    ).reshape(row_count, mu_block * ao_count)

    pair_dims = (((1,), (1,)), ((), ()))
    width = rows * row_count // groups
    partial = jnp.zeros((chips, 2, row_count, row_count), jnp.float32)
    for held, core in ((near, row % 2), (far, 1 - row % 2)):
        part = lax.dot_general(held, contracted, pair_dims, preferred_element_type=jnp.float32)
        part = part.reshape(chips, row_count, row_count)
        for step in range(chips):
            chip = (row // 2 - step + chips) % chips
            partial = lax.dynamic_update_slice(partial, part[step][None, None], (chip, core, 0, 0))
    slices = lax.all_to_all(partial.reshape(groups, width, row_count), GRID, 0, 0, tiled=True)
    return jnp.sum(slices, axis=0).T


def solution(mesh):
    return jax.shard_map(
        body,
        mesh=mesh,
        in_specs=(P("row", ("col", "rep"), None), P(None, ("row", "col"), None), P(), P()),
        out_specs=P("row", ("col", "rep")),
        check_vma=False,
    )
```

time: 97.8 us -> 92.5 us (0.946)
  waiting for transfers between devices: 25.2 us -> 20 us
  starting transfers between devices: 45.4 us -> 43.2 us
  other arithmetic: 2.82 us -> 4.5 us
    ppermute x5 -> x3, starting transfers between devices: 22.1 us -> 9.82 us  [along(): lax.ppermute(right, 'row', [(r, (r + 2 * step) % rows) for r in range(row...]
    all_to_all x1 -> x2, starting transfers between devices: 12.6 us -> 21.5 us  [the longest x1 12.2 us: body(): got = lax.all_to_all(sent, GRID, 0, 0, tiled=True)]
    all_to_all x1 -> x2, waiting for transfers between devices: 12.5 us -> 6.84 us  [the longest x1 4.02 us: body(): first = lax.all_to_all(first, 'row', 0, 0, tiled=True)]
    ppermute x5 -> x3, waiting for transfers between devices: 0.01 us -> 2.5 us  [along(): lax.ppermute(right, 'row', [(r, (r + 2 * step) % rows) for r in range(row...]
    all_to_all x1, waiting for transfers between devices: 12.7 us -> 10.6 us  [body(): lax.all_to_all(product.reshape(groups, mu_block, ao_count), GRID, 0, 0, t...]
    concatenate x1 -> x3, other arithmetic: 0.78 us -> 2.41 us  [the longest x1 1.58 us: body(): jnp.concatenate([own, jnp.broadcast_to(green_own, (rows, 2 * line, TILE))...]
    all_to_all x1, starting transfers between devices: 8.62 us -> 9.89 us  [body(): lax.all_to_all(product.reshape(groups, mu_block, ao_count), GRID, 0, 0, t...]
    slice x13 -> x2, local copies, waits for them, and re-layouts: 1.08 us -> 0.01 us  [the longest x1 0.01 us: body(): cyclic = first[:, :row_count // rows * line].reshape(groups, line, TILE)]
  transfers between devices with their start and end apart: 8 -> 7, of which waited for: 2 -> 4; matrix products, arithmetic and copies ran while one was open for 4% -> 3% of each run, Pallas kernels for 0% -> 0%
where the time goes in v3:
time: 92.5 us; the launch traced here: 92 us
  starting transfers between devices  43.2 us (47%)
  waiting for transfers between devices  20 us (22%)
  blocking collectives  16.6 us (18%)
  local copies, waits for them, and re-layouts  6.38 us (7%)
  other arithmetic  4.5 us (5%)
  matrix products  0.96 us (1%)
    all_to_all x1, blocking collectives, body(): lax.all_to_all(partial.reshape(groups, width, row_count), GRID, 0, 0, til...  16.6 us
    all_to_all x1, starting transfers between devices, body(): got = lax.all_to_all(sent, GRID, 0, 0, tiled=True)  12.2 us
    all_to_all x1, waiting for transfers between devices, body(): lax.all_to_all(product.reshape(groups, mu_block, ao_count), GRID, 0, 0, t...  10.6 us
    all_to_all x1, starting transfers between devices, body(): lax.all_to_all(product.reshape(groups, mu_block, ao_count), GRID, 0, 0, t...  9.89 us
    ppermute x3, starting transfers between devices, along(): lax.ppermute(right, 'row', [(r, (r + 2 * step) % rows) for r in range(row...  9.82 us
    all_to_all x1, starting transfers between devices, body(): first = lax.all_to_all(first, 'row', 0, 0, tiled=True)  9.33 us
    all_to_all x1, waiting for transfers between devices, body(): first = lax.all_to_all(first, 'row', 0, 0, tiled=True)  4.02 us
    all_to_all x1, waiting for transfers between devices, body(): got = lax.all_to_all(sent, GRID, 0, 0, tiled=True)  2.82 us
  transfers between devices with their start and end apart: 7, of which 4 were waited for; matrix products, arithmetic and copies ran while one was open for 3% of the time, Pallas kernels for 0%

profile of v3, /device:TPU:2, one launch (start us, length us, event | category | flops | bytes accessed | tf_op | source)
XLA Modules:
  0.0 92.0 jit_solution(18275320643123808079)
XLA Ops:
  0.0 0.7 broadcast_in_dim.37
  0.7 1.6 %pad_maximum_fusion.2 = bf16[8,80,128]{2,1,0:T(8,128)(2,1)} fusion(bf16[8,16,128]{2,1,0:T(8,128)(2,1)S(1)} %broadcast_in_dim.37, bf16[8,64,128]{2,1,0:T(8,128)(2,1)} %bitcast.79), kind=kLoop, calls=%fused_computation.6 | loop fusion | flops 327680 | bytes 327680 | tf_op jit(solution)/shard_map/concatenate | solution.py:23
  2.3 9.3 %all-to-all-start = ((bf16[8,80,128]{2,1,0:T(8,128)(2,1)}), bf16[8,80,128]{2,1,0:T(8,128)(2,1)S(1)}, u32[]{:S(2)}, u32[]{:S(2)}) async-start(bf16[8,80,128]{2,1,0:T(8,128)(2,1)} %pad_maximum_fusion.2), calls=%async_computation | async-start | bytes 327680 | tf_op jit(solution)/shard_map/all_to_all | solution.py:24
  11.6 0.7 copy-done.1
  12.3 0.2 fusion.8
  12.6 4.0 %all-to-all-done = bf16[8,80,128]{2,1,0:T(8,128)(2,1)S(1)} async-done(((bf16[8,80,128]{2,1,0:T(8,128)(2,1)}), bf16[8,80,128]{2,1,0:T(8,128)(2,1)S(1)}, u32[]{:S(2)}, u32[]{:S(2)}) %all-to-all-start) | async-done | bytes 163872 | tf_op jit(solution)/shard_map/all_to_all | solution.py:24
  16.7 0.8 pad_maximum_fusion.1
  17.5 12.2 %all-to-all-start.1 = ((bf16[64,24,128]{2,1,0:T(8,128)(2,1)}), bf16[64,24,128]{2,1,0:T(8,128)(2,1)S(1)}, u32[]{:S(2)}, u32[]{:S(2)}) async-start(bf16[64,24,128]{2,1,0:T(8,128)(2,1)} %pad_maximum_fusion.1), calls=%async_computation.1 | async-start | bytes 786432 | tf_op jit(solution)/shard_map/all_to_all | solution.py:37
  29.7 2.0 %collective-permute-start = (bf16[64,1024]{1,0:T(8,128)(2,1)S(1)}, bf16[64,1024]{1,0:T(8,128)(2,1)S(1)}, u32[]{:S(2)}, u32[]{:S(2)}) collective-permute-start(bf16[64,1024]{1,0:T(8,128)(2,1)S(1)} %bitcast.83), channel_id=1, source_target_pairs={{0,128},{64,192},{128,256},{192,320},{256,384},{320,448},{384,0},{... | collective-permute-start | bytes 393224 | tf_op jit(solution)/shard_map/ppermute | solution.py:34
  31.8 5.3 %collective-permute-start.1 = (bf16[64,1024]{1,0:T(8,128)(2,1)S(1)}, bf16[64,1024]{1,0:T(8,128)(2,1)S(1)}, u32[]{:S(2)}, u32[]{:S(2)}) collective-permute-start(bf16[64,1024]{1,0:T(8,128)(2,1)S(1)} %bitcast.84), channel_id=1, source_target_pairs={{0,256},{64,320},{128,384},{192,448},{256,0},{320,64},{384,128},{4... | collective-permute-start | bytes 393224 | tf_op jit(solution)/shard_map/ppermute | solution.py:34
  37.1 2.5 %collective-permute-start.2 = (bf16[64,1024]{1,0:T(8,128)(2,1)S(1)}, bf16[64,1024]{1,0:T(8,128)(2,1)S(1)}, u32[]{:S(2)}, u32[]{:S(2)}) collective-permute-start(bf16[64,1024]{1,0:T(8,128)(2,1)S(1)} %bitcast.85), channel_id=1, source_target_pairs={{0,384},{64,448},{128,0},{192,64},{256,128},{320,192},{384,256},{4... | collective-permute-start | bytes 393224 | tf_op jit(solution)/shard_map/ppermute | solution.py:34
  39.6 0.7 copy-done.2
  40.3 0.6 broadcast_in_dim.41
  40.9 0.2 reshape.79
  41.1 0.1 fusion.6
  41.2 0.1 copy.48
  41.3 0.1 broadcast_in_dim.42
  41.4 0.1 broadcast_in_dim.43
  41.5 2.5 %collective-permute-done.2 = bf16[64,1024]{1,0:T(8,128)(2,1)S(1)} collective-permute-done((bf16[64,1024]{1,0:T(8,128)(2,1)S(1)}, bf16[64,1024]{1,0:T(8,128)(2,1)S(1)}, u32[]{:S(2)}, u32[]{:S(2)}) %collective-permute-start.2) | collective-permute-done | bytes 131104 | tf_op jit(solution)/shard_map/ppermute | solution.py:34
  44.0 2.8 %all-to-all-done.1 = bf16[64,24,128]{2,1,0:T(8,128)(2,1)S(1)} async-done(((bf16[64,24,128]{2,1,0:T(8,128)(2,1)}), bf16[64,24,128]{2,1,0:T(8,128)(2,1)S(1)}, u32[]{:S(2)}, u32[]{:S(2)}) %all-to-all-start.1) | async-done | bytes 393248 | tf_op jit(solution)/shard_map/all_to_all | solution.py:37
  46.8 0.1 copy.36
  46.9 0.3 copy.58
  47.2 0.2 reshape.77
  47.4 0.1 fusion.5
  47.5 0.1 copy.39
  47.7 0.4 convolution_convert_fusion
  48.1 0.7 reshape.80
  48.8 9.9 %all-to-all-start.2 = ((bf16[64,4,256]{2,1,0:T(4,128)(2,1)}), bf16[64,4,256]{2,1,0:T(4,128)(2,1)S(1)}, u32[]{:S(2)}, u32[]{:S(2)}) async-start(bf16[64,4,256]{2,1,0:T(4,128)(2,1)} %reshape.80), calls=%async_computation.2 | async-start | bytes 262144 | tf_op jit(solution)/shard_map/all_to_all | solution.py:53
  58.8 1.9 %collective-permute-start.3 = (bf16[256,1024]{1,0:T(8,128)(2,1)S(1)}, bf16[256,1024]{1,0:T(8,128)(2,1)S(1)}, u32[]{:S(2)}, u32[]{:S(2)}) collective-permute-start(bf16[256,1024]{1,0:T(8,128)(2,1)S(1)} %pad_maximum_fusion), channel_id=1, source_target_pairs={{0,64},{64,0},{128,192},{192,128},{256,320},{320,256},{384,448},{4... | collective-permute-start | bytes 1572872 | tf_op jit(solution)/shard_map/ppermute | solution.py:52
  60.7 10.6 %all-to-all-done.2 = bf16[64,4,256]{2,1,0:T(4,128)(2,1)S(1)} async-done(((bf16[64,4,256]{2,1,0:T(4,128)(2,1)}), bf16[64,4,256]{2,1,0:T(4,128)(2,1)S(1)}, u32[]{:S(2)}, u32[]{:S(2)}) %all-to-all-start.2) | async-done | bytes 131104 | tf_op jit(solution)/shard_map/all_to_all | solution.py:53
  71.4 0.3 fusion.9
  71.7 0.1 slice_bitcast_fusion.11
  71.7 0.1 copy.40
  71.8 0.1 copy.41
  71.9 0.1 copy.42
  72.0 0.1 copy.43
  72.2 0.3 fusion.10
  72.5 0.1 slice_bitcast_fusion.7
  72.6 0.1 copy.44
  72.6 0.1 copy.45
  72.7 0.1 copy.46
  72.8 0.1 copy.47
  73.0 0.2 reshape.84
  73.2 16.6 %all_to_all.20 = f32[64,1,512]{2,1,0:T(1,128)S(1)} all-to-all(f32[64,1,512]{2,1,0:T(1,128)S(1)} %reshape.84), channel_id=1, replica_groups=mesh['row'=8,'col'=8,'rep'=8] {'col','rep'}, dimensions={0} | all-to-all | bytes 262144 | tf_op jit(solution)/shard_map/all_to_all | solution.py:66
  89.7 0.5 broadcast.15
  90.2 0.9 %reduce.2 = f32[64,512]{1,0:T(8,128)S(1)} reduce(f32[64,1,512]{2,1,0:T(1,128)S(1)} %all_to_all.20, f32[]{:T(128)} %broadcast.15), dimensions={1}, to_apply=%all_to_all.15.reduce_sub_computation | reduce | bytes 262148 | tf_op jit(solution)/shard_map/all_to_all | solution.py:66
  91.2 0.1 reshape.85
  91.3 0.7 reduce_sum.9
  (29 shorter events, 0.5 us)
Async XLA Ops:
  2.3 10.3 %copy-start = (bf16[64,4,256]{2,1,0:T(4,128)(2,1)S(1)}, bf16[64,4,256]{2,1,0:T(4,128)(2,1)}, u32[]{:S(2)}) copy-start(bf16[64,4,256]{2,1,0:T(4,128)(2,1)} %param.4) | copy-start | bytes 393220
  2.3 14.4 %all-to-all-start = ((bf16[8,80,128]{2,1,0:T(8,128)(2,1)}), bf16[8,80,128]{2,1,0:T(8,128)(2,1)S(1)}, u32[]{:S(2)}, u32[]{:S(2)}) async-start(bf16[8,80,128]{2,1,0:T(8,128)(2,1)} %pad_maximum_fusion.2), calls=%async_computation | async-start | bytes 327680 | tf_op jit(solution)/shard_map/all_to_all | solution.py:24
  11.6 0.7 copy-start.1
  17.5 29.3 %all-to-all-start.1 = ((bf16[64,24,128]{2,1,0:T(8,128)(2,1)}), bf16[64,24,128]{2,1,0:T(8,128)(2,1)S(1)}, u32[]{:S(2)}, u32[]{:S(2)}) async-start(bf16[64,24,128]{2,1,0:T(8,128)(2,1)} %pad_maximum_fusion.1), calls=%async_computation.1 | async-start | bytes 786432 | tf_op jit(solution)/shard_map/all_to_all | solution.py:37
  29.7 11.7 %collective-permute-start = (bf16[64,1024]{1,0:T(8,128)(2,1)S(1)}, bf16[64,1024]{1,0:T(8,128)(2,1)S(1)}, u32[]{:S(2)}, u32[]{:S(2)}) collective-permute-start(bf16[64,1024]{1,0:T(8,128)(2,1)S(1)} %bitcast.83), channel_id=1, source_target_pairs={{0,128},{64,192},{128,256},{192,320},{256,384},{320,448},{384,0},{... | collective-permute-start | bytes 393224 | tf_op jit(solution)/shard_map/ppermute | solution.py:34
  31.8 9.7 %collective-permute-start.1 = (bf16[64,1024]{1,0:T(8,128)(2,1)S(1)}, bf16[64,1024]{1,0:T(8,128)(2,1)S(1)}, u32[]{:S(2)}, u32[]{:S(2)}) collective-permute-start(bf16[64,1024]{1,0:T(8,128)(2,1)S(1)} %bitcast.84), channel_id=1, source_target_pairs={{0,256},{64,320},{128,384},{192,448},{256,0},{320,64},{384,128},{4... | collective-permute-start | bytes 393224 | tf_op jit(solution)/shard_map/ppermute | solution.py:34
  37.1 6.9 %collective-permute-start.2 = (bf16[64,1024]{1,0:T(8,128)(2,1)S(1)}, bf16[64,1024]{1,0:T(8,128)(2,1)S(1)}, u32[]{:S(2)}, u32[]{:S(2)}) collective-permute-start(bf16[64,1024]{1,0:T(8,128)(2,1)S(1)} %bitcast.85), channel_id=1, source_target_pairs={{0,384},{64,448},{128,0},{192,64},{256,128},{320,192},{384,256},{4... | collective-permute-start | bytes 393224 | tf_op jit(solution)/shard_map/ppermute | solution.py:34
  39.6 0.7 copy-start.2
  48.8 22.6 %all-to-all-start.2 = ((bf16[64,4,256]{2,1,0:T(4,128)(2,1)}), bf16[64,4,256]{2,1,0:T(4,128)(2,1)S(1)}, u32[]{:S(2)}, u32[]{:S(2)}) async-start(bf16[64,4,256]{2,1,0:T(4,128)(2,1)} %reshape.80), calls=%async_computation.2 | async-start | bytes 262144 | tf_op jit(solution)/shard_map/all_to_all | solution.py:53
  58.8 13.4 %collective-permute-start.3 = (bf16[256,1024]{1,0:T(8,128)(2,1)S(1)}, bf16[256,1024]{1,0:T(8,128)(2,1)S(1)}, u32[]{:S(2)}, u32[]{:S(2)}) collective-permute-start(bf16[256,1024]{1,0:T(8,128)(2,1)S(1)} %pad_maximum_fusion), channel_id=1, source_target_pairs={{0,64},{64,0},{128,192},{192,128},{256,320},{320,256},{384,448},{4... | collective-permute-start | bytes 1572872 | tf_op jit(solution)/shard_map/ppermute | solution.py:52

commit v4 on v3

v4 whole, which is shorter than its diff:
```python
import jax
import jax.numpy as jnp
import numpy as np
from jax import lax
from jax.experimental import pallas as pl
from jax.experimental.pallas import tpu as pltpu
from jax.sharding import PartitionSpec as P

TILE = 128
COST_F = 10**10
COST_A = 5 * 10**9
COST_1 = 1
GRID = ("col", "rep")
LINE = 8
BF16 = jnp.bfloat16
F32 = jnp.float32
VMEM = pl.BlockSpec(memory_space=pltpu.VMEM)
SMEM = pl.BlockSpec(memory_space=pltpu.SMEM)
NN = (((1,), (0,)), ((), ()))
NT = (((1,), (1,)), ((), ()))
TN = (((0,), (0,)), ((), ()))


def held(array):
    return pltpu.with_memory_space_constraint(array, pltpu.VMEM)


def dot(left, right, dims=NN):
    return lax.dot_general(left, right, dims, preferred_element_type=F32)


def pick(index):
    index = np.asarray(index)
    return jnp.asarray(index[:, None] == np.arange(index.size)[None, :], BF16)


def orders(groups):
    size = groups * LINE
    row = np.arange(size)
    half, place = row // (size // 2), row % (size // 2)
    block, inner = place // 4, place % 4
    natural = block * LINE + half * 4 + inner
    turned = (block % 8 * 8 + block // 8) * LINE + half * 4 + inner
    part, func = row // groups, row % groups
    return natural, turned, func * LINE + part % 2 * 4 + part // 2


def first_kernel(tile_ref, green_ref, m_ref, shard_ref, out_ref):
    tile, mu_tile = lax.axis_index("row") // 2, lax.axis_index("col") // 4
    green_tile = lax.axis_index("row") // 4
    length = m_ref.shape[1]

    def halves(count, low, high):
        line = lax.broadcasted_iota(jnp.int32, (count, TILE), 0) % LINE
        return jnp.where(line < 4, low.astype(F32), high.astype(F32))

    keep = halves(length, tile_ref[mu_tile, 0, tile], tile_ref[mu_tile, 1, tile])
    for k in range(out_ref.shape[0]):
        out_ref[k, :length] = (m_ref[k].astype(F32) * keep).astype(BF16)
    keep_green = jnp.concatenate(
        [halves(LINE, green_ref[w, green_tile, 0], green_ref[w, green_tile, 1]) for w in range(2)], axis=0
    )
    shard = (shard_ref[...].astype(F32) * keep_green).astype(BF16)
    for k in range(out_ref.shape[0]):
        out_ref[k, length:] = shard


def second_kernel(got_ref, out_ref):
    rows = got_ref.shape[0]
    groups = out_ref.shape[0]
    length = groups // rows * LINE
    out_ref[:, :LINE] = got_ref[:, :length].reshape(groups, LINE, TILE)
    shard = got_ref[lax.axis_index("rep"), length:]
    out_ref[:, LINE:] = jnp.broadcast_to(shard[None], (groups,) + shard.shape)


def product_kernel(natural_ref, turned_ref, got_ref, out_ref):
    groups = got_ref.shape[0]
    size = groups * LINE
    side = size // 2
    got = got_ref[...]
    m_part = got[:, :LINE].reshape(size, TILE)
    o_part = got[:, LINE : 2 * LINE].reshape(size, TILE)
    v_part = got[:, 2 * LINE :].reshape(size, TILE)
    natural = natural_ref[...]
    turned = turned_ref[...]

    def square(rows):
        rows = rows.astype(BF16)
        return jnp.concatenate([rows[:side], rows[side:]], axis=1)

    virtual = square(dot(turned, v_part))
    mine = square(dot(natural, m_part))
    occupied = square(dot(turned, o_part))
    halfway = dot(mine, virtual).astype(BF16)
    wide = dot(occupied, natural[:side] + natural[side:]).astype(BF16)
    product = dot(wide, halfway, TN)
    line = lax.broadcasted_iota(jnp.int32, (size, TILE), 0) % LINE
    out = jnp.where(line < 4, product[:, :TILE], product[:, TILE:]).astype(BF16)
    out_ref[...] = out.reshape(groups, LINE, TILE)


def near_kernel(order_ref, y_ref, near_ref, out_ref, flat_ref):
    count = y_ref.shape[0]
    picked = dot(order_ref[...], y_ref[...].reshape(count * LINE, TILE)).astype(BF16)
    flat = jnp.concatenate([picked[b * count : (b + 1) * count] for b in range(LINE)], axis=1)
    flat_ref[...] = flat
    place(flat, near_ref, out_ref, lax.axis_index("row") % 2)


def far_kernel(flat_ref, far_ref, part_ref, out_ref):
    out_ref[...] = part_ref[...]
    place(flat_ref[...], far_ref, out_ref, 1 - lax.axis_index("row") % 2)


def place(flat, held_ref, out_ref, parity):
    count = flat.shape[0]
    chip = lax.axis_index("row") // 2
    part = dot(held_ref[...], flat, NT)
    for step in range(4):
        rows = part[step * count : (step + 1) * count]
        wide = jnp.concatenate([rows[: count // 2], rows[count // 2 :]], axis=1)
        block = lax.rem(chip - step + 4, 4) * 2 + parity
        start = pl.multiple_of(block * (count // 2), count // 2)
        out_ref[pl.ds(start, count // 2), :] = wide


def gather_kernel(*refs):
    count = refs[0].shape[0]
    for step, ref in enumerate(refs[:-1]):
        refs[-1][step * count : (step + 1) * count] = ref[...]


def cost(flops):
    return pl.CostEstimate(flops=flops, bytes_accessed=0, transcendentals=0)


def sum_kernel(got_ref, out_ref):
    size = got_ref.shape[0]
    total = jnp.sum(got_ref[...].reshape(size // 8, 8, TILE), axis=0)
    total = total[:4] + total[4:]
    out_ref[...] = jnp.concatenate([total[:, :64], total[:, 64:]], axis=0)


def body(m_tensor, green, tile_mask, green_mask):
    row_count, mu_block, ao_count = m_tensor.shape
    groups = lax.axis_size(GRID)
    rows = lax.axis_size("row")
    halves = ao_count // TILE
    line = halves * mu_block
    row = lax.axis_index("row")
    natural, turned, flat_order = (pick(order) for order in orders(groups))

    own = m_tensor.reshape(row_count, mu_block, halves, TILE).transpose(0, 2, 1, 3)
    own = own.reshape(rows, row_count // rows * line, TILE)
    green_own = green.reshape(2, mu_block, halves, TILE).transpose(0, 2, 1, 3)
    green_own = green_own.reshape(2 * line, TILE)
    first = pl.pallas_call(
        first_kernel,
        out_shape=pltpu.VMEM((rows, row_count // rows * line + 2 * line, TILE), BF16),
        in_specs=[SMEM, SMEM, VMEM, VMEM],
        out_specs=VMEM,
    )(tile_mask.transpose(1, 2, 0), green_mask, own, green_own)
    first = lax.all_to_all(first, "row", 0, 0, tiled=True)
    sent = pl.pallas_call(
        second_kernel,
        out_shape=pltpu.VMEM((groups, 3 * line, TILE), BF16),
        in_specs=[VMEM],
        out_specs=VMEM,
    )(held(first))

    mu_tile = lax.axis_index(GRID) * mu_block // TILE
    keep_own = jnp.repeat(tile_mask[row * row_count // TILE, mu_tile].astype(BF16), TILE)
    right = m_tensor * keep_own[None, None, :]
    right = right.reshape(rows, 2, row_count // rows // 2, mu_block * ao_count).transpose(1, 0, 2, 3)
    right = right.reshape(row_count, mu_block * ao_count)

    def along(step):
        return lax.ppermute(right, "row", [(r, (r + 2 * step) % rows) for r in range(rows)])

    right, sent = lax.optimization_barrier((right, sent))
    got = lax.all_to_all(sent, GRID, 0, 0, tiled=True)
    product = pl.pallas_call(
        product_kernel,
        out_shape=pltpu.VMEM((groups, line, TILE), BF16),
        in_specs=[VMEM, VMEM, VMEM],
        out_specs=VMEM,
        cost_estimate=cost(COST_1),
    )(held(natural), held(turned), held(got))
    near = pl.pallas_call(
        gather_kernel,
        out_shape=pltpu.VMEM((4 * row_count, mu_block * ao_count), BF16),
        in_specs=[VMEM] * 4,
        out_specs=VMEM,
        cost_estimate=cost(COST_F),
    )(held(right), *[held(along(step)) for step in (1, 2, 3)])
    far = lax.ppermute(near, "row", [(r, r ^ 1) for r in range(rows)])
    contracted = lax.all_to_all(product, GRID, 0, 0, tiled=True)
    partial, flat = pl.pallas_call(
        near_kernel,
        out_shape=(pltpu.VMEM((groups * 4, TILE), F32), pltpu.VMEM((row_count, mu_block * ao_count), BF16)),
        in_specs=[VMEM, VMEM, VMEM],
        out_specs=(VMEM, VMEM),
        cost_estimate=cost(COST_A),
    )(held(flat_order), held(contracted), held(near))
    partial = pl.pallas_call(
        far_kernel,
        out_shape=pltpu.VMEM((groups * 4, TILE), F32),
        in_specs=[VMEM, VMEM, VMEM],
        out_specs=VMEM,
    )(held(flat), held(far), held(partial))
    slices = lax.all_to_all(partial.reshape(groups, 4, TILE), GRID, 0, 0, tiled=True)
    result = pl.pallas_call(
        sum_kernel,
        out_shape=jax.ShapeDtypeStruct((8, row_count), F32),
        in_specs=[VMEM],
        out_specs=VMEM,
    )(held(slices.reshape(groups * 4, TILE)))
    return result.T


def solution(mesh):
    return jax.shard_map(
        body,
        mesh=mesh,
        in_specs=(P("row", ("col", "rep"), None), P(None, ("row", "col"), None), P(), P()),
        out_specs=P("row", ("col", "rep")),
        check_vma=False,
    )
```

time: 92.5 us -> 85.2 us (0.921)
  Pallas kernels: 0 us -> 6.09 us
  local copies, waits for them, and re-layouts: 6.38 us -> 0.91 us
  other arithmetic: 4.5 us -> 0.25 us
  starting transfers between devices: 43.2 us -> 39 us
  waiting for transfers between devices: 20 us -> 21.7 us
  matrix products: 0.96 us -> 0 us
    pallas_call x0 -> x7, Pallas kernels: none -> 6.09 us  [the longest x1 1.8 us: body(): pl.pallas_call(product_kernel, out_shape=pltpu.VMEM((groups, line, TILE),...]
    all_to_all x1, waiting for transfers between devices: 2.82 us -> 7.24 us  [body(): got = lax.all_to_all(sent, GRID, 0, 0, tiled=True)]
    all_to_all x1, starting transfers between devices: 9.89 us -> 5.48 us  [body(): contracted = lax.all_to_all(product, GRID, 0, 0, tiled=True)]
    ppermute x3, waiting for transfers between devices: 2.5 us -> 0.01 us  [along(): lax.ppermute(right, 'row', [(r, (r + 2 * step) % rows) for r in range(row...]
    concatenate x3 -> x0, other arithmetic: 2.41 us -> none  [the longest x1 1.58 us: body(): jnp.concatenate([own, jnp.broadcast_to(green_own, (rows, 2 * line, TILE))...]
    broadcast_in_dim x8 -> x0, local copies, waits for them, and re-layouts: 1.55 us -> none  [the longest x1 0.69 us: body(): jnp.broadcast_to(green_own, (rows, 2 * line, TILE))]
    reshape x5 -> x3, local copies, waits for them, and re-layouts: 1.32 us -> 0.14 us  [the longest x2 0.11 us: body(): right.reshape(rows, 2, row_count // rows // 2, mu_block * ao_count)]
    unnamed x10, local copies, waits for them, and re-layouts: 1.67 us -> 0.7 us
  transfers between devices with their start and end apart: 7 -> 7, of which waited for: 4 -> 3; matrix products, arithmetic and copies ran while one was open for 3% -> 1% of each run, Pallas kernels for 0% -> 3%
where the time goes in v4:
time: 85.2 us; the launch traced here: 84.6 us
  starting transfers between devices  39 us (46%)
  waiting for transfers between devices  21.7 us (25%)
  blocking collectives  16.5 us (19%)
  Pallas kernels  6.09 us (7%)
  local copies, waits for them, and re-layouts  0.91 us (1%)
    all_to_all x1, blocking collectives, body(): lax.all_to_all(partial.reshape(groups, 4, TILE), GRID, 0, 0, tiled=True)  16.5 us
    all_to_all x1, starting transfers between devices, body(): got = lax.all_to_all(sent, GRID, 0, 0, tiled=True)  12.3 us
    all_to_all x1, waiting for transfers between devices, body(): contracted = lax.all_to_all(product, GRID, 0, 0, tiled=True)  10.6 us
    ppermute x3, starting transfers between devices, along(): lax.ppermute(right, 'row', [(r, (r + 2 * step) % rows) for r in range(row...  9.82 us
    all_to_all x1, starting transfers between devices, body(): first = lax.all_to_all(first, 'row', 0, 0, tiled=True)  9.33 us
    all_to_all x1, waiting for transfers between devices, body(): got = lax.all_to_all(sent, GRID, 0, 0, tiled=True)  7.24 us
    all_to_all x1, starting transfers between devices, body(): contracted = lax.all_to_all(product, GRID, 0, 0, tiled=True)  5.48 us
    all_to_all x1, waiting for transfers between devices, body(): first = lax.all_to_all(first, 'row', 0, 0, tiled=True)  3.89 us
  transfers between devices with their start and end apart: 7, of which 3 were waited for; matrix products, arithmetic and copies ran while one was open for 1% of the time, Pallas kernels for 3%

profile of v4, /device:TPU:2, one launch (start us, length us, event | category | flops | bytes accessed | tf_op | source)
XLA Modules:
  0.0 84.6 jit_solution(9086277556360921262)
XLA Ops:
  0.0 1.6 %shard_map.73 = bf16[8,80,128]{2,1,0:T(8,128)(2,1)} custom-call(s32[2,2,4]{2,1,0:T(2,128)} %bitcast.23, s32[2,2,2]{2,1,0:T(2,128)} %green_ref.1, bf16[8,64,128]{2,1,0:T(8,128)(2,1)} %bitcast.21, bf16[16,128]{1,0:T(8,128)(2,1)} %bitcast.24), custom_call_target="tpu_custom_call" | custom-call | tf_op jit(solution)/shard_map/pallas_call | solution.py:158
  1.6 0.0 copy-start.3
  1.6 9.3 %all-to-all-start = ((bf16[8,80,128]{2,1,0:T(8,128)(2,1)}), bf16[8,80,128]{2,1,0:T(8,128)(2,1)S(1)}, u32[]{:S(2)}, u32[]{:S(2)}) async-start(bf16[8,80,128]{2,1,0:T(8,128)(2,1)} %shard_map.73), calls=%async_computation | async-start | bytes 327680 | tf_op jit(solution)/shard_map/all_to_all | solution.py:164
  11.0 0.0 copy-start.4
  11.0 0.7 copy-done.4
  11.7 0.2 fusion
  11.8 0.1 broadcast_bitcast_fusion
  11.9 0.0 copy-done.3
  11.9 0.1 broadcast_multiply_fusion
  12.0 0.1 reshape.26
  12.1 3.9 %all-to-all-done.got_ref = bf16[8,80,128]{2,1,0:T(8,128)(2,1)S(1)} async-done(((bf16[8,80,128]{2,1,0:T(8,128)(2,1)}), bf16[8,80,128]{2,1,0:T(8,128)(2,1)S(1)}, u32[]{:S(2)}, u32[]{:S(2)}) %all-to-all-start) | async-done | bytes 163872 | tf_op jit(solution)/shard_map/all_to_all | solution.py:164
  16.0 0.0 copy-start.1
  16.0 0.8 shard_map.74
  16.8 0.0 copy-start
  16.8 12.3 %all-to-all-start.1 = ((bf16[64,24,128]{2,1,0:T(8,128)(2,1)}), bf16[64,24,128]{2,1,0:T(8,128)(2,1)S(1)}, u32[]{:S(2)}, u32[]{:S(2)}) async-start(bf16[64,24,128]{2,1,0:T(8,128)(2,1)} %shard_map.74), calls=%async_computation.1 | async-start | bytes 786432 | tf_op jit(solution)/shard_map/all_to_all | solution.py:182
  29.2 3.4 %collective-permute-start.2 = (bf16[64,1024]{1,0:T(8,128)(2,1)S(1)}, bf16[64,1024]{1,0:T(8,128)(2,1)S(1)}, u32[]{:S(2)}, u32[]{:S(2)}) collective-permute-start(bf16[64,1024]{1,0:T(8,128)(2,1)S(1)} %reshape.27.refs_0_), channel_id=1, source_target_pairs={{0,384},{64,448},{128,0},{192,64},{256,128},{320,192},{384,256},{4... | collective-permute-start | bytes 393224 | tf_op jit(solution)/shard_map/ppermute | solution.py:179
  32.5 2.0 %collective-permute-start.1 = (bf16[64,1024]{1,0:T(8,128)(2,1)S(1)}, bf16[64,1024]{1,0:T(8,128)(2,1)S(1)}, u32[]{:S(2)}, u32[]{:S(2)}) collective-permute-start(bf16[64,1024]{1,0:T(8,128)(2,1)S(1)} %reshape.27.refs_0_), channel_id=1, source_target_pairs={{0,256},{64,320},{128,384},{192,448},{256,0},{320,64},{384,128},{4... | collective-permute-start | bytes 393224 | tf_op jit(solution)/shard_map/ppermute | solution.py:179
  34.6 4.4 %collective-permute-start = (bf16[64,1024]{1,0:T(8,128)(2,1)S(1)}, bf16[64,1024]{1,0:T(8,128)(2,1)S(1)}, u32[]{:S(2)}, u32[]{:S(2)}) collective-permute-start(bf16[64,1024]{1,0:T(8,128)(2,1)S(1)} %reshape.27.refs_0_), channel_id=1, source_target_pairs={{0,128},{64,192},{128,256},{192,320},{256,384},{320,448},{384,0},{... | collective-permute-start | bytes 393224 | tf_op jit(solution)/shard_map/ppermute | solution.py:179
  39.0 7.2 %all-to-all-done.1.got_ref = bf16[64,24,128]{2,1,0:T(8,128)(2,1)S(1)} async-done(((bf16[64,24,128]{2,1,0:T(8,128)(2,1)}), bf16[64,24,128]{2,1,0:T(8,128)(2,1)S(1)}, u32[]{:S(2)}, u32[]{:S(2)}) %all-to-all-start.1) | async-done | bytes 393248 | tf_op jit(solution)/shard_map/all_to_all | solution.py:182
  46.2 0.0 copy-done.1
  46.2 0.0 copy-done
  46.2 1.8 %shard_map.75 = bf16[64,8,128]{2,1,0:T(8,128)(2,1)} custom-call(bf16[512,512]{1,0:T(8,128)(2,1)S(1)} %copy-done.1, bf16[512,512]{1,0:T(8,128)(2,1)S(1)} %copy-done, bf16[64,24,128]{2,1,0:T(8,128)(2,1)S(1)} %all-to-all-done.1.got_ref), custom_call_target="tpu_custom_call" | custom-call | flops 1 | tf_op jit(solution)/shard_map/pallas_call | solution.py:183
  48.0 5.5 %all-to-all-start.2 = ((bf16[64,8,128]{2,1,0:T(8,128)(2,1)}), bf16[64,8,128]{2,1,0:T(8,128)(2,1)S(1)}, u32[]{:S(2)}, u32[]{:S(2)}) async-start(bf16[64,8,128]{2,1,0:T(8,128)(2,1)} %shard_map.75), calls=%async_computation.2 | async-start | bytes 262144 | tf_op jit(solution)/shard_map/all_to_all | solution.py:198
  53.5 0.0 copy-start.2
  53.6 0.0 collective-permute-done.2.refs_3_
  53.6 0.0 collective-permute-done.1.refs_2_
  53.6 0.0 collective-permute-done.refs_1_
  53.6 2.1 %collective-permute-start.3 = (bf16[256,1024]{1,0:T(8,128)(2,1)S(1)}, bf16[256,1024]{1,0:T(8,128)(2,1)S(1)}, u32[]{:S(2)}, u32[]{:S(2)}) collective-permute-start(bf16[256,1024]{1,0:T(8,128)(2,1)S(1)} %shard_map.76.near_ref), channel_id=1, source_target_pairs={{0,64},{64,0},{128,192},{192,128},{256,320},{320,256},{384,448},{4... | collective-permute-start | bytes 1572872 | tf_op jit(solution)/shard_map/ppermute | solution.py:197
  55.7 10.6 %all-to-all-done.2.y_ref = bf16[64,8,128]{2,1,0:T(8,128)(2,1)S(1)} async-done(((bf16[64,8,128]{2,1,0:T(8,128)(2,1)}), bf16[64,8,128]{2,1,0:T(8,128)(2,1)S(1)}, u32[]{:S(2)}, u32[]{:S(2)}) %all-to-all-start.2) | async-done | bytes 131104 | tf_op jit(solution)/shard_map/all_to_all | solution.py:198
  66.3 0.0 copy-done.2
  66.3 0.8 shard_map.77
  67.0 0.0 collective-permute-done.3.far_ref
  67.0 0.4 shard_map.78
  67.4 16.5 %all_to_all.20 = f32[64,4,128]{2,1,0:T(4,128)S(1)} all-to-all(f32[64,4,128]{2,1,0:T(4,128)S(1)} %bitcast.19), channel_id=1, replica_groups=mesh['row'=8,'col'=8,'rep'=8] {'col','rep'}, dimensions={0} | all-to-all | bytes 262144 | tf_op jit(solution)/shard_map/all_to_all | solution.py:212
  83.9 0.7 shard_map.79
  (3 shorter events, 0.1 us)
Async XLA Ops:
  1.6 10.3 %copy-start.3 = (bf16[64,4,256]{2,1,0:T(4,128)(2,1)S(1)}, bf16[64,4,256]{2,1,0:T(4,128)(2,1)}, u32[]{:S(2)}) copy-start(bf16[64,4,256]{2,1,0:T(4,128)(2,1)} %param.7) | copy-start | bytes 393220
  1.6 14.4 %all-to-all-start = ((bf16[8,80,128]{2,1,0:T(8,128)(2,1)}), bf16[8,80,128]{2,1,0:T(8,128)(2,1)S(1)}, u32[]{:S(2)}, u32[]{:S(2)}) async-start(bf16[8,80,128]{2,1,0:T(8,128)(2,1)} %shard_map.73), calls=%async_computation | async-start | bytes 327680 | tf_op jit(solution)/shard_map/all_to_all | solution.py:164
  11.0 0.7 copy-start.4
  16.0 30.2 %copy-start.1 = (bf16[512,512]{1,0:T(8,128)(2,1)S(1)}, bf16[512,512]{1,0:T(8,128)(2,1)}, u32[]{:S(2)}) copy-start(bf16[512,512]{1,0:T(8,128)(2,1)} %constant.49.clone.natural_ref) | copy-start | bytes 1572868
  16.8 29.4 %copy-start = (bf16[512,512]{1,0:T(8,128)(2,1)S(1)}, bf16[512,512]{1,0:T(8,128)(2,1)}, u32[]{:S(2)}) copy-start(bf16[512,512]{1,0:T(8,128)(2,1)} %constant.50.clone.turned_ref) | copy-start | bytes 1572868
  16.8 29.4 %all-to-all-start.1 = ((bf16[64,24,128]{2,1,0:T(8,128)(2,1)}), bf16[64,24,128]{2,1,0:T(8,128)(2,1)S(1)}, u32[]{:S(2)}, u32[]{:S(2)}) async-start(bf16[64,24,128]{2,1,0:T(8,128)(2,1)} %shard_map.74), calls=%async_computation.1 | async-start | bytes 786432 | tf_op jit(solution)/shard_map/all_to_all | solution.py:182
  29.2 24.4 %collective-permute-start.2 = (bf16[64,1024]{1,0:T(8,128)(2,1)S(1)}, bf16[64,1024]{1,0:T(8,128)(2,1)S(1)}, u32[]{:S(2)}, u32[]{:S(2)}) collective-permute-start(bf16[64,1024]{1,0:T(8,128)(2,1)S(1)} %reshape.27.refs_0_), channel_id=1, source_target_pairs={{0,384},{64,448},{128,0},{192,64},{256,128},{320,192},{384,256},{4... | collective-permute-start | bytes 393224 | tf_op jit(solution)/shard_map/ppermute | solution.py:179
  32.5 21.0 %collective-permute-start.1 = (bf16[64,1024]{1,0:T(8,128)(2,1)S(1)}, bf16[64,1024]{1,0:T(8,128)(2,1)S(1)}, u32[]{:S(2)}, u32[]{:S(2)}) collective-permute-start(bf16[64,1024]{1,0:T(8,128)(2,1)S(1)} %reshape.27.refs_0_), channel_id=1, source_target_pairs={{0,256},{64,320},{128,384},{192,448},{256,0},{320,64},{384,128},{4... | collective-permute-start | bytes 393224 | tf_op jit(solution)/shard_map/ppermute | solution.py:179
  34.6 19.0 %collective-permute-start = (bf16[64,1024]{1,0:T(8,128)(2,1)S(1)}, bf16[64,1024]{1,0:T(8,128)(2,1)S(1)}, u32[]{:S(2)}, u32[]{:S(2)}) collective-permute-start(bf16[64,1024]{1,0:T(8,128)(2,1)S(1)} %reshape.27.refs_0_), channel_id=1, source_target_pairs={{0,128},{64,192},{128,256},{192,320},{256,384},{320,448},{384,0},{... | collective-permute-start | bytes 393224 | tf_op jit(solution)/shard_map/ppermute | solution.py:179
  48.0 18.2 %all-to-all-start.2 = ((bf16[64,8,128]{2,1,0:T(8,128)(2,1)}), bf16[64,8,128]{2,1,0:T(8,128)(2,1)S(1)}, u32[]{:S(2)}, u32[]{:S(2)}) async-start(bf16[64,8,128]{2,1,0:T(8,128)(2,1)} %shard_map.75), calls=%async_computation.2 | async-start | bytes 262144 | tf_op jit(solution)/shard_map/all_to_all | solution.py:198
  53.5 12.7 %copy-start.2 = (bf16[512,512]{1,0:T(8,128)(2,1)S(1)}, bf16[512,512]{1,0:T(8,128)(2,1)}, u32[]{:S(2)}) copy-start(bf16[512,512]{1,0:T(8,128)(2,1)} %constant.51.clone.order_ref) | copy-start | bytes 1572868
  53.6 13.4 %collective-permute-start.3 = (bf16[256,1024]{1,0:T(8,128)(2,1)S(1)}, bf16[256,1024]{1,0:T(8,128)(2,1)S(1)}, u32[]{:S(2)}, u32[]{:S(2)}) collective-permute-start(bf16[256,1024]{1,0:T(8,128)(2,1)S(1)} %shard_map.76.near_ref), channel_id=1, source_target_pairs={{0,64},{64,0},{128,192},{192,128},{256,320},{320,256},{384,448},{4... | collective-permute-start | bytes 1572872 | tf_op jit(solution)/shard_map/ppermute | solution.py:197

commit v5 on v4

v5 whole, which is shorter than its diff:
```python
import jax
import jax.numpy as jnp
import numpy as np
from jax import lax
from jax.experimental import pallas as pl
from jax.experimental.pallas import tpu as pltpu
from jax.sharding import PartitionSpec as P

TILE = 128
FIRST = (4, 4)
SECOND = (4, 4)
THIRD = (4, 4)
ROWS = 1
COST_F = 10**10
COST_A = 10**9
COST_1 = 1
COST_G = 10**10
GRID = ("col", "rep")
LINE = 8
BF16 = jnp.bfloat16
F32 = jnp.float32
VMEM = pl.BlockSpec(memory_space=pltpu.VMEM)
SMEM = pl.BlockSpec(memory_space=pltpu.SMEM)
NN = (((1,), (0,)), ((), ()))
NT = (((1,), (1,)), ((), ()))
TN = (((0,), (0,)), ((), ()))


def held(array):
    return pltpu.with_memory_space_constraint(array, pltpu.VMEM)


def dot(left, right, dims=NN):
    return lax.dot_general(left, right, dims, preferred_element_type=F32)


def pick(index):
    index = np.asarray(index)
    return jnp.asarray(index[:, None] == np.arange(index.size)[None, :], BF16)


def peers(side, start):
    order = [
        (start[0] + i) % side * side + (start[1] + j) % side for i in range(side) for j in range(side)
    ]
    return order, np.argsort(order)


def orders(groups):
    side = int(round(groups**0.5))
    size = groups * LINE
    first, first_place = peers(side, FIRST)
    _, second_place = peers(side, SECOND)
    row = np.arange(size)
    half, place = row // (size // 2), row % (size // 2)
    block, inner = place // 4, place % 4
    natural = first_place[block] * LINE + half * 4 + inner
    turned = first_place[block % side * side + block // side] * LINE + half * 4 + inner
    spread = second_place[block] * LINE + half * 4 + inner
    part, func = row // groups, row % groups
    flat = second_place[np.asarray(first)[func]] * LINE + part % 2 * 4 + part // 2
    return natural, turned, spread, flat


def first_kernel(tile_ref, green_ref, m_ref, shard_ref, out_ref):
    tile, mu_tile = lax.axis_index("row") // 2, lax.axis_index("col") // 4
    green_tile = lax.axis_index("row") // 4
    length = m_ref.shape[1]

    def halves(count, low, high):
        line = lax.broadcasted_iota(jnp.int32, (count, TILE), 0) % LINE
        return jnp.where(line < 4, low.astype(F32), high.astype(F32))

    keep = halves(length, tile_ref[mu_tile, 0, tile], tile_ref[mu_tile, 1, tile])
    for k in range(out_ref.shape[0]):
        out_ref[k, :length] = (m_ref[k ^ ROWS].astype(F32) * keep).astype(BF16)
    keep_green = jnp.concatenate(
        [halves(LINE, green_ref[w, green_tile, 0], green_ref[w, green_tile, 1]) for w in range(2)], axis=0
    )
    shard = (shard_ref[...].astype(F32) * keep_green).astype(BF16)
    for k in range(out_ref.shape[0]):
        out_ref[k, length:] = shard


def second_kernel(got_ref, out_ref):
    rows = got_ref.shape[0]
    groups = out_ref.shape[0]
    length = groups // rows * LINE
    each = groups // rows
    for k in range(rows):
        out_ref[k * each : (k + 1) * each, :LINE] = got_ref[k ^ ROWS, :length].reshape(each, LINE, TILE)
    shard = got_ref[lax.axis_index("rep") ^ ROWS, length:]
    out_ref[:, LINE:] = jnp.broadcast_to(shard[None], (groups,) + shard.shape)


def product_kernel(natural_ref, turned_ref, spread_ref, got_ref, out_ref):
    groups = got_ref.shape[0]
    size = groups * LINE
    side = size // 2
    got = got_ref[...]
    m_part = got[:, :LINE].reshape(size, TILE)
    o_part = got[:, LINE : 2 * LINE].reshape(size, TILE)
    v_part = got[:, 2 * LINE :].reshape(size, TILE)
    natural = natural_ref[...]
    turned = turned_ref[...]

    def square(rows):
        rows = rows.astype(BF16)
        return jnp.concatenate([rows[:side], rows[side:]], axis=1)

    virtual = square(dot(turned, v_part))
    mine = square(dot(natural, m_part))
    occupied = square(dot(turned, o_part))
    halfway = dot(mine, virtual).astype(BF16)
    spread = spread_ref[...]
    wide = dot(occupied, spread[:side] + spread[side:]).astype(BF16)
    product = dot(wide, halfway, TN)
    line = lax.broadcasted_iota(jnp.int32, (size, TILE), 0) % LINE
    out = jnp.where(line < 4, product[:, :TILE], product[:, TILE:]).astype(BF16)
    out_ref[...] = out.reshape(groups, LINE, TILE)


def pair_kernel(order_ref, y_ref, held_ref, out_ref):
    count = y_ref.shape[0]
    half = count // 2
    picked = dot(order_ref[...], y_ref[...].reshape(count * LINE, TILE)).astype(BF16)
    flat = jnp.concatenate([picked[b * count : (b + 1) * count] for b in range(LINE)], axis=1)
    chip, core = lax.axis_index("row") // 2, lax.axis_index("row") % 2
    part = dot(held_ref[...], flat, NT)
    for step in range(4):
        for other in range(2):
            rows = part[(step * 2 + other) * count :][:count]
            wide = jnp.concatenate([rows[:half], rows[half:]], axis=1)
            block = lax.rem(chip - step + 4, 4) * 2 + lax.rem(core + other, 2)
            block = lax.rem(block + 8 - THIRD[0], 8)
            cut = THIRD[1] * 4
            wide = jnp.concatenate([wide[cut:], wide[:cut]], axis=0)
            out_ref[pl.ds(pl.multiple_of(block * half, half), half), :] = wide


def gather_kernel(*refs):
    count = refs[0].shape[0]
    for step, ref in enumerate(refs[:-1]):
        refs[-1][step * count : (step + 1) * count] = ref[...]


def cost(flops):
    return pl.CostEstimate(flops=flops, bytes_accessed=0, transcendentals=0)


def sum_kernel(got_ref, out_ref):
    size = got_ref.shape[0]
    total = jnp.sum(got_ref[...].reshape(size // 8, 8, TILE), axis=0)
    total = total[:4] + total[4:]
    out_ref[...] = jnp.concatenate([total[:, :64], total[:, 64:]], axis=0)


def exchange(array, start):
    order, _ = peers(lax.axis_size("col"), start)
    return lax.all_to_all(array, GRID, 0, 0, tiled=True, axis_index_groups=[order])


def body(m_tensor, green, tile_mask, green_mask):
    row_count, mu_block, ao_count = m_tensor.shape
    groups = lax.axis_size(GRID)
    rows = lax.axis_size("row")
    halves = ao_count // TILE
    line = halves * mu_block
    row = lax.axis_index("row")
    natural, turned, spread, flat_order = (pick(order) for order in orders(groups))

    own = m_tensor.reshape(row_count, mu_block, halves, TILE).transpose(0, 2, 1, 3)
    own = own.reshape(rows, row_count // rows * line, TILE)
    green_own = green.reshape(2, mu_block, halves, TILE).transpose(0, 2, 1, 3)
    green_own = green_own.reshape(2 * line, TILE)
    first = pl.pallas_call(
        first_kernel,
        out_shape=pltpu.VMEM((rows, row_count // rows * line + 2 * line, TILE), BF16),
        in_specs=[SMEM, SMEM, VMEM, VMEM],
        out_specs=VMEM,
    )(tile_mask.transpose(1, 2, 0), green_mask, own, green_own)
    order = [[k ^ ROWS for k in range(rows)]]
    first = lax.all_to_all(first, "row", 0, 0, tiled=True, axis_index_groups=order)
    sent = pl.pallas_call(
        second_kernel,
        out_shape=pltpu.VMEM((groups, 3 * line, TILE), BF16),
        in_specs=[VMEM],
        out_specs=VMEM,
    )(held(first))

    mu_tile = lax.axis_index(GRID) * mu_block // TILE
    keep_own = jnp.repeat(tile_mask[row * row_count // TILE, mu_tile].astype(BF16), TILE)
    right = m_tensor * keep_own[None, None, :]
    right = right.reshape(rows, 2, row_count // rows // 2, mu_block * ao_count).transpose(1, 0, 2, 3)
    right = right.reshape(row_count, mu_block * ao_count)

    def gathered(parts, flops):
        return pl.pallas_call(
            gather_kernel,
            out_shape=pltpu.VMEM((sum(part.shape[0] for part in parts), parts[0].shape[1]), BF16),
            in_specs=[VMEM] * len(parts),
            out_specs=VMEM,
            cost_estimate=cost(flops),
        )(*[held(part) for part in parts])

    other = lax.ppermute(right, "row", [(r, r ^ 1) for r in range(rows)])
    pair = gathered([right, other], COST_G)
    along = [lax.ppermute(pair, "row", [(r, (r + 2 * step) % rows) for r in range(rows)]) for step in (1, 2, 3)]
    near = gathered([pair] + along, COST_F)
    got = exchange(sent, FIRST)
    product = pl.pallas_call(
        product_kernel,
        out_shape=pltpu.VMEM((groups, line, TILE), BF16),
        in_specs=[VMEM, VMEM, VMEM, VMEM],
        out_specs=VMEM,
        cost_estimate=cost(COST_1),
    )(held(natural), held(turned), held(spread), held(got))
    contracted = exchange(product, SECOND)
    partial = pl.pallas_call(
        pair_kernel,
        out_shape=pltpu.VMEM((groups * 4, TILE), F32),
        in_specs=[VMEM, VMEM, VMEM],
        out_specs=VMEM,
        cost_estimate=cost(COST_A),
    )(held(flat_order), held(contracted), held(near))
    slices = exchange(partial.reshape(groups, 4, TILE), THIRD)
    result = pl.pallas_call(
        sum_kernel,
        out_shape=jax.ShapeDtypeStruct((8, row_count), F32),
        in_specs=[VMEM],
        out_specs=VMEM,
    )(held(slices.reshape(groups * 4, TILE)))
    return result.T


def solution(mesh):
    return jax.shard_map(
        body,
        mesh=mesh,
        in_specs=(P("row", ("col", "rep"), None), P(None, ("row", "col"), None), P(), P()),
        out_specs=P("row", ("col", "rep")),
        check_vma=False,
    )
```

time: 85.2 us -> 78.7 us (0.924)
  the two profiles are of different devices: /device:TPU:2 before, /device:TPU:8 now
where the time goes in v5:
time: 78.7 us; the launch traced here: 78.2 us
  starting transfers between devices  46.5 us (59%)
  blocking collectives  16.6 us (21%)
  waiting for transfers between devices  7.88 us (10%)
  Pallas kernels  5.94 us (8%)
  local copies, waits for them, and re-layouts  0.92 us (1%)
    all_to_all x2, starting transfers between devices, exchange(): lax.all_to_all(array, GRID, 0, 0, tiled=True, axis_index_groups=[order])  30.9 us
    all_to_all x1, blocking collectives, exchange(): lax.all_to_all(array, GRID, 0, 0, tiled=True, axis_index_groups=[order])  16.6 us
    ppermute x3, starting transfers between devices, body(): lax.ppermute(pair, 'row', [(r, (r + 2 * step) % rows) for r in range(rows)])  9.22 us
    all_to_all x2, waiting for transfers between devices, exchange(): lax.all_to_all(array, GRID, 0, 0, tiled=True, axis_index_groups=[order])  4.9 us
    all_to_all x1, starting transfers between devices, body(): lax.all_to_all(first, 'row', 0, 0, tiled=True, axis_index_groups=order)  4.54 us
    all_to_all x1, waiting for transfers between devices, body(): lax.all_to_all(first, 'row', 0, 0, tiled=True, axis_index_groups=order)  2.97 us
    ppermute x1, starting transfers between devices, body(): other = lax.ppermute(right, 'row', [(r, r ^ 1) for r in range(rows)])  1.92 us
    pallas_call x1, Pallas kernels, body(): pl.pallas_call(product_kernel, out_shape=pltpu.VMEM((groups, line, TILE),...  1.81 us
  transfers between devices with their start and end apart: 7, of which 3 were waited for; matrix products, arithmetic and copies ran while one was open for 1% of the time, Pallas kernels for 3%

profile of v5, /device:TPU:8, one launch (start us, length us, event | category | flops | bytes accessed | tf_op | source)
XLA Modules:
  0.0 78.2 jit_solution(2090592348232926289)
XLA Ops:
  0.0 1.6 %shard_map.82 = bf16[8,80,128]{2,1,0:T(8,128)(2,1)} custom-call(s32[2,2,4]{2,1,0:T(2,128)} %bitcast.23, s32[2,2,2]{2,1,0:T(2,128)} %green_ref.1, bf16[8,64,128]{2,1,0:T(8,128)(2,1)} %bitcast.21, bf16[16,128]{1,0:T(8,128)(2,1)} %bitcast.24), custom_call_target="tpu_custom_call" | custom-call | tf_op jit(solution)/shard_map/pallas_call | solution.py:176
  1.6 0.0 copy-start.3
  1.6 4.5 %all-to-all-start = ((bf16[8,80,128]{2,1,0:T(8,128)(2,1)}), bf16[8,80,128]{2,1,0:T(8,128)(2,1)S(1)}, u32[]{:S(2)}, u32[]{:S(2)}) async-start(bf16[8,80,128]{2,1,0:T(8,128)(2,1)} %shard_map.82), calls=%async_computation | async-start | bytes 327680 | tf_op jit(solution)/shard_map/all_to_all | solution.py:183
  6.2 0.0 copy-start.4
  6.2 0.7 copy-done.4
  6.9 0.2 fusion
  7.1 0.1 broadcast_bitcast_fusion
  7.1 0.0 copy-done.3
  7.1 0.1 broadcast_multiply_fusion
  7.2 0.1 reshape.30
  7.3 1.9 %collective-permute-start = (bf16[64,1024]{1,0:T(8,128)(2,1)S(1)}, bf16[64,1024]{1,0:T(8,128)(2,1)S(1)}, u32[]{:S(2)}, u32[]{:S(2)}) collective-permute-start(bf16[64,1024]{1,0:T(8,128)(2,1)S(1)} %reshape.31.refs_0_), channel_id=1, source_target_pairs={{0,64},{64,0},{128,192},{192,128},{256,320},{320,256},{384,448},{4... | collective-permute-start | bytes 393224 | tf_op jit(solution)/shard_map/ppermute | solution.py:206
  9.3 3.0 %all-to-all-done.got_ref = bf16[8,80,128]{2,1,0:T(8,128)(2,1)S(1)} async-done(((bf16[8,80,128]{2,1,0:T(8,128)(2,1)}), bf16[8,80,128]{2,1,0:T(8,128)(2,1)S(1)}, u32[]{:S(2)}, u32[]{:S(2)}) %all-to-all-start) | async-done | bytes 163872 | tf_op jit(solution)/shard_map/all_to_all | solution.py:183
  12.2 0.8 %shard_map.83 = bf16[64,24,128]{2,1,0:T(8,128)(2,1)} custom-call(bf16[8,80,128]{2,1,0:T(8,128)(2,1)S(1)} %all-to-all-done.got_ref), custom_call_target="tpu_custom_call" | custom-call | tf_op jit(solution)/shard_map/pallas_call | solution.py:184
  13.0 18.9 %all-to-all-start.1 = ((bf16[64,24,128]{2,1,0:T(8,128)(2,1)}), bf16[64,24,128]{2,1,0:T(8,128)(2,1)S(1)}, u32[]{:S(2)}, u32[]{:S(2)}) async-start(bf16[64,24,128]{2,1,0:T(8,128)(2,1)} %shard_map.83), calls=%async_computation.1 | async-start | bytes 786432 | tf_op jit(solution)/shard_map/all_to_all | solution.py:160
  31.9 0.0 copy-start
  31.9 0.0 copy-start.1
  31.9 0.0 collective-permute-done.refs_1_
  32.0 2.6 %collective-permute-start.1 = (bf16[128,1024]{1,0:T(8,128)(2,1)S(1)}, bf16[128,1024]{1,0:T(8,128)(2,1)S(1)}, u32[]{:S(2)}, u32[]{:S(2)}) collective-permute-start(bf16[128,1024]{1,0:T(8,128)(2,1)S(1)} %shard_map.85.refs_0_), channel_id=1, source_target_pairs={{0,128},{64,192},{128,256},{192,320},{256,384},{320,448},{384,0},{... | collective-permute-start | bytes 786440 | tf_op jit(solution)/shard_map/ppermute | solution.py:208
  34.6 4.0 %collective-permute-start.2 = (bf16[128,1024]{1,0:T(8,128)(2,1)S(1)}, bf16[128,1024]{1,0:T(8,128)(2,1)S(1)}, u32[]{:S(2)}, u32[]{:S(2)}) collective-permute-start(bf16[128,1024]{1,0:T(8,128)(2,1)S(1)} %shard_map.85.refs_0_), channel_id=1, source_target_pairs={{0,256},{64,320},{128,384},{192,448},{256,0},{320,64},{384,128},{4... | collective-permute-start | bytes 786440 | tf_op jit(solution)/shard_map/ppermute | solution.py:208
  38.6 2.6 %collective-permute-start.3 = (bf16[128,1024]{1,0:T(8,128)(2,1)S(1)}, bf16[128,1024]{1,0:T(8,128)(2,1)S(1)}, u32[]{:S(2)}, u32[]{:S(2)}) collective-permute-start(bf16[128,1024]{1,0:T(8,128)(2,1)S(1)} %shard_map.85.refs_0_), channel_id=1, source_target_pairs={{0,384},{64,448},{128,0},{192,64},{256,128},{320,192},{384,256},{4... | collective-permute-start | bytes 786440 | tf_op jit(solution)/shard_map/ppermute | solution.py:208
  41.2 0.7 all-to-all-done.1.got_ref
  41.9 0.0 copy-done
  41.9 0.0 copy-done.1
  41.9 1.8 %shard_map.84 = bf16[64,8,128]{2,1,0:T(8,128)(2,1)} custom-call(bf16[512,512]{1,0:T(8,128)(2,1)S(1)} %copy-done, bf16[512,512]{1,0:T(8,128)(2,1)S(1)} %copy-done.1, bf16[512,512]{1,0:T(8,128)(2,1)S(1)} %copy-done, bf16[64,24,128]{2,1,0:T(8,128)(2,1)S(1)} %all-to-all-done.1.got_ref), custom_call_target="tpu_custom_call" | custom-call | flops 1 | tf_op jit(solution)/shard_map/pallas_call | solution.py:211
  43.7 12.0 %all-to-all-start.2 = ((bf16[64,8,128]{2,1,0:T(8,128)(2,1)}), bf16[64,8,128]{2,1,0:T(8,128)(2,1)S(1)}, u32[]{:S(2)}, u32[]{:S(2)}) async-start(bf16[64,8,128]{2,1,0:T(8,128)(2,1)} %shard_map.84), calls=%async_computation.2 | async-start | bytes 262144 | tf_op jit(solution)/shard_map/all_to_all | solution.py:160
  55.8 0.0 copy-start.2
  55.8 0.0 collective-permute-done.1.refs_1_
  55.8 0.0 collective-permute-done.2.refs_2_
  55.8 0.0 collective-permute-done.3.refs_3_
  55.8 0.1 shard_map.86.held_ref
  55.9 4.2 %all-to-all-done.2.y_ref = bf16[64,8,128]{2,1,0:T(8,128)(2,1)S(1)} async-done(((bf16[64,8,128]{2,1,0:T(8,128)(2,1)}), bf16[64,8,128]{2,1,0:T(8,128)(2,1)S(1)}, u32[]{:S(2)}, u32[]{:S(2)}) %all-to-all-start.2) | async-done | bytes 131104 | tf_op jit(solution)/shard_map/all_to_all | solution.py:160
  60.1 0.0 copy-done.2
  60.1 0.9 %shard_map.87 = f32[256,128]{1,0:T(8,128)S(1)} custom-call(bf16[512,512]{1,0:T(8,128)(2,1)S(1)} %copy-done.2, bf16[64,8,128]{2,1,0:T(8,128)(2,1)S(1)} %all-to-all-done.2.y_ref, bf16[512,1024]{1,0:T(8,128)(2,1)S(1)} %shard_map.86.held_ref), custom_call_target="tpu_custom_call" | custom-call | flops 1000000000 | tf_op jit(solution)/shard_map/pallas_call | solution.py:219
  61.0 16.6 %all_to_all.20 = f32[64,4,128]{2,1,0:T(4,128)S(1)} all-to-all(f32[64,4,128]{2,1,0:T(4,128)S(1)} %bitcast.20), channel_id=1, replica_groups={{36,37,38,39,32,33,34,35,44,45,46,47,40,41,42,43,52,53,54,55,48,49,50,5..., dimensions={0} | all-to-all | bytes 262144 | tf_op jit(solution)/shard_map/all_to_all | solution.py:160
  77.5 0.7 shard_map.88
  (3 shorter events, 0.1 us)
Async XLA Ops:
  1.6 5.5 %copy-start.3 = (bf16[64,4,256]{2,1,0:T(4,128)(2,1)S(1)}, bf16[64,4,256]{2,1,0:T(4,128)(2,1)}, u32[]{:S(2)}) copy-start(bf16[64,4,256]{2,1,0:T(4,128)(2,1)} %param.8) | copy-start | bytes 393220
  1.6 10.6 %all-to-all-start = ((bf16[8,80,128]{2,1,0:T(8,128)(2,1)}), bf16[8,80,128]{2,1,0:T(8,128)(2,1)S(1)}, u32[]{:S(2)}, u32[]{:S(2)}) async-start(bf16[8,80,128]{2,1,0:T(8,128)(2,1)} %shard_map.82), calls=%async_computation | async-start | bytes 327680 | tf_op jit(solution)/shard_map/all_to_all | solution.py:183
  6.2 0.7 copy-start.4
  7.3 24.6 %collective-permute-start = (bf16[64,1024]{1,0:T(8,128)(2,1)S(1)}, bf16[64,1024]{1,0:T(8,128)(2,1)S(1)}, u32[]{:S(2)}, u32[]{:S(2)}) collective-permute-start(bf16[64,1024]{1,0:T(8,128)(2,1)S(1)} %reshape.31.refs_0_), channel_id=1, source_target_pairs={{0,64},{64,0},{128,192},{192,128},{256,320},{320,256},{384,448},{4... | collective-permute-start | bytes 393224 | tf_op jit(solution)/shard_map/ppermute | solution.py:206
  13.0 28.9 %all-to-all-start.1 = ((bf16[64,24,128]{2,1,0:T(8,128)(2,1)}), bf16[64,24,128]{2,1,0:T(8,128)(2,1)S(1)}, u32[]{:S(2)}, u32[]{:S(2)}) async-start(bf16[64,24,128]{2,1,0:T(8,128)(2,1)} %shard_map.83), calls=%async_computation.1 | async-start | bytes 786432 | tf_op jit(solution)/shard_map/all_to_all | solution.py:160
  31.9 10.0 %copy-start = (bf16[512,512]{1,0:T(8,128)(2,1)S(1)}, bf16[512,512]{1,0:T(8,128)(2,1)}, u32[]{:S(2)}) copy-start(bf16[512,512]{1,0:T(8,128)(2,1)} %constant.49.clone.natural_ref.spread_ref) | copy-start | bytes 1572868
  31.9 10.0 %copy-start.1 = (bf16[512,512]{1,0:T(8,128)(2,1)S(1)}, bf16[512,512]{1,0:T(8,128)(2,1)}, u32[]{:S(2)}) copy-start(bf16[512,512]{1,0:T(8,128)(2,1)} %constant.50.clone.turned_ref) | copy-start | bytes 1572868
  32.0 23.8 %collective-permute-start.1 = (bf16[128,1024]{1,0:T(8,128)(2,1)S(1)}, bf16[128,1024]{1,0:T(8,128)(2,1)S(1)}, u32[]{:S(2)}, u32[]{:S(2)}) collective-permute-start(bf16[128,1024]{1,0:T(8,128)(2,1)S(1)} %shard_map.85.refs_0_), channel_id=1, source_target_pairs={{0,128},{64,192},{128,256},{192,320},{256,384},{320,448},{384,0},{... | collective-permute-start | bytes 786440 | tf_op jit(solution)/shard_map/ppermute | solution.py:208
  34.6 21.2 %collective-permute-start.2 = (bf16[128,1024]{1,0:T(8,128)(2,1)S(1)}, bf16[128,1024]{1,0:T(8,128)(2,1)S(1)}, u32[]{:S(2)}, u32[]{:S(2)}) collective-permute-start(bf16[128,1024]{1,0:T(8,128)(2,1)S(1)} %shard_map.85.refs_0_), channel_id=1, source_target_pairs={{0,256},{64,320},{128,384},{192,448},{256,0},{320,64},{384,128},{4... | collective-permute-start | bytes 786440 | tf_op jit(solution)/shard_map/ppermute | solution.py:208
  38.6 17.2 %collective-permute-start.3 = (bf16[128,1024]{1,0:T(8,128)(2,1)S(1)}, bf16[128,1024]{1,0:T(8,128)(2,1)S(1)}, u32[]{:S(2)}, u32[]{:S(2)}) collective-permute-start(bf16[128,1024]{1,0:T(8,128)(2,1)S(1)} %shard_map.85.refs_0_), channel_id=1, source_target_pairs={{0,384},{64,448},{128,0},{192,64},{256,128},{320,192},{384,256},{4... | collective-permute-start | bytes 786440 | tf_op jit(solution)/shard_map/ppermute | solution.py:208
  43.7 16.3 %all-to-all-start.2 = ((bf16[64,8,128]{2,1,0:T(8,128)(2,1)}), bf16[64,8,128]{2,1,0:T(8,128)(2,1)S(1)}, u32[]{:S(2)}, u32[]{:S(2)}) async-start(bf16[64,8,128]{2,1,0:T(8,128)(2,1)} %shard_map.84), calls=%async_computation.2 | async-start | bytes 262144 | tf_op jit(solution)/shard_map/all_to_all | solution.py:160
  55.8 4.3 %copy-start.2 = (bf16[512,512]{1,0:T(8,128)(2,1)S(1)}, bf16[512,512]{1,0:T(8,128)(2,1)}, u32[]{:S(2)}) copy-start(bf16[512,512]{1,0:T(8,128)(2,1)} %constant.51.clone.order_ref) | copy-start | bytes 1572868

commit v6 on v5

--- a/solution.py
+++ b/solution.py
@@ -7,9 +7,7 @@
 from jax.sharding import PartitionSpec as P
 
 TILE = 128
-FIRST = (4, 4)
-SECOND = (4, 4)
-THIRD = (4, 4)
+START = 4
 ROWS = 1
 COST_F = 10**10
 COST_A = 10**9
@@ -39,9 +37,9 @@
     return jnp.asarray(index[:, None] == np.arange(index.size)[None, :], BF16)
 
 
-def peers(side, start):
+def peers(side):
     order = [
-        (start[0] + i) % side * side + (start[1] + j) % side for i in range(side) for j in range(side)
+        (START + i) % side * side + (START + j) % side for i in range(side) for j in range(side)
     ]
     return order, np.argsort(order)
 
@@ -49,17 +47,13 @@
 def orders(groups):
     side = int(round(groups**0.5))
     size = groups * LINE
-    first, first_place = peers(side, FIRST)
-    _, second_place = peers(side, SECOND)
+    order, place = peers(side)
     row = np.arange(size)
-    half, place = row // (size // 2), row % (size // 2)
-    block, inner = place // 4, place % 4
-    natural = first_place[block] * LINE + half * 4 + inner
-    turned = first_place[block % side * side + block // side] * LINE + half * 4 + inner
-    spread = second_place[block] * LINE + half * 4 + inner
-    part, func = row // groups, row % groups
-    flat = second_place[np.asarray(first)[func]] * LINE + part % 2 * 4 + part // 2
-    return natural, turned, spread, flat
+    half, nu = row // (size // 2), row % (size // 2)
+    block, inner = nu // 4, nu % 4
+    source = place[block % side * side + block // side]
+    column = np.arange(size // 2)
+    return source * LINE + half * 4 + inner, np.asarray(order)[column % groups] * 4 + column // groups
 
 
 def first_kernel(tile_ref, green_ref, m_ref, shard_ref, out_ref):
@@ -93,47 +87,57 @@
     out_ref[:, LINE:] = jnp.broadcast_to(shard[None], (groups,) + shard.shape)
 
 
-def product_kernel(natural_ref, turned_ref, spread_ref, got_ref, out_ref):
+def product_kernel(nu_ref, l_ref, got_ref, out_ref, m_ref, o_ref, y_ref):
     groups = got_ref.shape[0]
+    side = 8
     size = groups * LINE
-    side = size // 2
     got = got_ref[...]
-    m_part = got[:, :LINE].reshape(size, TILE)
-    o_part = got[:, LINE : 2 * LINE].reshape(size, TILE)
-    v_part = got[:, 2 * LINE :].reshape(size, TILE)
-    natural = natural_ref[...]
-    turned = turned_ref[...]
-
-    def square(rows):
-        rows = rows.astype(BF16)
-        return jnp.concatenate([rows[:side], rows[side:]], axis=1)
-
-    virtual = square(dot(turned, v_part))
-    mine = square(dot(natural, m_part))
-    occupied = square(dot(turned, o_part))
+    rows = dot(nu_ref[...], got[:, 2 * LINE :].reshape(size, TILE)).astype(BF16)
+    virtual = jnp.concatenate([rows[: size // 2], rows[size // 2 :]], axis=1)
+    m_ref[...] = got[:, :LINE].reshape(size, TILE).astype(F32)
+    o_ref[...] = got[:, LINE : 2 * LINE].reshape(size, TILE).astype(F32)
+    mine = [
+        jnp.concatenate([m_ref[pl.ds(half * 4 + i, groups, stride=LINE), :] for i in range(4)], axis=0)
+        for half in range(2)
+    ]
+    occupied = [
+        jnp.concatenate(
+            [
+                o_ref[pl.ds(m * LINE + half * 4 + i, side, stride=side * LINE), :]
+                for i in range(4)
+                for m in range(side)
+            ],
+            axis=0,
+        )
+        for half in range(2)
+    ]
+    mine = jnp.concatenate(mine, axis=1).astype(BF16)
+    occupied = jnp.concatenate(occupied, axis=1).astype(BF16)
     halfway = dot(mine, virtual).astype(BF16)
-    spread = spread_ref[...]
-    wide = dot(occupied, spread[:side] + spread[side:]).astype(BF16)
-    product = dot(wide, halfway, TN)
-    line = lax.broadcasted_iota(jnp.int32, (size, TILE), 0) % LINE
-    out = jnp.where(line < 4, product[:, :TILE], product[:, TILE:]).astype(BF16)
-    out_ref[...] = out.reshape(groups, LINE, TILE)
-
-
-def pair_kernel(order_ref, y_ref, held_ref, out_ref):
+    product = dot(dot(occupied, l_ref[...]).astype(BF16), halfway, TN)
+    for i in range(4):
+        for half in range(2):
+            block = product[i * groups : (i + 1) * groups, half * TILE : (half + 1) * TILE]
+            y_ref[pl.ds(half * 4 + i, groups, stride=LINE), :] = block
+    out_ref[...] = y_ref[...].astype(BF16).reshape(groups, LINE, TILE)
+
+
+def pair_kernel(y_ref, *refs):
+    out_ref, wide_ref = refs[-2:]
     count = y_ref.shape[0]
     half = count // 2
-    picked = dot(order_ref[...], y_ref[...].reshape(count * LINE, TILE)).astype(BF16)
-    flat = jnp.concatenate([picked[b * count : (b + 1) * count] for b in range(LINE)], axis=1)
+    wide_ref[...] = y_ref[...].reshape(count * LINE, TILE).astype(F32)
+    picked = [wide_ref[pl.ds(line, count, stride=LINE), :].astype(BF16) for line in (0, 4, 1, 5, 2, 6, 3, 7)]
+    flat = jnp.concatenate(picked, axis=1)
     chip, core = lax.axis_index("row") // 2, lax.axis_index("row") % 2
-    part = dot(held_ref[...], flat, NT)
     for step in range(4):
+        part = dot(refs[step][...], flat, NT)
         for other in range(2):
-            rows = part[(step * 2 + other) * count :][:count]
+            rows = part[other * count :][:count]
             wide = jnp.concatenate([rows[:half], rows[half:]], axis=1)
             block = lax.rem(chip - step + 4, 4) * 2 + lax.rem(core + other, 2)
-            block = lax.rem(block + 8 - THIRD[0], 8)
-            cut = THIRD[1] * 4
+            block = lax.rem(block + 8 - START, 8)
+            cut = START * 4
             wide = jnp.concatenate([wide[cut:], wide[:cut]], axis=0)
             out_ref[pl.ds(pl.multiple_of(block * half, half), half), :] = wide
 
@@ -155,8 +159,8 @@
     out_ref[...] = jnp.concatenate([total[:, :64], total[:, 64:]], axis=0)
 
 
-def exchange(array, start):
-    order, _ = peers(lax.axis_size("col"), start)
+def exchange(array):
+    order, _ = peers(lax.axis_size("col"))
     return lax.all_to_all(array, GRID, 0, 0, tiled=True, axis_index_groups=[order])
 
 
@@ -167,7 +171,7 @@
     halves = ao_count // TILE
     line = halves * mu_block
     row = lax.axis_index("row")
-    natural, turned, spread, flat_order = (pick(order) for order in orders(groups))
+    nu_order, l_order = orders(groups)
 
     own = m_tensor.reshape(row_count, mu_block, halves, TILE).transpose(0, 2, 1, 3)
     own = own.reshape(rows, row_count // rows * line, TILE)
@@ -206,24 +210,25 @@
     other = lax.ppermute(right, "row", [(r, r ^ 1) for r in range(rows)])
     pair = gathered([right, other], COST_G)
     along = [lax.ppermute(pair, "row", [(r, (r + 2 * step) % rows) for r in range(rows)]) for step in (1, 2, 3)]
-    near = gathered([pair] + along, COST_F)
-    got = exchange(sent, FIRST)
+    got = exchange(sent)
     product = pl.pallas_call(
         product_kernel,
         out_shape=pltpu.VMEM((groups, line, TILE), BF16),
-        in_specs=[VMEM, VMEM, VMEM, VMEM],
-        out_specs=VMEM,
+        in_specs=[VMEM, VMEM, VMEM],
+        out_specs=VMEM,
+        scratch_shapes=[pltpu.VMEM((groups * line, TILE), F32)] * 3,
         cost_estimate=cost(COST_1),
-    )(held(natural), held(turned), held(spread), held(got))
-    contracted = exchange(product, SECOND)
+    )(held(pick(nu_order)), held(pick(l_order).T), held(got))
+    contracted = exchange(product)
     partial = pl.pallas_call(
         pair_kernel,
         out_shape=pltpu.VMEM((groups * 4, TILE), F32),
-        in_specs=[VMEM, VMEM, VMEM],
-        out_specs=VMEM,
+        in_specs=[VMEM] * 5,
+        out_specs=VMEM,
+        scratch_shapes=[pltpu.VMEM((groups * line, TILE), F32)],
         cost_estimate=cost(COST_A),
-    )(held(flat_order), held(contracted), held(near))
-    slices = exchange(partial.reshape(groups, 4, TILE), THIRD)
+    )(held(contracted), *[held(part) for part in [pair] + along])
+    slices = exchange(partial.reshape(groups, 4, TILE))
     result = pl.pallas_call(
         sum_kernel,
         out_shape=jax.ShapeDtypeStruct((8, row_count), F32),

time: 78.7 us -> 78 us (level)
  the two profiles are of different devices: /device:TPU:8 before, /device:TPU:4 now
where the time goes in v6:
time: 78 us; the launch traced here: 77.5 us
  starting transfers between devices  49.7 us (64%)
  blocking collectives  16.5 us (21%)
  Pallas kernels  5.21 us (7%)
  waiting for transfers between devices  4.77 us (6%)
  local copies, waits for them, and re-layouts  0.91 us (1%)
    all_to_all x2, starting transfers between devices, exchange(): lax.all_to_all(array, GRID, 0, 0, tiled=True, axis_index_groups=[order])  28.9 us
    all_to_all x1, blocking collectives, exchange(): lax.all_to_all(array, GRID, 0, 0, tiled=True, axis_index_groups=[order])  16.5 us
    ppermute x3, starting transfers between devices, body(): lax.ppermute(pair, 'row', [(r, (r + 2 * step) % rows) for r in range(rows)])  11.3 us
    all_to_all x1, starting transfers between devices, body(): lax.all_to_all(first, 'row', 0, 0, tiled=True, axis_index_groups=order)  7.43 us
    all_to_all x2, waiting for transfers between devices, exchange(): lax.all_to_all(array, GRID, 0, 0, tiled=True, axis_index_groups=[order])  3.43 us
    ppermute x1, starting transfers between devices, body(): other = lax.ppermute(right, 'row', [(r, r ^ 1) for r in range(rows)])  1.99 us
    pallas_call x1, Pallas kernels, body(): pl.pallas_call(first_kernel, out_shape=pltpu.VMEM((rows, row_count // row...  1.63 us
    pallas_call x1, Pallas kernels, body(): pl.pallas_call(product_kernel, out_shape=pltpu.VMEM((groups, line, TILE),...  1.56 us
  transfers between devices with their start and end apart: 7, of which 2 were waited for; matrix products, arithmetic and copies ran while one was open for 1% of the time, Pallas kernels for 3%

profile of v6, /device:TPU:4, one launch (start us, length us, event | category | flops | bytes accessed | tf_op | source)
XLA Modules:
  0.0 77.5 jit_solution(13693915685012265809)
XLA Ops:
  0.0 1.6 %shard_map.64 = bf16[8,80,128]{2,1,0:T(8,128)(2,1)} custom-call(s32[2,2,4]{2,1,0:T(2,128)} %bitcast.23, s32[2,2,2]{2,1,0:T(2,128)} %green_ref.1, bf16[8,64,128]{2,1,0:T(8,128)(2,1)} %bitcast.21, bf16[16,128]{1,0:T(8,128)(2,1)} %bitcast.24), custom_call_target="tpu_custom_call" | custom-call | tf_op jit(solution)/shard_map/pallas_call | solution.py:180
  1.6 0.0 copy-start.2
  1.6 7.4 %all-to-all-start = ((bf16[8,80,128]{2,1,0:T(8,128)(2,1)}), bf16[8,80,128]{2,1,0:T(8,128)(2,1)S(1)}, u32[]{:S(2)}, u32[]{:S(2)}) async-start(bf16[8,80,128]{2,1,0:T(8,128)(2,1)} %shard_map.64), calls=%async_computation | async-start | bytes 327680 | tf_op jit(solution)/shard_map/all_to_all | solution.py:187
  9.1 0.0 copy-start.3
  9.1 0.7 copy-done.3
  9.7 0.2 fusion
  9.9 0.1 broadcast_bitcast_fusion
  10.0 0.0 copy-done.2
  10.0 0.1 broadcast_multiply_fusion
  10.1 0.1 reshape.30
  10.2 2.0 %collective-permute-start = (bf16[64,1024]{1,0:T(8,128)(2,1)S(1)}, bf16[64,1024]{1,0:T(8,128)(2,1)S(1)}, u32[]{:S(2)}, u32[]{:S(2)}) collective-permute-start(bf16[64,1024]{1,0:T(8,128)(2,1)S(1)} %reshape.31.refs_0_), channel_id=1, source_target_pairs={{0,64},{64,0},{128,192},{192,128},{256,320},{320,256},{384,448},{4... | collective-permute-start | bytes 393224 | tf_op jit(solution)/shard_map/ppermute | solution.py:210
  12.2 1.3 %all-to-all-done.got_ref = bf16[8,80,128]{2,1,0:T(8,128)(2,1)S(1)} async-done(((bf16[8,80,128]{2,1,0:T(8,128)(2,1)}), bf16[8,80,128]{2,1,0:T(8,128)(2,1)S(1)}, u32[]{:S(2)}, u32[]{:S(2)}) %all-to-all-start) | async-done | bytes 163872 | tf_op jit(solution)/shard_map/all_to_all | solution.py:187
  13.6 0.8 %shard_map.65 = bf16[64,24,128]{2,1,0:T(8,128)(2,1)} custom-call(bf16[8,80,128]{2,1,0:T(8,128)(2,1)S(1)} %all-to-all-done.got_ref), custom_call_target="tpu_custom_call" | custom-call | tf_op jit(solution)/shard_map/pallas_call | solution.py:188
  14.4 16.2 %all-to-all-start.1 = ((bf16[64,24,128]{2,1,0:T(8,128)(2,1)}), bf16[64,24,128]{2,1,0:T(8,128)(2,1)S(1)}, u32[]{:S(2)}, u32[]{:S(2)}) async-start(bf16[64,24,128]{2,1,0:T(8,128)(2,1)} %shard_map.65), calls=%async_computation.1 | async-start | bytes 786432 | tf_op jit(solution)/shard_map/all_to_all | solution.py:164
  30.6 0.0 copy-start
  30.6 0.0 copy-start.1
  30.6 0.0 collective-permute-done.refs_1_
  30.7 3.9 %collective-permute-start.3 = (bf16[128,1024]{1,0:T(8,128)(2,1)S(1)}, bf16[128,1024]{1,0:T(8,128)(2,1)S(1)}, u32[]{:S(2)}, u32[]{:S(2)}) collective-permute-start(bf16[128,1024]{1,0:T(8,128)(2,1)S(1)} %shard_map.67.refs_0_), channel_id=1, source_target_pairs={{0,384},{64,448},{128,0},{192,64},{256,128},{320,192},{384,256},{4... | collective-permute-start | bytes 786440 | tf_op jit(solution)/shard_map/ppermute | solution.py:212
  34.6 4.0 %collective-permute-start.2 = (bf16[128,1024]{1,0:T(8,128)(2,1)S(1)}, bf16[128,1024]{1,0:T(8,128)(2,1)S(1)}, u32[]{:S(2)}, u32[]{:S(2)}) collective-permute-start(bf16[128,1024]{1,0:T(8,128)(2,1)S(1)} %shard_map.67.refs_0_), channel_id=1, source_target_pairs={{0,256},{64,320},{128,384},{192,448},{256,0},{320,64},{384,128},{4... | collective-permute-start | bytes 786440 | tf_op jit(solution)/shard_map/ppermute | solution.py:212
  38.6 3.4 %collective-permute-start.1 = (bf16[128,1024]{1,0:T(8,128)(2,1)S(1)}, bf16[128,1024]{1,0:T(8,128)(2,1)S(1)}, u32[]{:S(2)}, u32[]{:S(2)}) collective-permute-start(bf16[128,1024]{1,0:T(8,128)(2,1)S(1)} %shard_map.67.refs_0_), channel_id=1, source_target_pairs={{0,128},{64,192},{128,256},{192,320},{256,384},{320,448},{384,0},{... | collective-permute-start | bytes 786440 | tf_op jit(solution)/shard_map/ppermute | solution.py:212
  42.0 0.0 all-to-all-done.1.got_ref
  42.0 0.0 copy-done
  42.0 0.0 copy-done.1
  42.0 1.6 %shard_map.66 = bf16[64,8,128]{2,1,0:T(8,128)(2,1)} custom-call(bf16[512,512]{1,0:T(8,128)(2,1)S(1)} %copy-done, bf16[256,256]{1,0:T(8,128)(2,1)S(1)} %copy-done.1, bf16[64,24,128]{2,1,0:T(8,128)(2,1)S(1)} %all-to-all-done.1.got_ref), custom_call_target="tpu_custom_call" | custom-call | flops 1 | tf_op jit(solution)/shard_map/pallas_call | solution.py:214
  43.6 12.7 %all-to-all-start.2 = ((bf16[64,8,128]{2,1,0:T(8,128)(2,1)}), bf16[64,8,128]{2,1,0:T(8,128)(2,1)S(1)}, u32[]{:S(2)}, u32[]{:S(2)}) async-start(bf16[64,8,128]{2,1,0:T(8,128)(2,1)} %shard_map.66), calls=%async_computation.2 | async-start | bytes 262144 | tf_op jit(solution)/shard_map/all_to_all | solution.py:164
  56.3 0.0 collective-permute-done.3.refs_3_
  56.3 0.0 collective-permute-done.2.refs_2_
  56.3 0.0 collective-permute-done.1.refs_1_
  56.3 3.4 %all-to-all-done.2.y_ref = bf16[64,8,128]{2,1,0:T(8,128)(2,1)S(1)} async-done(((bf16[64,8,128]{2,1,0:T(8,128)(2,1)}), bf16[64,8,128]{2,1,0:T(8,128)(2,1)S(1)}, u32[]{:S(2)}, u32[]{:S(2)}) %all-to-all-start.2) | async-done | bytes 131104 | tf_op jit(solution)/shard_map/all_to_all | solution.py:164
  59.7 0.5 shard_map.68
  60.3 16.5 %all_to_all.20 = f32[64,4,128]{2,1,0:T(4,128)S(1)} all-to-all(f32[64,4,128]{2,1,0:T(4,128)S(1)} %bitcast.20), channel_id=1, replica_groups={{36,37,38,39,32,33,34,35,44,45,46,47,40,41,42,43,52,53,54,55,48,49,50,5..., dimensions={0} | all-to-all | bytes 262144 | tf_op jit(solution)/shard_map/all_to_all | solution.py:164
  76.8 0.7 shard_map.69
  (3 shorter events, 0.1 us)
Async XLA Ops:
  1.6 8.4 %copy-start.2 = (bf16[64,4,256]{2,1,0:T(4,128)(2,1)S(1)}, bf16[64,4,256]{2,1,0:T(4,128)(2,1)}, u32[]{:S(2)}) copy-start(bf16[64,4,256]{2,1,0:T(4,128)(2,1)} %param.6) | copy-start | bytes 393220
  1.6 11.9 %all-to-all-start = ((bf16[8,80,128]{2,1,0:T(8,128)(2,1)}), bf16[8,80,128]{2,1,0:T(8,128)(2,1)S(1)}, u32[]{:S(2)}, u32[]{:S(2)}) async-start(bf16[8,80,128]{2,1,0:T(8,128)(2,1)} %shard_map.64), calls=%async_computation | async-start | bytes 327680 | tf_op jit(solution)/shard_map/all_to_all | solution.py:187
  9.1 0.7 copy-start.3
  10.2 20.4 %collective-permute-start = (bf16[64,1024]{1,0:T(8,128)(2,1)S(1)}, bf16[64,1024]{1,0:T(8,128)(2,1)S(1)}, u32[]{:S(2)}, u32[]{:S(2)}) collective-permute-start(bf16[64,1024]{1,0:T(8,128)(2,1)S(1)} %reshape.31.refs_0_), channel_id=1, source_target_pairs={{0,64},{64,0},{128,192},{192,128},{256,320},{320,256},{384,448},{4... | collective-permute-start | bytes 393224 | tf_op jit(solution)/shard_map/ppermute | solution.py:210
  14.4 27.6 %all-to-all-start.1 = ((bf16[64,24,128]{2,1,0:T(8,128)(2,1)}), bf16[64,24,128]{2,1,0:T(8,128)(2,1)S(1)}, u32[]{:S(2)}, u32[]{:S(2)}) async-start(bf16[64,24,128]{2,1,0:T(8,128)(2,1)} %shard_map.65), calls=%async_computation.1 | async-start | bytes 786432 | tf_op jit(solution)/shard_map/all_to_all | solution.py:164
  30.6 11.4 %copy-start = (bf16[512,512]{1,0:T(8,128)(2,1)S(1)}, bf16[512,512]{1,0:T(8,128)(2,1)}, u32[]{:S(2)}) copy-start(bf16[512,512]{1,0:T(8,128)(2,1)} %constant.47.clone.nu_ref) | copy-start | bytes 1572868
  30.6 11.4 %copy-start.1 = (bf16[256,256]{1,0:T(8,128)(2,1)S(1)}, bf16[256,256]{1,0:T(8,128)(2,1)}, u32[]{:S(2)}) copy-start(bf16[256,256]{1,0:T(8,128)(2,1)} %constant.51.l_ref) | copy-start | bytes 393220
  30.7 25.6 %collective-permute-start.3 = (bf16[128,1024]{1,0:T(8,128)(2,1)S(1)}, bf16[128,1024]{1,0:T(8,128)(2,1)S(1)}, u32[]{:S(2)}, u32[]{:S(2)}) collective-permute-start(bf16[128,1024]{1,0:T(8,128)(2,1)S(1)} %shard_map.67.refs_0_), channel_id=1, source_target_pairs={{0,384},{64,448},{128,0},{192,64},{256,128},{320,192},{384,256},{4... | collective-permute-start | bytes 786440 | tf_op jit(solution)/shard_map/ppermute | solution.py:212
  34.6 21.7 %collective-permute-start.2 = (bf16[128,1024]{1,0:T(8,128)(2,1)S(1)}, bf16[128,1024]{1,0:T(8,128)(2,1)S(1)}, u32[]{:S(2)}, u32[]{:S(2)}) collective-permute-start(bf16[128,1024]{1,0:T(8,128)(2,1)S(1)} %shard_map.67.refs_0_), channel_id=1, source_target_pairs={{0,256},{64,320},{128,384},{192,448},{256,0},{320,64},{384,128},{4... | collective-permute-start | bytes 786440 | tf_op jit(solution)/shard_map/ppermute | solution.py:212
  38.6 17.7 %collective-permute-start.1 = (bf16[128,1024]{1,0:T(8,128)(2,1)S(1)}, bf16[128,1024]{1,0:T(8,128)(2,1)S(1)}, u32[]{:S(2)}, u32[]{:S(2)}) collective-permute-start(bf16[128,1024]{1,0:T(8,128)(2,1)S(1)} %shard_map.67.refs_0_), channel_id=1, source_target_pairs={{0,128},{64,192},{128,256},{192,320},{256,384},{320,448},{384,0},{... | collective-permute-start | bytes 786440 | tf_op jit(solution)/shard_map/ppermute | solution.py:212
  43.6 16.2 %all-to-all-start.2 = ((bf16[64,8,128]{2,1,0:T(8,128)(2,1)}), bf16[64,8,128]{2,1,0:T(8,128)(2,1)S(1)}, u32[]{:S(2)}, u32[]{:S(2)}) async-start(bf16[64,8,128]{2,1,0:T(8,128)(2,1)} %shard_map.66), calls=%async_computation.2 | async-start | bytes 262144 | tf_op jit(solution)/shard_map/all_to_all | solution.py:164

commit v7 on v6

--- a/solution.py
+++ b/solution.py
@@ -9,8 +9,8 @@
 TILE = 128
 START = 4
 ROWS = 1
-COST_F = 10**10
-COST_A = 10**9
+COST_F = 1
+COST_A = 1
 COST_1 = 1
 COST_G = 10**10
 GRID = ("col", "rep")
@@ -122,24 +122,35 @@
     out_ref[...] = y_ref[...].astype(BF16).reshape(groups, LINE, TILE)
 
 
-def pair_kernel(y_ref, *refs):
-    out_ref, wide_ref = refs[-2:]
+def near_kernel(y_ref, pair_ref, out_ref, flat_ref, wide_ref):
     count = y_ref.shape[0]
-    half = count // 2
     wide_ref[...] = y_ref[...].reshape(count * LINE, TILE).astype(F32)
     picked = [wide_ref[pl.ds(line, count, stride=LINE), :].astype(BF16) for line in (0, 4, 1, 5, 2, 6, 3, 7)]
     flat = jnp.concatenate(picked, axis=1)
+    flat_ref[...] = flat
+    place(flat, pair_ref, 0, out_ref)
+
+
+def far_kernel(flat_ref, part_ref, *refs):
+    out_ref = refs[-1]
+    out_ref[...] = part_ref[...]
+    for step, ref in enumerate(refs[:-1]):
+        place(flat_ref[...], ref, step + 1, out_ref)
+
+
+def place(flat, pair_ref, step, out_ref):
+    count = flat.shape[0]
+    half = count // 2
     chip, core = lax.axis_index("row") // 2, lax.axis_index("row") % 2
-    for step in range(4):
-        part = dot(refs[step][...], flat, NT)
-        for other in range(2):
-            rows = part[other * count :][:count]
-            wide = jnp.concatenate([rows[:half], rows[half:]], axis=1)
-            block = lax.rem(chip - step + 4, 4) * 2 + lax.rem(core + other, 2)
-            block = lax.rem(block + 8 - START, 8)
-            cut = START * 4
-            wide = jnp.concatenate([wide[cut:], wide[:cut]], axis=0)
-            out_ref[pl.ds(pl.multiple_of(block * half, half), half), :] = wide
+    part = dot(pair_ref[...], flat, NT)
+    for other in range(2):
+        rows = part[other * count :][:count]
+        wide = jnp.concatenate([rows[:half], rows[half:]], axis=1)
+        block = lax.rem(chip - step + 4, 4) * 2 + lax.rem(core + other, 2)
+        block = lax.rem(block + 8 - START, 8)
+        cut = START * 4
+        wide = jnp.concatenate([wide[cut:], wide[:cut]], axis=0)
+        out_ref[pl.ds(pl.multiple_of(block * half, half), half), :] = wide
 
 
 def gather_kernel(*refs):
@@ -220,14 +231,24 @@
         cost_estimate=cost(COST_1),
     )(held(pick(nu_order)), held(pick(l_order).T), held(got))
     contracted = exchange(product)
+    partial, flat = pl.pallas_call(
+        near_kernel,
+        out_shape=(
+            pltpu.VMEM((groups * 4, TILE), F32),
+            pltpu.VMEM((row_count, mu_block * ao_count), BF16),
+        ),
+        in_specs=[VMEM] * 2,
+        out_specs=(VMEM, VMEM),
+        scratch_shapes=[pltpu.VMEM((groups * line, TILE), F32)],
+        cost_estimate=cost(COST_A),
+    )(held(contracted), held(pair))
     partial = pl.pallas_call(
-        pair_kernel,
+        far_kernel,
         out_shape=pltpu.VMEM((groups * 4, TILE), F32),
         in_specs=[VMEM] * 5,
         out_specs=VMEM,
-        scratch_shapes=[pltpu.VMEM((groups * line, TILE), F32)],
-        cost_estimate=cost(COST_A),
-    )(held(contracted), *[held(part) for part in [pair] + along])
+        cost_estimate=cost(COST_F),
+    )(held(flat), held(partial), *[held(part) for part in along])
     slices = exchange(partial.reshape(groups, 4, TILE))
     result = pl.pallas_call(
         sum_kernel,

time: 78 us -> 77.4 us (level)
  blocking collectives: 16.5 us -> 32.5 us
  starting transfers between devices: 49.7 us -> 37 us
  waiting for transfers between devices: 4.77 us -> 1.34 us
    all_to_all x1 -> x2, blocking collectives: 16.5 us -> 32.5 us  [exchange(): lax.all_to_all(array, GRID, 0, 0, tiled=True, axis_index_groups=[order])]
    all_to_all x2 -> x1, starting transfers between devices: 28.9 us -> 16.2 us  [exchange(): lax.all_to_all(array, GRID, 0, 0, tiled=True, axis_index_groups=[order])]
    all_to_all x2 -> x1, waiting for transfers between devices: 3.43 us -> 0.01 us  [exchange(): lax.all_to_all(array, GRID, 0, 0, tiled=True, axis_index_groups=[order])]
  transfers between devices with their start and end apart: 7 -> 6, of which waited for: 2 -> 1; matrix products, arithmetic and copies ran while one was open for 1% -> 1% of each run, Pallas kernels for 3% -> 3%
where the time goes in v7:
time: 77.4 us; the launch traced here: 76.9 us
  starting transfers between devices  37 us (48%)
  blocking collectives  32.5 us (42%)
  Pallas kernels  4.79 us (6%)
  waiting for transfers between devices  1.34 us (2%)
  local copies, waits for them, and re-layouts  0.91 us (1%)
    all_to_all x2, blocking collectives, exchange(): lax.all_to_all(array, GRID, 0, 0, tiled=True, axis_index_groups=[order])  32.5 us
    all_to_all x1, starting transfers between devices, exchange(): lax.all_to_all(array, GRID, 0, 0, tiled=True, axis_index_groups=[order])  16.2 us
    ppermute x3, starting transfers between devices, body(): lax.ppermute(pair, 'row', [(r, (r + 2 * step) % rows) for r in range(rows)])  11.3 us
    all_to_all x1, starting transfers between devices, body(): lax.all_to_all(first, 'row', 0, 0, tiled=True, axis_index_groups=order)  7.43 us
    ppermute x1, starting transfers between devices, body(): other = lax.ppermute(right, 'row', [(r, r ^ 1) for r in range(rows)])  1.99 us
    pallas_call x1, Pallas kernels, body(): pl.pallas_call(first_kernel, out_shape=pltpu.VMEM((rows, row_count // row...  1.63 us
  transfers between devices with their start and end apart: 6, of which 1 were waited for; matrix products, arithmetic and copies ran while one was open for 1% of the time, Pallas kernels for 3%

profile of v7, /device:TPU:4, one launch (start us, length us, event | category | flops | bytes accessed | tf_op | source)
XLA Modules:
  0.0 76.9 jit_solution(9962276357259073240)
XLA Ops:
  0.0 1.6 %shard_map.64 = bf16[8,80,128]{2,1,0:T(8,128)(2,1)} custom-call(s32[2,2,4]{2,1,0:T(2,128)} %bitcast.23, s32[2,2,2]{2,1,0:T(2,128)} %green_ref.1, bf16[8,64,128]{2,1,0:T(8,128)(2,1)} %bitcast.21, bf16[16,128]{1,0:T(8,128)(2,1)} %bitcast.24), custom_call_target="tpu_custom_call" | custom-call | tf_op jit(solution)/shard_map/pallas_call | solution.py:191
  1.6 0.0 copy-start.2
  1.6 7.4 %all-to-all-start = ((bf16[8,80,128]{2,1,0:T(8,128)(2,1)}), bf16[8,80,128]{2,1,0:T(8,128)(2,1)S(1)}, u32[]{:S(2)}, u32[]{:S(2)}) async-start(bf16[8,80,128]{2,1,0:T(8,128)(2,1)} %shard_map.64), calls=%async_computation | async-start | bytes 327680 | tf_op jit(solution)/shard_map/all_to_all | solution.py:198
  9.1 0.0 copy-start.3
  9.1 0.7 copy-done.3
  9.7 0.2 fusion
  9.9 0.1 broadcast_bitcast_fusion
  10.0 0.0 copy-done.2
  10.0 0.1 broadcast_multiply_fusion
  10.1 0.1 reshape.30
  10.2 2.0 %collective-permute-start = (bf16[64,1024]{1,0:T(8,128)(2,1)S(1)}, bf16[64,1024]{1,0:T(8,128)(2,1)S(1)}, u32[]{:S(2)}, u32[]{:S(2)}) collective-permute-start(bf16[64,1024]{1,0:T(8,128)(2,1)S(1)} %reshape.31.refs_0_), channel_id=1, source_target_pairs={{0,64},{64,0},{128,192},{192,128},{256,320},{320,256},{384,448},{4... | collective-permute-start | bytes 393224 | tf_op jit(solution)/shard_map/ppermute | solution.py:221
  12.2 1.3 %all-to-all-done.got_ref = bf16[8,80,128]{2,1,0:T(8,128)(2,1)S(1)} async-done(((bf16[8,80,128]{2,1,0:T(8,128)(2,1)}), bf16[8,80,128]{2,1,0:T(8,128)(2,1)S(1)}, u32[]{:S(2)}, u32[]{:S(2)}) %all-to-all-start) | async-done | bytes 163872 | tf_op jit(solution)/shard_map/all_to_all | solution.py:198
  13.6 0.8 %shard_map.65 = bf16[64,24,128]{2,1,0:T(8,128)(2,1)} custom-call(bf16[8,80,128]{2,1,0:T(8,128)(2,1)S(1)} %all-to-all-done.got_ref), custom_call_target="tpu_custom_call" | custom-call | tf_op jit(solution)/shard_map/pallas_call | solution.py:199
  14.4 16.2 %all-to-all-start.1 = ((bf16[64,24,128]{2,1,0:T(8,128)(2,1)}), bf16[64,24,128]{2,1,0:T(8,128)(2,1)S(1)}, u32[]{:S(2)}, u32[]{:S(2)}) async-start(bf16[64,24,128]{2,1,0:T(8,128)(2,1)} %shard_map.65), calls=%async_computation.1 | async-start | bytes 786432 | tf_op jit(solution)/shard_map/all_to_all | solution.py:175
  30.6 0.0 copy-start
  30.6 0.0 copy-start.1
  30.6 0.0 collective-permute-done.refs_1_
  30.7 3.9 %collective-permute-start.3 = (bf16[128,1024]{1,0:T(8,128)(2,1)S(1)}, bf16[128,1024]{1,0:T(8,128)(2,1)S(1)}, u32[]{:S(2)}, u32[]{:S(2)}) collective-permute-start(bf16[128,1024]{1,0:T(8,128)(2,1)S(1)} %shard_map.67.pair_ref), channel_id=1, source_target_pairs={{0,384},{64,448},{128,0},{192,64},{256,128},{320,192},{384,256},{4... | collective-permute-start | bytes 786440 | tf_op jit(solution)/shard_map/ppermute | solution.py:223
  34.6 4.0 %collective-permute-start.2 = (bf16[128,1024]{1,0:T(8,128)(2,1)S(1)}, bf16[128,1024]{1,0:T(8,128)(2,1)S(1)}, u32[]{:S(2)}, u32[]{:S(2)}) collective-permute-start(bf16[128,1024]{1,0:T(8,128)(2,1)S(1)} %shard_map.67.pair_ref), channel_id=1, source_target_pairs={{0,256},{64,320},{128,384},{192,448},{256,0},{320,64},{384,128},{4... | collective-permute-start | bytes 786440 | tf_op jit(solution)/shard_map/ppermute | solution.py:223
  38.6 3.4 %collective-permute-start.1 = (bf16[128,1024]{1,0:T(8,128)(2,1)S(1)}, bf16[128,1024]{1,0:T(8,128)(2,1)S(1)}, u32[]{:S(2)}, u32[]{:S(2)}) collective-permute-start(bf16[128,1024]{1,0:T(8,128)(2,1)S(1)} %shard_map.67.pair_ref), channel_id=1, source_target_pairs={{0,128},{64,192},{128,256},{192,320},{256,384},{320,448},{384,0},{... | collective-permute-start | bytes 786440 | tf_op jit(solution)/shard_map/ppermute | solution.py:223
  42.0 0.0 all-to-all-done.1.got_ref
  42.0 0.0 copy-done
  42.0 0.0 copy-done.1
  42.0 0.9 %shard_map.66 = bf16[64,8,128]{2,1,0:T(8,128)(2,1)S(1)} custom-call(bf16[512,512]{1,0:T(8,128)(2,1)S(1)} %copy-done, bf16[256,256]{1,0:T(8,128)(2,1)S(1)} %copy-done.1, bf16[64,24,128]{2,1,0:T(8,128)(2,1)S(1)} %all-to-all-done.1.got_ref), custom_call_target="tpu_custom_call" | custom-call | flops 1 | tf_op jit(solution)/shard_map/pallas_call | solution.py:225
  42.9 15.9 %all_to_all.20.y_ref = bf16[64,8,128]{2,1,0:T(8,128)(2,1)S(1)} all-to-all(bf16[64,8,128]{2,1,0:T(8,128)(2,1)S(1)} %shard_map.66), channel_id=1, replica_groups={{36,37,38,39,32,33,34,35,44,45,46,47,40,41,42,43,52,53,54,55,48,49,50,5..., dimensions={0} | all-to-all | bytes 262144 | tf_op jit(solution)/shard_map/all_to_all | solution.py:175
  58.9 0.3 shard_map.68
  59.2 0.0 collective-permute-done.3.refs_2_
  59.2 0.0 collective-permute-done.2.refs_1_
  59.2 0.0 collective-permute-done.1.refs_0_
  59.2 0.4 shard_map.69
  59.6 16.5 %all_to_all.21 = f32[64,4,128]{2,1,0:T(4,128)S(1)} all-to-all(f32[64,4,128]{2,1,0:T(4,128)S(1)} %bitcast.19), channel_id=1, replica_groups={{36,37,38,39,32,33,34,35,44,45,46,47,40,41,42,43,52,53,54,55,48,49,50,5..., dimensions={0} | all-to-all | bytes 262144 | tf_op jit(solution)/shard_map/all_to_all | solution.py:175
  76.2 0.7 shard_map.70
  (3 shorter events, 0.1 us)
Async XLA Ops:
  1.6 8.4 %copy-start.2 = (bf16[64,4,256]{2,1,0:T(4,128)(2,1)S(1)}, bf16[64,4,256]{2,1,0:T(4,128)(2,1)}, u32[]{:S(2)}) copy-start(bf16[64,4,256]{2,1,0:T(4,128)(2,1)} %param.6) | copy-start | bytes 393220
  1.6 11.9 %all-to-all-start = ((bf16[8,80,128]{2,1,0:T(8,128)(2,1)}), bf16[8,80,128]{2,1,0:T(8,128)(2,1)S(1)}, u32[]{:S(2)}, u32[]{:S(2)}) async-start(bf16[8,80,128]{2,1,0:T(8,128)(2,1)} %shard_map.64), calls=%async_computation | async-start | bytes 327680 | tf_op jit(solution)/shard_map/all_to_all | solution.py:198
  9.1 0.7 copy-start.3
  10.2 20.4 %collective-permute-start = (bf16[64,1024]{1,0:T(8,128)(2,1)S(1)}, bf16[64,1024]{1,0:T(8,128)(2,1)S(1)}, u32[]{:S(2)}, u32[]{:S(2)}) collective-permute-start(bf16[64,1024]{1,0:T(8,128)(2,1)S(1)} %reshape.31.refs_0_), channel_id=1, source_target_pairs={{0,64},{64,0},{128,192},{192,128},{256,320},{320,256},{384,448},{4... | collective-permute-start | bytes 393224 | tf_op jit(solution)/shard_map/ppermute | solution.py:221
  14.4 27.6 %all-to-all-start.1 = ((bf16[64,24,128]{2,1,0:T(8,128)(2,1)}), bf16[64,24,128]{2,1,0:T(8,128)(2,1)S(1)}, u32[]{:S(2)}, u32[]{:S(2)}) async-start(bf16[64,24,128]{2,1,0:T(8,128)(2,1)} %shard_map.65), calls=%async_computation.1 | async-start | bytes 786432 | tf_op jit(solution)/shard_map/all_to_all | solution.py:175
  30.6 11.4 %copy-start = (bf16[512,512]{1,0:T(8,128)(2,1)S(1)}, bf16[512,512]{1,0:T(8,128)(2,1)}, u32[]{:S(2)}) copy-start(bf16[512,512]{1,0:T(8,128)(2,1)} %constant.47.clone.nu_ref) | copy-start | bytes 1572868
  30.6 11.4 %copy-start.1 = (bf16[256,256]{1,0:T(8,128)(2,1)S(1)}, bf16[256,256]{1,0:T(8,128)(2,1)}, u32[]{:S(2)}) copy-start(bf16[256,256]{1,0:T(8,128)(2,1)} %constant.51.l_ref) | copy-start | bytes 393220
  30.7 28.5 %collective-permute-start.3 = (bf16[128,1024]{1,0:T(8,128)(2,1)S(1)}, bf16[128,1024]{1,0:T(8,128)(2,1)S(1)}, u32[]{:S(2)}, u32[]{:S(2)}) collective-permute-start(bf16[128,1024]{1,0:T(8,128)(2,1)S(1)} %shard_map.67.pair_ref), channel_id=1, source_target_pairs={{0,384},{64,448},{128,0},{192,64},{256,128},{320,192},{384,256},{4... | collective-permute-start | bytes 786440 | tf_op jit(solution)/shard_map/ppermute | solution.py:223
  34.6 24.6 %collective-permute-start.2 = (bf16[128,1024]{1,0:T(8,128)(2,1)S(1)}, bf16[128,1024]{1,0:T(8,128)(2,1)S(1)}, u32[]{:S(2)}, u32[]{:S(2)}) collective-permute-start(bf16[128,1024]{1,0:T(8,128)(2,1)S(1)} %shard_map.67.pair_ref), channel_id=1, source_target_pairs={{0,256},{64,320},{128,384},{192,448},{256,0},{320,64},{384,128},{4... | collective-permute-start | bytes 786440 | tf_op jit(solution)/shard_map/ppermute | solution.py:223
  38.6 20.6 %collective-permute-start.1 = (bf16[128,1024]{1,0:T(8,128)(2,1)S(1)}, bf16[128,1024]{1,0:T(8,128)(2,1)S(1)}, u32[]{:S(2)}, u32[]{:S(2)}) collective-permute-start(bf16[128,1024]{1,0:T(8,128)(2,1)S(1)} %shard_map.67.pair_ref), channel_id=1, source_target_pairs={{0,128},{64,192},{128,256},{192,320},{256,384},{320,448},{384,0},{... | collective-permute-start | bytes 786440 | tf_op jit(solution)/shard_map/ppermute | solution.py:223

commit v8 on v7

--- a/solution.py
+++ b/solution.py
@@ -8,11 +8,12 @@
 
 TILE = 128
 START = 4
-ROWS = 1
+ROWS = 5
 COST_F = 1
 COST_A = 1
 COST_1 = 1
 COST_G = 10**10
+COST_H = 1
 GRID = ("col", "rep")
 LINE = 8
 BF16 = jnp.bfloat16
@@ -122,32 +123,28 @@
     out_ref[...] = y_ref[...].astype(BF16).reshape(groups, LINE, TILE)
 
 
-def near_kernel(y_ref, pair_ref, out_ref, flat_ref, wide_ref):
+def near_kernel(y_ref, near_ref, out_ref, flat_ref, wide_ref):
     count = y_ref.shape[0]
     wide_ref[...] = y_ref[...].reshape(count * LINE, TILE).astype(F32)
     picked = [wide_ref[pl.ds(line, count, stride=LINE), :].astype(BF16) for line in (0, 4, 1, 5, 2, 6, 3, 7)]
     flat = jnp.concatenate(picked, axis=1)
     flat_ref[...] = flat
-    place(flat, pair_ref, 0, out_ref)
-
-
-def far_kernel(flat_ref, part_ref, *refs):
-    out_ref = refs[-1]
+    place(flat, near_ref, 0, out_ref)
+
+
+def far_kernel(flat_ref, part_ref, far_ref, out_ref):
     out_ref[...] = part_ref[...]
-    for step, ref in enumerate(refs[:-1]):
-        place(flat_ref[...], ref, step + 1, out_ref)
-
-
-def place(flat, pair_ref, step, out_ref):
+    place(flat_ref[...], far_ref, 2, out_ref)
+
+
+def place(flat, held_ref, base, out_ref):
     count = flat.shape[0]
     half = count // 2
-    chip, core = lax.axis_index("row") // 2, lax.axis_index("row") % 2
-    part = dot(pair_ref[...], flat, NT)
-    for other in range(2):
-        rows = part[other * count :][:count]
+    part = dot(held_ref[...], flat, NT)
+    for index, mask in enumerate((0, 4, 1, 5)):
+        rows = part[index * count :][:count]
         wide = jnp.concatenate([rows[:half], rows[half:]], axis=1)
-        block = lax.rem(chip - step + 4, 4) * 2 + lax.rem(core + other, 2)
-        block = lax.rem(block + 8 - START, 8)
+        block = lax.rem((lax.axis_index("row") ^ (mask ^ base)) + 8 - START, 8)
         cut = START * 4
         wide = jnp.concatenate([wide[cut:], wide[:cut]], axis=0)
         out_ref[pl.ds(pl.multiple_of(block * half, half), half), :] = wide
@@ -218,9 +215,12 @@
             cost_estimate=cost(flops),
         )(*[held(part) for part in parts])
 
-    other = lax.ppermute(right, "row", [(r, r ^ 1) for r in range(rows)])
-    pair = gathered([right, other], COST_G)
-    along = [lax.ppermute(pair, "row", [(r, (r + 2 * step) % rows) for r in range(rows)]) for step in (1, 2, 3)]
+    def swap(array, bit):
+        return lax.ppermute(array, "row", [(r, r ^ bit) for r in range(rows)])
+
+    near = gathered([right, swap(right, 4)], COST_G)
+    near = gathered([near, swap(near, 1)], COST_H)
+    far = swap(near, 2)
     got = exchange(sent)
     product = pl.pallas_call(
         product_kernel,
@@ -241,14 +241,14 @@
         out_specs=(VMEM, VMEM),
         scratch_shapes=[pltpu.VMEM((groups * line, TILE), F32)],
         cost_estimate=cost(COST_A),
-    )(held(contracted), held(pair))
+    )(held(contracted), held(near))
     partial = pl.pallas_call(
         far_kernel,
         out_shape=pltpu.VMEM((groups * 4, TILE), F32),
-        in_specs=[VMEM] * 5,
+        in_specs=[VMEM] * 3,
         out_specs=VMEM,
         cost_estimate=cost(COST_F),
-    )(held(flat), held(partial), *[held(part) for part in along])
+    )(held(flat), held(partial), held(far))
     slices = exchange(partial.reshape(groups, 4, TILE))
     result = pl.pallas_call(
         sum_kernel,

time: 77.4 us -> 76.3 us (0.986)
  starting transfers between devices: 37 us -> 32.7 us
  waiting for transfers between devices: 1.34 us -> 4.36 us
    ppermute x4 -> x3, starting transfers between devices: 13.3 us -> 9.62 us  [swap(): return lax.ppermute(array, 'row', [(r, r ^ bit) for r in range(rows)])]
    all_to_all x1, waiting for transfers between devices: 0.01 us -> 2.85 us  [exchange(): lax.all_to_all(array, GRID, 0, 0, tiled=True, axis_index_groups=[order])]
    ppermute x4 -> x3, waiting for transfers between devices: 0.01 us -> 1.51 us  [swap(): return lax.ppermute(array, 'row', [(r, r ^ bit) for r in range(rows)])]
    all_to_all x1, waiting for transfers between devices: 1.33 us -> 0.01 us  [body(): lax.all_to_all(first, 'row', 0, 0, tiled=True, axis_index_groups=order)]
  transfers between devices with their start and end apart: 6 -> 5, of which waited for: 1 -> 2; matrix products, arithmetic and copies ran while one was open for 1% -> 1% of each run, Pallas kernels for 3% -> 3%
where the time goes in v8:
time: 76.3 us; the launch traced here: 75.8 us
  starting transfers between devices  32.7 us (43%)
  blocking collectives  32.6 us (43%)
  Pallas kernels  4.81 us (6%)
  waiting for transfers between devices  4.36 us (6%)
  local copies, waits for them, and re-layouts  0.91 us (1%)
    all_to_all x2, blocking collectives, exchange(): lax.all_to_all(array, GRID, 0, 0, tiled=True, axis_index_groups=[order])  32.6 us
    all_to_all x1, starting transfers between devices, exchange(): lax.all_to_all(array, GRID, 0, 0, tiled=True, axis_index_groups=[order])  15.7 us
    ppermute x3, starting transfers between devices, swap(): return lax.ppermute(array, 'row', [(r, r ^ bit) for r in range(rows)])  9.62 us
    all_to_all x1, starting transfers between devices, body(): lax.all_to_all(first, 'row', 0, 0, tiled=True, axis_index_groups=order)  7.4 us
    all_to_all x1, waiting for transfers between devices, exchange(): lax.all_to_all(array, GRID, 0, 0, tiled=True, axis_index_groups=[order])  2.85 us
    pallas_call x1, Pallas kernels, body(): pl.pallas_call(first_kernel, out_shape=pltpu.VMEM((rows, row_count // row...  1.62 us
  transfers between devices with their start and end apart: 5, of which 2 were waited for; matrix products, arithmetic and copies ran while one was open for 1% of the time, Pallas kernels for 3%

profile of v8, /device:TPU:4, one launch (start us, length us, event | category | flops | bytes accessed | tf_op | source)
XLA Modules:
  0.0 75.8 jit_solution(4447088324223269350)
XLA Ops:
  0.0 1.6 %shard_map.64 = bf16[8,80,128]{2,1,0:T(8,128)(2,1)} custom-call(s32[2,2,4]{2,1,0:T(2,128)} %bitcast.23, s32[2,2,2]{2,1,0:T(2,128)} %green_ref.1, bf16[8,64,128]{2,1,0:T(8,128)(2,1)} %bitcast.21, bf16[16,128]{1,0:T(8,128)(2,1)} %bitcast.24), custom_call_target="tpu_custom_call" | custom-call | tf_op jit(solution)/shard_map/pallas_call | solution.py:188
  1.6 0.0 copy-start.2
  1.6 7.4 %all-to-all-start = ((bf16[8,80,128]{2,1,0:T(8,128)(2,1)}), bf16[8,80,128]{2,1,0:T(8,128)(2,1)S(1)}, u32[]{:S(2)}, u32[]{:S(2)}) async-start(bf16[8,80,128]{2,1,0:T(8,128)(2,1)} %shard_map.64), calls=%async_computation | async-start | bytes 327680 | tf_op jit(solution)/shard_map/all_to_all | solution.py:195
  9.0 0.0 copy-start.3
  9.0 0.7 copy-done.3
  9.7 0.2 fusion
  9.9 0.1 broadcast_bitcast_fusion
  10.0 0.0 copy-done.2
  10.0 0.1 broadcast_multiply_fusion
  10.0 0.1 reshape.30
  10.2 5.1 %collective-permute-start = (bf16[64,1024]{1,0:T(8,128)(2,1)S(1)}, bf16[64,1024]{1,0:T(8,128)(2,1)S(1)}, u32[]{:S(2)}, u32[]{:S(2)}) collective-permute-start(bf16[64,1024]{1,0:T(8,128)(2,1)S(1)} %reshape.31.refs_0_), channel_id=1, source_target_pairs={{0,256},{64,320},{128,384},{192,448},{256,0},{320,64},{384,128},{4... | collective-permute-start | bytes 393224 | tf_op jit(solution)/shard_map/ppermute | solution.py:219
  15.3 0.0 all-to-all-done.got_ref
  15.3 0.8 %shard_map.65 = bf16[64,24,128]{2,1,0:T(8,128)(2,1)} custom-call(bf16[8,80,128]{2,1,0:T(8,128)(2,1)S(1)} %all-to-all-done.got_ref), custom_call_target="tpu_custom_call" | custom-call | tf_op jit(solution)/shard_map/pallas_call | solution.py:196
  16.1 15.7 %all-to-all-start.1 = ((bf16[64,24,128]{2,1,0:T(8,128)(2,1)}), bf16[64,24,128]{2,1,0:T(8,128)(2,1)S(1)}, u32[]{:S(2)}, u32[]{:S(2)}) async-start(bf16[64,24,128]{2,1,0:T(8,128)(2,1)} %shard_map.65), calls=%async_computation.1 | async-start | bytes 786432 | tf_op jit(solution)/shard_map/all_to_all | solution.py:172
  31.8 0.0 collective-permute-done.refs_1_
  31.9 0.0 copy-start
  31.9 0.0 copy-start.1
  31.9 2.1 %collective-permute-start.1 = (bf16[128,1024]{1,0:T(8,128)(2,1)S(1)}, bf16[128,1024]{1,0:T(8,128)(2,1)S(1)}, u32[]{:S(2)}, u32[]{:S(2)}) collective-permute-start(bf16[128,1024]{1,0:T(8,128)(2,1)S(1)} %shard_map.67.refs_0_), channel_id=1, source_target_pairs={{0,64},{64,0},{128,192},{192,128},{256,320},{320,256},{384,448},{4... | collective-permute-start | bytes 786440 | tf_op jit(solution)/shard_map/ppermute | solution.py:219
  33.9 1.5 %collective-permute-done.1.refs_1_ = bf16[128,1024]{1,0:T(8,128)(2,1)S(1)} collective-permute-done((bf16[128,1024]{1,0:T(8,128)(2,1)S(1)}, bf16[128,1024]{1,0:T(8,128)(2,1)S(1)}, u32[]{:S(2)}, u32[]{:S(2)}) %collective-permute-start.1) | collective-permute-done | bytes 262176 | tf_op jit(solution)/shard_map/ppermute | solution.py:219
  35.5 2.5 %collective-permute-start.2 = (bf16[256,1024]{1,0:T(8,128)(2,1)S(1)}, bf16[256,1024]{1,0:T(8,128)(2,1)S(1)}, u32[]{:S(2)}, u32[]{:S(2)}) collective-permute-start(bf16[256,1024]{1,0:T(8,128)(2,1)S(1)} %shard_map.68.near_ref), channel_id=1, source_target_pairs={{0,128},{64,192},{128,0},{192,64},{256,384},{320,448},{384,256},{4... | collective-permute-start | bytes 1572872 | tf_op jit(solution)/shard_map/ppermute | solution.py:219
  38.0 2.8 %all-to-all-done.1.got_ref = bf16[64,24,128]{2,1,0:T(8,128)(2,1)S(1)} async-done(((bf16[64,24,128]{2,1,0:T(8,128)(2,1)}), bf16[64,24,128]{2,1,0:T(8,128)(2,1)S(1)}, u32[]{:S(2)}, u32[]{:S(2)}) %all-to-all-start.1) | async-done | bytes 393248 | tf_op jit(solution)/shard_map/all_to_all | solution.py:172
  40.8 0.0 copy-done
  40.8 0.0 copy-done.1
  40.8 0.9 %shard_map.66 = bf16[64,8,128]{2,1,0:T(8,128)(2,1)S(1)} custom-call(bf16[512,512]{1,0:T(8,128)(2,1)S(1)} %copy-done, bf16[256,256]{1,0:T(8,128)(2,1)S(1)} %copy-done.1, bf16[64,24,128]{2,1,0:T(8,128)(2,1)S(1)} %all-to-all-done.1.got_ref), custom_call_target="tpu_custom_call" | custom-call | flops 1 | tf_op jit(solution)/shard_map/pallas_call | solution.py:225
  41.8 16.1 %all_to_all.20.y_ref = bf16[64,8,128]{2,1,0:T(8,128)(2,1)S(1)} all-to-all(bf16[64,8,128]{2,1,0:T(8,128)(2,1)S(1)} %shard_map.66), channel_id=1, replica_groups={{36,37,38,39,32,33,34,35,44,45,46,47,40,41,42,43,52,53,54,55,48,49,50,5..., dimensions={0} | all-to-all | bytes 262144 | tf_op jit(solution)/shard_map/all_to_all | solution.py:172
  57.9 0.4 shard_map.69
  58.2 0.0 collective-permute-done.2.far_ref
  58.2 0.3 shard_map.70
  58.6 16.5 %all_to_all.21 = f32[64,4,128]{2,1,0:T(4,128)S(1)} all-to-all(f32[64,4,128]{2,1,0:T(4,128)S(1)} %bitcast.19), channel_id=1, replica_groups={{36,37,38,39,32,33,34,35,44,45,46,47,40,41,42,43,52,53,54,55,48,49,50,5..., dimensions={0} | all-to-all | bytes 262144 | tf_op jit(solution)/shard_map/all_to_all | solution.py:172
  75.1 0.7 shard_map.71
  (4 shorter events, 0.1 us)
Async XLA Ops:
  1.6 8.3 %copy-start.2 = (bf16[64,4,256]{2,1,0:T(4,128)(2,1)S(1)}, bf16[64,4,256]{2,1,0:T(4,128)(2,1)}, u32[]{:S(2)}) copy-start(bf16[64,4,256]{2,1,0:T(4,128)(2,1)} %param.6) | copy-start | bytes 393220
  1.6 13.7 %all-to-all-start = ((bf16[8,80,128]{2,1,0:T(8,128)(2,1)}), bf16[8,80,128]{2,1,0:T(8,128)(2,1)S(1)}, u32[]{:S(2)}, u32[]{:S(2)}) async-start(bf16[8,80,128]{2,1,0:T(8,128)(2,1)} %shard_map.64), calls=%async_computation | async-start | bytes 327680 | tf_op jit(solution)/shard_map/all_to_all | solution.py:195
  9.0 0.7 copy-start.3
  10.2 21.6 %collective-permute-start = (bf16[64,1024]{1,0:T(8,128)(2,1)S(1)}, bf16[64,1024]{1,0:T(8,128)(2,1)S(1)}, u32[]{:S(2)}, u32[]{:S(2)}) collective-permute-start(bf16[64,1024]{1,0:T(8,128)(2,1)S(1)} %reshape.31.refs_0_), channel_id=1, source_target_pairs={{0,256},{64,320},{128,384},{192,448},{256,0},{320,64},{384,128},{4... | collective-permute-start | bytes 393224 | tf_op jit(solution)/shard_map/ppermute | solution.py:219
  16.1 24.7 %all-to-all-start.1 = ((bf16[64,24,128]{2,1,0:T(8,128)(2,1)}), bf16[64,24,128]{2,1,0:T(8,128)(2,1)S(1)}, u32[]{:S(2)}, u32[]{:S(2)}) async-start(bf16[64,24,128]{2,1,0:T(8,128)(2,1)} %shard_map.65), calls=%async_computation.1 | async-start | bytes 786432 | tf_op jit(solution)/shard_map/all_to_all | solution.py:172
  31.9 9.0 %copy-start = (bf16[512,512]{1,0:T(8,128)(2,1)S(1)}, bf16[512,512]{1,0:T(8,128)(2,1)}, u32[]{:S(2)}) copy-start(bf16[512,512]{1,0:T(8,128)(2,1)} %constant.47.clone.nu_ref) | copy-start | bytes 1572868
  31.9 9.0 %copy-start.1 = (bf16[256,256]{1,0:T(8,128)(2,1)S(1)}, bf16[256,256]{1,0:T(8,128)(2,1)}, u32[]{:S(2)}) copy-start(bf16[256,256]{1,0:T(8,128)(2,1)} %constant.51.l_ref) | copy-start | bytes 393220
  31.9 3.6 %collective-permute-start.1 = (bf16[128,1024]{1,0:T(8,128)(2,1)S(1)}, bf16[128,1024]{1,0:T(8,128)(2,1)S(1)}, u32[]{:S(2)}, u32[]{:S(2)}) collective-permute-start(bf16[128,1024]{1,0:T(8,128)(2,1)S(1)} %shard_map.67.refs_0_), channel_id=1, source_target_pairs={{0,64},{64,0},{128,192},{192,128},{256,320},{320,256},{384,448},{4... | collective-permute-start | bytes 786440 | tf_op jit(solution)/shard_map/ppermute | solution.py:219
  35.5 22.8 %collective-permute-start.2 = (bf16[256,1024]{1,0:T(8,128)(2,1)S(1)}, bf16[256,1024]{1,0:T(8,128)(2,1)S(1)}, u32[]{:S(2)}, u32[]{:S(2)}) collective-permute-start(bf16[256,1024]{1,0:T(8,128)(2,1)S(1)} %shard_map.68.near_ref), channel_id=1, source_target_pairs={{0,128},{64,192},{128,0},{192,64},{256,384},{320,448},{384,256},{4... | collective-permute-start | bytes 1572872 | tf_op jit(solution)/shard_map/ppermute | solution.py:219

commit v9 on v8

--- a/solution.py
+++ b/solution.py
@@ -95,8 +95,8 @@
     got = got_ref[...]
     rows = dot(nu_ref[...], got[:, 2 * LINE :].reshape(size, TILE)).astype(BF16)
     virtual = jnp.concatenate([rows[: size // 2], rows[size // 2 :]], axis=1)
-    m_ref[...] = got[:, :LINE].reshape(size, TILE).astype(F32)
-    o_ref[...] = got[:, LINE : 2 * LINE].reshape(size, TILE).astype(F32)
+    m_ref[:size] = got[:, :LINE].reshape(size, TILE).astype(F32)
+    o_ref[:size] = got[:, LINE : 2 * LINE].reshape(size, TILE).astype(F32)
     mine = [
         jnp.concatenate([m_ref[pl.ds(half * 4 + i, groups, stride=LINE), :] for i in range(4)], axis=0)
         for half in range(2)
@@ -120,12 +120,12 @@
         for half in range(2):
             block = product[i * groups : (i + 1) * groups, half * TILE : (half + 1) * TILE]
             y_ref[pl.ds(half * 4 + i, groups, stride=LINE), :] = block
-    out_ref[...] = y_ref[...].astype(BF16).reshape(groups, LINE, TILE)
+    out_ref[...] = y_ref[:size].astype(BF16).reshape(groups, LINE, TILE)
 
 
 def near_kernel(y_ref, near_ref, out_ref, flat_ref, wide_ref):
     count = y_ref.shape[0]
-    wide_ref[...] = y_ref[...].reshape(count * LINE, TILE).astype(F32)
+    wide_ref[: count * LINE] = y_ref[...].reshape(count * LINE, TILE).astype(F32)
     picked = [wide_ref[pl.ds(line, count, stride=LINE), :].astype(BF16) for line in (0, 4, 1, 5, 2, 6, 3, 7)]
     flat = jnp.concatenate(picked, axis=1)
     flat_ref[...] = flat
@@ -227,7 +227,7 @@
         out_shape=pltpu.VMEM((groups, line, TILE), BF16),
         in_specs=[VMEM, VMEM, VMEM],
         out_specs=VMEM,
-        scratch_shapes=[pltpu.VMEM((groups * line, TILE), F32)] * 3,
+        scratch_shapes=[pltpu.VMEM((groups * line + rows * line, TILE), F32)] * 3,
         cost_estimate=cost(COST_1),
     )(held(pick(nu_order)), held(pick(l_order).T), held(got))
     contracted = exchange(product)
@@ -239,7 +239,7 @@
         ),
         in_specs=[VMEM] * 2,
         out_specs=(VMEM, VMEM),
-        scratch_shapes=[pltpu.VMEM((groups * line, TILE), F32)],
+        scratch_shapes=[pltpu.VMEM((groups * line + rows * line, TILE), F32)],
         cost_estimate=cost(COST_A),
     )(held(contracted), held(near))
     partial = pl.pallas_call(

time: 76.3 us -> 76.3 us (level)
  no operation moved by 1% of the time
where the time goes in v9:
time: 76.3 us; the launch traced here: 75.8 us
  starting transfers between devices  32.7 us (43%)
  blocking collectives  32.6 us (43%)
  Pallas kernels  4.81 us (6%)
  waiting for transfers between devices  4.36 us (6%)
  local copies, waits for them, and re-layouts  0.91 us (1%)
    all_to_all x2, blocking collectives, exchange(): lax.all_to_all(array, GRID, 0, 0, tiled=True, axis_index_groups=[order])  32.6 us
    all_to_all x1, starting transfers between devices, exchange(): lax.all_to_all(array, GRID, 0, 0, tiled=True, axis_index_groups=[order])  15.7 us
    ppermute x3, starting transfers between devices, swap(): return lax.ppermute(array, 'row', [(r, r ^ bit) for r in range(rows)])  9.62 us
    all_to_all x1, starting transfers between devices, body(): lax.all_to_all(first, 'row', 0, 0, tiled=True, axis_index_groups=order)  7.4 us
    all_to_all x1, waiting for transfers between devices, exchange(): lax.all_to_all(array, GRID, 0, 0, tiled=True, axis_index_groups=[order])  2.85 us
    pallas_call x1, Pallas kernels, body(): pl.pallas_call(first_kernel, out_shape=pltpu.VMEM((rows, row_count // row...  1.62 us
  transfers between devices with their start and end apart: 5, of which 2 were waited for; matrix products, arithmetic and copies ran while one was open for 1% of the time, Pallas kernels for 3%

profile of v9, /device:TPU:4, one launch (start us, length us, event | category | flops | bytes accessed | tf_op | source)
XLA Modules:
  0.0 75.8 jit_solution(13402070403844883084)
XLA Ops:
  0.0 1.6 %shard_map.64 = bf16[8,80,128]{2,1,0:T(8,128)(2,1)} custom-call(s32[2,2,4]{2,1,0:T(2,128)} %bitcast.23, s32[2,2,2]{2,1,0:T(2,128)} %green_ref.1, bf16[8,64,128]{2,1,0:T(8,128)(2,1)} %bitcast.21, bf16[16,128]{1,0:T(8,128)(2,1)} %bitcast.24), custom_call_target="tpu_custom_call" | custom-call | tf_op jit(solution)/shard_map/pallas_call | solution.py:188
  1.6 0.0 copy-start.2
  1.6 7.4 %all-to-all-start = ((bf16[8,80,128]{2,1,0:T(8,128)(2,1)}), bf16[8,80,128]{2,1,0:T(8,128)(2,1)S(1)}, u32[]{:S(2)}, u32[]{:S(2)}) async-start(bf16[8,80,128]{2,1,0:T(8,128)(2,1)} %shard_map.64), calls=%async_computation | async-start | bytes 327680 | tf_op jit(solution)/shard_map/all_to_all | solution.py:195
  9.0 0.0 copy-start.3
  9.0 0.7 copy-done.3
  9.7 0.2 fusion
  9.9 0.1 broadcast_bitcast_fusion
  10.0 0.0 copy-done.2
  10.0 0.1 broadcast_multiply_fusion
  10.0 0.1 reshape.30
  10.2 5.1 %collective-permute-start = (bf16[64,1024]{1,0:T(8,128)(2,1)S(1)}, bf16[64,1024]{1,0:T(8,128)(2,1)S(1)}, u32[]{:S(2)}, u32[]{:S(2)}) collective-permute-start(bf16[64,1024]{1,0:T(8,128)(2,1)S(1)} %reshape.31.refs_0_), channel_id=1, source_target_pairs={{0,256},{64,320},{128,384},{192,448},{256,0},{320,64},{384,128},{4... | collective-permute-start | bytes 393224 | tf_op jit(solution)/shard_map/ppermute | solution.py:219
  15.3 0.0 all-to-all-done.got_ref
  15.3 0.8 %shard_map.65 = bf16[64,24,128]{2,1,0:T(8,128)(2,1)} custom-call(bf16[8,80,128]{2,1,0:T(8,128)(2,1)S(1)} %all-to-all-done.got_ref), custom_call_target="tpu_custom_call" | custom-call | tf_op jit(solution)/shard_map/pallas_call | solution.py:196
  16.1 15.7 %all-to-all-start.1 = ((bf16[64,24,128]{2,1,0:T(8,128)(2,1)}), bf16[64,24,128]{2,1,0:T(8,128)(2,1)S(1)}, u32[]{:S(2)}, u32[]{:S(2)}) async-start(bf16[64,24,128]{2,1,0:T(8,128)(2,1)} %shard_map.65), calls=%async_computation.1 | async-start | bytes 786432 | tf_op jit(solution)/shard_map/all_to_all | solution.py:172
  31.8 0.0 collective-permute-done.refs_1_
  31.9 0.0 copy-start
  31.9 0.0 copy-start.1
  31.9 2.1 %collective-permute-start.1 = (bf16[128,1024]{1,0:T(8,128)(2,1)S(1)}, bf16[128,1024]{1,0:T(8,128)(2,1)S(1)}, u32[]{:S(2)}, u32[]{:S(2)}) collective-permute-start(bf16[128,1024]{1,0:T(8,128)(2,1)S(1)} %shard_map.67.refs_0_), channel_id=1, source_target_pairs={{0,64},{64,0},{128,192},{192,128},{256,320},{320,256},{384,448},{4... | collective-permute-start | bytes 786440 | tf_op jit(solution)/shard_map/ppermute | solution.py:219
  33.9 1.5 %collective-permute-done.1.refs_1_ = bf16[128,1024]{1,0:T(8,128)(2,1)S(1)} collective-permute-done((bf16[128,1024]{1,0:T(8,128)(2,1)S(1)}, bf16[128,1024]{1,0:T(8,128)(2,1)S(1)}, u32[]{:S(2)}, u32[]{:S(2)}) %collective-permute-start.1) | collective-permute-done | bytes 262176 | tf_op jit(solution)/shard_map/ppermute | solution.py:219
  35.5 2.5 %collective-permute-start.2 = (bf16[256,1024]{1,0:T(8,128)(2,1)S(1)}, bf16[256,1024]{1,0:T(8,128)(2,1)S(1)}, u32[]{:S(2)}, u32[]{:S(2)}) collective-permute-start(bf16[256,1024]{1,0:T(8,128)(2,1)S(1)} %shard_map.68.near_ref), channel_id=1, source_target_pairs={{0,128},{64,192},{128,0},{192,64},{256,384},{320,448},{384,256},{4... | collective-permute-start | bytes 1572872 | tf_op jit(solution)/shard_map/ppermute | solution.py:219
  38.0 2.8 %all-to-all-done.1.got_ref = bf16[64,24,128]{2,1,0:T(8,128)(2,1)S(1)} async-done(((bf16[64,24,128]{2,1,0:T(8,128)(2,1)}), bf16[64,24,128]{2,1,0:T(8,128)(2,1)S(1)}, u32[]{:S(2)}, u32[]{:S(2)}) %all-to-all-start.1) | async-done | bytes 393248 | tf_op jit(solution)/shard_map/all_to_all | solution.py:172
  40.8 0.0 copy-done
  40.8 0.0 copy-done.1
  40.8 0.9 %shard_map.66 = bf16[64,8,128]{2,1,0:T(8,128)(2,1)S(1)} custom-call(bf16[512,512]{1,0:T(8,128)(2,1)S(1)} %copy-done, bf16[256,256]{1,0:T(8,128)(2,1)S(1)} %copy-done.1, bf16[64,24,128]{2,1,0:T(8,128)(2,1)S(1)} %all-to-all-done.1.got_ref), custom_call_target="tpu_custom_call" | custom-call | flops 1 | tf_op jit(solution)/shard_map/pallas_call | solution.py:225
  41.8 16.1 %all_to_all.20.y_ref = bf16[64,8,128]{2,1,0:T(8,128)(2,1)S(1)} all-to-all(bf16[64,8,128]{2,1,0:T(8,128)(2,1)S(1)} %shard_map.66), channel_id=1, replica_groups={{36,37,38,39,32,33,34,35,44,45,46,47,40,41,42,43,52,53,54,55,48,49,50,5..., dimensions={0} | all-to-all | bytes 262144 | tf_op jit(solution)/shard_map/all_to_all | solution.py:172
  57.9 0.4 shard_map.69
  58.2 0.0 collective-permute-done.2.far_ref
  58.2 0.3 shard_map.70
  58.6 16.5 %all_to_all.21 = f32[64,4,128]{2,1,0:T(4,128)S(1)} all-to-all(f32[64,4,128]{2,1,0:T(4,128)S(1)} %bitcast.19), channel_id=1, replica_groups={{36,37,38,39,32,33,34,35,44,45,46,47,40,41,42,43,52,53,54,55,48,49,50,5..., dimensions={0} | all-to-all | bytes 262144 | tf_op jit(solution)/shard_map/all_to_all | solution.py:172
  75.1 0.7 shard_map.71
  (4 shorter events, 0.1 us)
Async XLA Ops:
  1.6 8.3 %copy-start.2 = (bf16[64,4,256]{2,1,0:T(4,128)(2,1)S(1)}, bf16[64,4,256]{2,1,0:T(4,128)(2,1)}, u32[]{:S(2)}) copy-start(bf16[64,4,256]{2,1,0:T(4,128)(2,1)} %param.6) | copy-start | bytes 393220
  1.6 13.7 %all-to-all-start = ((bf16[8,80,128]{2,1,0:T(8,128)(2,1)}), bf16[8,80,128]{2,1,0:T(8,128)(2,1)S(1)}, u32[]{:S(2)}, u32[]{:S(2)}) async-start(bf16[8,80,128]{2,1,0:T(8,128)(2,1)} %shard_map.64), calls=%async_computation | async-start | bytes 327680 | tf_op jit(solution)/shard_map/all_to_all | solution.py:195
  9.0 0.7 copy-start.3
  10.2 21.6 %collective-permute-start = (bf16[64,1024]{1,0:T(8,128)(2,1)S(1)}, bf16[64,1024]{1,0:T(8,128)(2,1)S(1)}, u32[]{:S(2)}, u32[]{:S(2)}) collective-permute-start(bf16[64,1024]{1,0:T(8,128)(2,1)S(1)} %reshape.31.refs_0_), channel_id=1, source_target_pairs={{0,256},{64,320},{128,384},{192,448},{256,0},{320,64},{384,128},{4... | collective-permute-start | bytes 393224 | tf_op jit(solution)/shard_map/ppermute | solution.py:219
  16.1 24.7 %all-to-all-start.1 = ((bf16[64,24,128]{2,1,0:T(8,128)(2,1)}), bf16[64,24,128]{2,1,0:T(8,128)(2,1)S(1)}, u32[]{:S(2)}, u32[]{:S(2)}) async-start(bf16[64,24,128]{2,1,0:T(8,128)(2,1)} %shard_map.65), calls=%async_computation.1 | async-start | bytes 786432 | tf_op jit(solution)/shard_map/all_to_all | solution.py:172
  31.9 9.0 %copy-start = (bf16[512,512]{1,0:T(8,128)(2,1)S(1)}, bf16[512,512]{1,0:T(8,128)(2,1)}, u32[]{:S(2)}) copy-start(bf16[512,512]{1,0:T(8,128)(2,1)} %constant.47.clone.nu_ref) | copy-start | bytes 1572868
  31.9 9.0 %copy-start.1 = (bf16[256,256]{1,0:T(8,128)(2,1)S(1)}, bf16[256,256]{1,0:T(8,128)(2,1)}, u32[]{:S(2)}) copy-start(bf16[256,256]{1,0:T(8,128)(2,1)} %constant.51.l_ref) | copy-start | bytes 393220
  31.9 3.6 %collective-permute-start.1 = (bf16[128,1024]{1,0:T(8,128)(2,1)S(1)}, bf16[128,1024]{1,0:T(8,128)(2,1)S(1)}, u32[]{:S(2)}, u32[]{:S(2)}) collective-permute-start(bf16[128,1024]{1,0:T(8,128)(2,1)S(1)} %shard_map.67.refs_0_), channel_id=1, source_target_pairs={{0,64},{64,0},{128,192},{192,128},{256,320},{320,256},{384,448},{4... | collective-permute-start | bytes 786440 | tf_op jit(solution)/shard_map/ppermute | solution.py:219
  35.5 22.8 %collective-permute-start.2 = (bf16[256,1024]{1,0:T(8,128)(2,1)S(1)}, bf16[256,1024]{1,0:T(8,128)(2,1)S(1)}, u32[]{:S(2)}, u32[]{:S(2)}) collective-permute-start(bf16[256,1024]{1,0:T(8,128)(2,1)S(1)} %shard_map.68.near_ref), channel_id=1, source_target_pairs={{0,128},{64,192},{128,0},{192,64},{256,384},{320,448},{384,256},{4... | collective-permute-start | bytes 1572872 | tf_op jit(solution)/shard_map/ppermute | solution.py:219

commit v10 on v9

--- a/solution.py
+++ b/solution.py
@@ -12,7 +12,7 @@
 COST_F = 1
 COST_A = 1
 COST_1 = 1
-COST_G = 10**10
+COST_G = 2 * 10**9
 COST_H = 1
 GRID = ("col", "rep")
 LINE = 8
@@ -202,9 +202,11 @@
 
     mu_tile = lax.axis_index(GRID) * mu_block // TILE
     keep_own = jnp.repeat(tile_mask[row * row_count // TILE, mu_tile].astype(BF16), TILE)
-    right = m_tensor * keep_own[None, None, :]
-    right = right.reshape(rows, 2, row_count // rows // 2, mu_block * ao_count).transpose(1, 0, 2, 3)
-    right = right.reshape(row_count, mu_block * ao_count)
+    masked = m_tensor * keep_own[None, None, :]
+
+    def flat_rows(block):
+        block = block.reshape(rows, 2, row_count // rows // 2, mu_block * ao_count)
+        return block.transpose(1, 0, 2, 3).reshape(row_count, mu_block * ao_count)
 
     def gathered(parts, flops):
         return pl.pallas_call(
@@ -218,7 +220,7 @@
     def swap(array, bit):
         return lax.ppermute(array, "row", [(r, r ^ bit) for r in range(rows)])
 
-    near = gathered([right, swap(right, 4)], COST_G)
+    near = gathered([flat_rows(masked), flat_rows(swap(masked, 4))], COST_G)
     near = gathered([near, swap(near, 1)], COST_H)
     far = swap(near, 2)
     got = exchange(sent)

time: 76.3 us -> 76.1 us (level)
  no operation moved by 1% of the time
where the time goes in v10:
time: 76.1 us; the launch traced here: 75.6 us
  starting transfers between devices  32.8 us (43%)
  blocking collectives  32.6 us (43%)
  Pallas kernels  4.81 us (6%)
  waiting for transfers between devices  4 us (5%)
  local copies, waits for them, and re-layouts  1.06 us (1%)
    all_to_all x2, blocking collectives, exchange(): lax.all_to_all(array, GRID, 0, 0, tiled=True, axis_index_groups=[order])  32.6 us
    all_to_all x1, starting transfers between devices, exchange(): lax.all_to_all(array, GRID, 0, 0, tiled=True, axis_index_groups=[order])  15.7 us
    ppermute x3, starting transfers between devices, swap(): return lax.ppermute(array, 'row', [(r, r ^ bit) for r in range(rows)])  9.66 us
    all_to_all x1, starting transfers between devices, body(): lax.all_to_all(first, 'row', 0, 0, tiled=True, axis_index_groups=order)  7.4 us
    all_to_all x1, waiting for transfers between devices, exchange(): lax.all_to_all(array, GRID, 0, 0, tiled=True, axis_index_groups=[order])  2.49 us
    pallas_call x1, Pallas kernels, body(): pl.pallas_call(first_kernel, out_shape=pltpu.VMEM((rows, row_count // row...  1.62 us
  transfers between devices with their start and end apart: 5, of which 2 were waited for; matrix products, arithmetic and copies ran while one was open for 1% of the time, Pallas kernels for 3%

profile of v10, /device:TPU:4, one launch (start us, length us, event | category | flops | bytes accessed | tf_op | source)
XLA Modules:
  0.0 75.6 jit_solution(17493233903707342625)
XLA Ops:
  0.0 1.6 %shard_map.64 = bf16[8,80,128]{2,1,0:T(8,128)(2,1)} custom-call(s32[2,2,4]{2,1,0:T(2,128)} %bitcast.27, s32[2,2,2]{2,1,0:T(2,128)} %green_ref.1, bf16[8,64,128]{2,1,0:T(8,128)(2,1)} %bitcast.24, bf16[16,128]{1,0:T(8,128)(2,1)} %bitcast.28), custom_call_target="tpu_custom_call" | custom-call | tf_op jit(solution)/shard_map/pallas_call | solution.py:188
  1.6 0.0 copy-start.2
  1.6 7.4 %all-to-all-start = ((bf16[8,80,128]{2,1,0:T(8,128)(2,1)}), bf16[8,80,128]{2,1,0:T(8,128)(2,1)S(1)}, u32[]{:S(2)}, u32[]{:S(2)}) async-start(bf16[8,80,128]{2,1,0:T(8,128)(2,1)} %shard_map.64), calls=%async_computation | async-start | bytes 327680 | tf_op jit(solution)/shard_map/all_to_all | solution.py:195
  9.0 0.0 copy-start.3
  9.0 0.7 copy-done.3
  9.7 0.2 fusion
  9.9 0.1 broadcast_bitcast_fusion
  10.0 0.0 copy-done.2
  10.0 0.1 broadcast_multiply_fusion
  10.0 5.1 %collective-permute-start = (bf16[64,4,256]{2,1,0:T(4,128)(2,1)S(1)}, bf16[64,4,256]{2,1,0:T(4,128)(2,1)S(1)}, u32[]{:S(2)}, u32[]{:S(2)}) collective-permute-start(bf16[64,4,256]{2,1,0:T(4,128)(2,1)S(1)} %broadcast_multiply_fusion), channel_id=1, source_target_pairs={{0,256},{64,320},{128,384},{192,448},{256,0},{320,64},{384,128},{4... | collective-permute-start | bytes 393224 | tf_op jit(solution)/shard_map/ppermute | solution.py:221
  15.1 0.0 all-to-all-done.got_ref
  15.1 0.8 %shard_map.65 = bf16[64,24,128]{2,1,0:T(8,128)(2,1)} custom-call(bf16[8,80,128]{2,1,0:T(8,128)(2,1)S(1)} %all-to-all-done.got_ref), custom_call_target="tpu_custom_call" | custom-call | tf_op jit(solution)/shard_map/pallas_call | solution.py:196
  15.9 15.7 %all-to-all-start.1 = ((bf16[64,24,128]{2,1,0:T(8,128)(2,1)}), bf16[64,24,128]{2,1,0:T(8,128)(2,1)S(1)}, u32[]{:S(2)}, u32[]{:S(2)}) async-start(bf16[64,24,128]{2,1,0:T(8,128)(2,1)} %shard_map.65), calls=%async_computation.1 | async-start | bytes 786432 | tf_op jit(solution)/shard_map/all_to_all | solution.py:172
  31.7 0.1 reshape.36
  31.8 0.0 collective-permute-done
  31.8 0.1 reshape.38
  32.0 0.0 copy-start
  32.0 0.0 copy-start.1
  32.0 2.1 %collective-permute-start.1 = (bf16[128,1024]{1,0:T(8,128)(2,1)S(1)}, bf16[128,1024]{1,0:T(8,128)(2,1)S(1)}, u32[]{:S(2)}, u32[]{:S(2)}) collective-permute-start(bf16[128,1024]{1,0:T(8,128)(2,1)S(1)} %shard_map.67.refs_0_), channel_id=1, source_target_pairs={{0,64},{64,0},{128,192},{192,128},{256,320},{320,256},{384,448},{4... | collective-permute-start | bytes 786440 | tf_op jit(solution)/shard_map/ppermute | solution.py:221
  34.1 1.5 %collective-permute-done.1.refs_1_ = bf16[128,1024]{1,0:T(8,128)(2,1)S(1)} collective-permute-done((bf16[128,1024]{1,0:T(8,128)(2,1)S(1)}, bf16[128,1024]{1,0:T(8,128)(2,1)S(1)}, u32[]{:S(2)}, u32[]{:S(2)}) %collective-permute-start.1) | collective-permute-done | bytes 262176 | tf_op jit(solution)/shard_map/ppermute | solution.py:221
  35.6 2.5 %collective-permute-start.2 = (bf16[256,1024]{1,0:T(8,128)(2,1)S(1)}, bf16[256,1024]{1,0:T(8,128)(2,1)S(1)}, u32[]{:S(2)}, u32[]{:S(2)}) collective-permute-start(bf16[256,1024]{1,0:T(8,128)(2,1)S(1)} %shard_map.68.near_ref), channel_id=1, source_target_pairs={{0,128},{64,192},{128,0},{192,64},{256,384},{320,448},{384,256},{4... | collective-permute-start | bytes 1572872 | tf_op jit(solution)/shard_map/ppermute | solution.py:221
  38.2 2.5 %all-to-all-done.1.got_ref = bf16[64,24,128]{2,1,0:T(8,128)(2,1)S(1)} async-done(((bf16[64,24,128]{2,1,0:T(8,128)(2,1)}), bf16[64,24,128]{2,1,0:T(8,128)(2,1)S(1)}, u32[]{:S(2)}, u32[]{:S(2)}) %all-to-all-start.1) | async-done | bytes 393248 | tf_op jit(solution)/shard_map/all_to_all | solution.py:172
  40.7 0.0 copy-done
  40.7 0.0 copy-done.1
  40.7 0.9 %shard_map.66 = bf16[64,8,128]{2,1,0:T(8,128)(2,1)S(1)} custom-call(bf16[512,512]{1,0:T(8,128)(2,1)S(1)} %copy-done, bf16[256,256]{1,0:T(8,128)(2,1)S(1)} %copy-done.1, bf16[64,24,128]{2,1,0:T(8,128)(2,1)S(1)} %all-to-all-done.1.got_ref), custom_call_target="tpu_custom_call" | custom-call | flops 1 | tf_op jit(solution)/shard_map/pallas_call | solution.py:227
  41.6 16.1 %all_to_all.20.y_ref = bf16[64,8,128]{2,1,0:T(8,128)(2,1)S(1)} all-to-all(bf16[64,8,128]{2,1,0:T(8,128)(2,1)S(1)} %shard_map.66), channel_id=1, replica_groups={{36,37,38,39,32,33,34,35,44,45,46,47,40,41,42,43,52,53,54,55,48,49,50,5..., dimensions={0} | all-to-all | bytes 262144 | tf_op jit(solution)/shard_map/all_to_all | solution.py:172
  57.7 0.4 shard_map.69
  58.1 0.0 collective-permute-done.2.far_ref
  58.1 0.3 shard_map.70
  58.4 16.5 %all_to_all.21 = f32[64,4,128]{2,1,0:T(4,128)S(1)} all-to-all(f32[64,4,128]{2,1,0:T(4,128)S(1)} %bitcast.22), channel_id=1, replica_groups={{36,37,38,39,32,33,34,35,44,45,46,47,40,41,42,43,52,53,54,55,48,49,50,5..., dimensions={0} | all-to-all | bytes 262144 | tf_op jit(solution)/shard_map/all_to_all | solution.py:172
  74.9 0.7 shard_map.71
  (6 shorter events, 0.2 us)
Async XLA Ops:
  1.6 8.3 %copy-start.2 = (bf16[64,4,256]{2,1,0:T(4,128)(2,1)S(1)}, bf16[64,4,256]{2,1,0:T(4,128)(2,1)}, u32[]{:S(2)}) copy-start(bf16[64,4,256]{2,1,0:T(4,128)(2,1)} %param.6) | copy-start | bytes 393220
  1.6 13.5 %all-to-all-start = ((bf16[8,80,128]{2,1,0:T(8,128)(2,1)}), bf16[8,80,128]{2,1,0:T(8,128)(2,1)S(1)}, u32[]{:S(2)}, u32[]{:S(2)}) async-start(bf16[8,80,128]{2,1,0:T(8,128)(2,1)} %shard_map.64), calls=%async_computation | async-start | bytes 327680 | tf_op jit(solution)/shard_map/all_to_all | solution.py:195
  9.0 0.7 copy-start.3
  10.0 21.8 %collective-permute-start = (bf16[64,4,256]{2,1,0:T(4,128)(2,1)S(1)}, bf16[64,4,256]{2,1,0:T(4,128)(2,1)S(1)}, u32[]{:S(2)}, u32[]{:S(2)}) collective-permute-start(bf16[64,4,256]{2,1,0:T(4,128)(2,1)S(1)} %broadcast_multiply_fusion), channel_id=1, source_target_pairs={{0,256},{64,320},{128,384},{192,448},{256,0},{320,64},{384,128},{4... | collective-permute-start | bytes 393224 | tf_op jit(solution)/shard_map/ppermute | solution.py:221
  15.9 24.7 %all-to-all-start.1 = ((bf16[64,24,128]{2,1,0:T(8,128)(2,1)}), bf16[64,24,128]{2,1,0:T(8,128)(2,1)S(1)}, u32[]{:S(2)}, u32[]{:S(2)}) async-start(bf16[64,24,128]{2,1,0:T(8,128)(2,1)} %shard_map.65), calls=%async_computation.1 | async-start | bytes 786432 | tf_op jit(solution)/shard_map/all_to_all | solution.py:172
  32.0 8.7 %copy-start = (bf16[512,512]{1,0:T(8,128)(2,1)S(1)}, bf16[512,512]{1,0:T(8,128)(2,1)}, u32[]{:S(2)}) copy-start(bf16[512,512]{1,0:T(8,128)(2,1)} %constant.47.clone.nu_ref) | copy-start | bytes 1572868
  32.0 8.6 %copy-start.1 = (bf16[256,256]{1,0:T(8,128)(2,1)S(1)}, bf16[256,256]{1,0:T(8,128)(2,1)}, u32[]{:S(2)}) copy-start(bf16[256,256]{1,0:T(8,128)(2,1)} %constant.51.l_ref) | copy-start | bytes 393220
  32.0 3.6 %collective-permute-start.1 = (bf16[128,1024]{1,0:T(8,128)(2,1)S(1)}, bf16[128,1024]{1,0:T(8,128)(2,1)S(1)}, u32[]{:S(2)}, u32[]{:S(2)}) collective-permute-start(bf16[128,1024]{1,0:T(8,128)(2,1)S(1)} %shard_map.67.refs_0_), channel_id=1, source_target_pairs={{0,64},{64,0},{128,192},{192,128},{256,320},{320,256},{384,448},{4... | collective-permute-start | bytes 786440 | tf_op jit(solution)/shard_map/ppermute | solution.py:221
  35.6 22.4 %collective-permute-start.2 = (bf16[256,1024]{1,0:T(8,128)(2,1)S(1)}, bf16[256,1024]{1,0:T(8,128)(2,1)S(1)}, u32[]{:S(2)}, u32[]{:S(2)}) collective-permute-start(bf16[256,1024]{1,0:T(8,128)(2,1)S(1)} %shard_map.68.near_ref), channel_id=1, source_target_pairs={{0,128},{64,192},{128,0},{192,64},{256,384},{320,448},{384,256},{4... | collective-permute-start | bytes 1572872 | tf_op jit(solution)/shard_map/ppermute | solution.py:221

commit v11 on v9

--- a/solution.py
+++ b/solution.py
@@ -77,15 +77,20 @@
         out_ref[k, length:] = shard
 
 
-def second_kernel(got_ref, out_ref):
+def second_kernel(got_ref, out_ref, made_ref, sems):
     rows = got_ref.shape[0]
-    groups = out_ref.shape[0]
-    length = groups // rows * LINE
-    each = groups // rows
+    each = out_ref.shape[0] // rows
+    length = each * LINE
+    shard = got_ref[lax.axis_index("rep") ^ ROWS, length:]
+    leave = []
     for k in range(rows):
-        out_ref[k * each : (k + 1) * each, :LINE] = got_ref[k ^ ROWS, :length].reshape(each, LINE, TILE)
-    shard = got_ref[lax.axis_index("rep") ^ ROWS, length:]
-    out_ref[:, LINE:] = jnp.broadcast_to(shard[None], (groups,) + shard.shape)
+        part = pl.ds(k * each, each)
+        made_ref[part, :LINE] = got_ref[k ^ ROWS, :length].reshape(each, LINE, TILE)
+        made_ref[part, LINE:] = jnp.broadcast_to(shard[None], (each,) + shard.shape)
+        leave.append(pltpu.make_async_copy(made_ref.at[part], out_ref.at[part], sems.at[k]))
+        leave[-1].start()
+    for copy in leave:
+        copy.wait()
 
 
 def product_kernel(nu_ref, l_ref, got_ref, out_ref, m_ref, o_ref, y_ref):
@@ -195,9 +200,10 @@
     first = lax.all_to_all(first, "row", 0, 0, tiled=True, axis_index_groups=order)
     sent = pl.pallas_call(
         second_kernel,
-        out_shape=pltpu.VMEM((groups, 3 * line, TILE), BF16),
+        out_shape=jax.ShapeDtypeStruct((groups, 3 * line, TILE), BF16),
         in_specs=[VMEM],
-        out_specs=VMEM,
+        out_specs=pl.BlockSpec(memory_space=pl.ANY),
+        scratch_shapes=[pltpu.VMEM((groups, 3 * line, TILE), BF16), pltpu.SemaphoreType.DMA((rows,))],
     )(held(first))
 
     mu_tile = lax.axis_index(GRID) * mu_block // TILE

time: 76.3 us -> 76.3 us (level)
  no operation moved by 1% of the time
where the time goes in v11:
time: 76.3 us; the launch traced here: 75.8 us
  starting transfers between devices  32.8 us (43%)
  blocking collectives  32.6 us (43%)
  Pallas kernels  4.83 us (6%)
  waiting for transfers between devices  4.36 us (6%)
  local copies, waits for them, and re-layouts  0.91 us (1%)
    all_to_all x2, blocking collectives, exchange(): lax.all_to_all(array, GRID, 0, 0, tiled=True, axis_index_groups=[order])  32.6 us
    all_to_all x1, starting transfers between devices, exchange(): lax.all_to_all(array, GRID, 0, 0, tiled=True, axis_index_groups=[order])  15.7 us
    ppermute x3, starting transfers between devices, swap(): return lax.ppermute(array, 'row', [(r, r ^ bit) for r in range(rows)])  9.62 us
    all_to_all x1, starting transfers between devices, body(): lax.all_to_all(first, 'row', 0, 0, tiled=True, axis_index_groups=order)  7.4 us
    all_to_all x1, waiting for transfers between devices, exchange(): lax.all_to_all(array, GRID, 0, 0, tiled=True, axis_index_groups=[order])  2.85 us
    pallas_call x1, Pallas kernels, body(): pl.pallas_call(first_kernel, out_shape=pltpu.VMEM((rows, row_count // row...  1.62 us
  transfers between devices with their start and end apart: 5, of which 2 were waited for; matrix products, arithmetic and copies ran while one was open for 1% of the time, Pallas kernels for 3%

profile of v11, /device:TPU:4, one launch (start us, length us, event | category | flops | bytes accessed | tf_op | source)
XLA Modules:
  0.0 75.8 jit_solution(15579532008228664781)
XLA Ops:
  0.0 1.6 %shard_map.64 = bf16[8,80,128]{2,1,0:T(8,128)(2,1)} custom-call(s32[2,2,4]{2,1,0:T(2,128)} %bitcast.23, s32[2,2,2]{2,1,0:T(2,128)} %green_ref.1, bf16[8,64,128]{2,1,0:T(8,128)(2,1)} %bitcast.21, bf16[16,128]{1,0:T(8,128)(2,1)} %bitcast.24), custom_call_target="tpu_custom_call" | custom-call | tf_op jit(solution)/shard_map/pallas_call | solution.py:193
  1.6 0.0 copy-start.2
  1.6 7.4 %all-to-all-start = ((bf16[8,80,128]{2,1,0:T(8,128)(2,1)}), bf16[8,80,128]{2,1,0:T(8,128)(2,1)S(1)}, u32[]{:S(2)}, u32[]{:S(2)}) async-start(bf16[8,80,128]{2,1,0:T(8,128)(2,1)} %shard_map.64), calls=%async_computation | async-start | bytes 327680 | tf_op jit(solution)/shard_map/all_to_all | solution.py:200
  9.0 0.0 copy-start.3
  9.0 0.7 copy-done.3
  9.7 0.2 fusion
  9.9 0.1 broadcast_bitcast_fusion
  10.0 0.0 copy-done.2
  10.0 0.1 broadcast_multiply_fusion
  10.0 0.1 reshape.30
  10.2 5.1 %collective-permute-start = (bf16[64,1024]{1,0:T(8,128)(2,1)S(1)}, bf16[64,1024]{1,0:T(8,128)(2,1)S(1)}, u32[]{:S(2)}, u32[]{:S(2)}) collective-permute-start(bf16[64,1024]{1,0:T(8,128)(2,1)S(1)} %reshape.31.refs_0_), channel_id=1, source_target_pairs={{0,256},{64,320},{128,384},{192,448},{256,0},{320,64},{384,128},{4... | collective-permute-start | bytes 393224 | tf_op jit(solution)/shard_map/ppermute | solution.py:225
  15.3 0.0 all-to-all-done.got_ref
  15.3 0.8 %shard_map.65 = bf16[64,24,128]{2,1,0:T(8,128)(2,1)} custom-call(bf16[8,80,128]{2,1,0:T(8,128)(2,1)S(1)} %all-to-all-done.got_ref), custom_call_target="tpu_custom_call" | custom-call | tf_op jit(solution)/shard_map/pallas_call | solution.py:201
  16.1 15.7 %all-to-all-start.1 = ((bf16[64,24,128]{2,1,0:T(8,128)(2,1)}), bf16[64,24,128]{2,1,0:T(8,128)(2,1)S(1)}, u32[]{:S(2)}, u32[]{:S(2)}) async-start(bf16[64,24,128]{2,1,0:T(8,128)(2,1)} %shard_map.65), calls=%async_computation.1 | async-start | bytes 786432 | tf_op jit(solution)/shard_map/all_to_all | solution.py:177
  31.9 0.0 collective-permute-done.refs_1_
  31.9 0.0 copy-start
  31.9 0.0 copy-start.1
  31.9 2.1 %collective-permute-start.1 = (bf16[128,1024]{1,0:T(8,128)(2,1)S(1)}, bf16[128,1024]{1,0:T(8,128)(2,1)S(1)}, u32[]{:S(2)}, u32[]{:S(2)}) collective-permute-start(bf16[128,1024]{1,0:T(8,128)(2,1)S(1)} %shard_map.67.refs_0_), channel_id=1, source_target_pairs={{0,64},{64,0},{128,192},{192,128},{256,320},{320,256},{384,448},{4... | collective-permute-start | bytes 786440 | tf_op jit(solution)/shard_map/ppermute | solution.py:225
  34.0 1.5 %collective-permute-done.1.refs_1_ = bf16[128,1024]{1,0:T(8,128)(2,1)S(1)} collective-permute-done((bf16[128,1024]{1,0:T(8,128)(2,1)S(1)}, bf16[128,1024]{1,0:T(8,128)(2,1)S(1)}, u32[]{:S(2)}, u32[]{:S(2)}) %collective-permute-start.1) | collective-permute-done | bytes 262176 | tf_op jit(solution)/shard_map/ppermute | solution.py:225
  35.5 2.5 %collective-permute-start.2 = (bf16[256,1024]{1,0:T(8,128)(2,1)S(1)}, bf16[256,1024]{1,0:T(8,128)(2,1)S(1)}, u32[]{:S(2)}, u32[]{:S(2)}) collective-permute-start(bf16[256,1024]{1,0:T(8,128)(2,1)S(1)} %shard_map.68.near_ref), channel_id=1, source_target_pairs={{0,128},{64,192},{128,0},{192,64},{256,384},{320,448},{384,256},{4... | collective-permute-start | bytes 1572872 | tf_op jit(solution)/shard_map/ppermute | solution.py:225
  38.0 2.8 %all-to-all-done.1.got_ref = bf16[64,24,128]{2,1,0:T(8,128)(2,1)S(1)} async-done(((bf16[64,24,128]{2,1,0:T(8,128)(2,1)}), bf16[64,24,128]{2,1,0:T(8,128)(2,1)S(1)}, u32[]{:S(2)}, u32[]{:S(2)}) %all-to-all-start.1) | async-done | bytes 393248 | tf_op jit(solution)/shard_map/all_to_all | solution.py:177
  40.9 0.0 copy-done
  40.9 0.0 copy-done.1
  40.9 0.9 %shard_map.66 = bf16[64,8,128]{2,1,0:T(8,128)(2,1)S(1)} custom-call(bf16[512,512]{1,0:T(8,128)(2,1)S(1)} %copy-done, bf16[256,256]{1,0:T(8,128)(2,1)S(1)} %copy-done.1, bf16[64,24,128]{2,1,0:T(8,128)(2,1)S(1)} %all-to-all-done.1.got_ref), custom_call_target="tpu_custom_call" | custom-call | flops 1 | tf_op jit(solution)/shard_map/pallas_call | solution.py:231
  41.8 16.1 %all_to_all.20.y_ref = bf16[64,8,128]{2,1,0:T(8,128)(2,1)S(1)} all-to-all(bf16[64,8,128]{2,1,0:T(8,128)(2,1)S(1)} %shard_map.66), channel_id=1, replica_groups={{36,37,38,39,32,33,34,35,44,45,46,47,40,41,42,43,52,53,54,55,48,49,50,5..., dimensions={0} | all-to-all | bytes 262144 | tf_op jit(solution)/shard_map/all_to_all | solution.py:177
  57.9 0.4 shard_map.69
  58.3 0.0 collective-permute-done.2.far_ref
  58.3 0.3 shard_map.70
  58.6 16.5 %all_to_all.21 = f32[64,4,128]{2,1,0:T(4,128)S(1)} all-to-all(f32[64,4,128]{2,1,0:T(4,128)S(1)} %bitcast.19), channel_id=1, replica_groups={{36,37,38,39,32,33,34,35,44,45,46,47,40,41,42,43,52,53,54,55,48,49,50,5..., dimensions={0} | all-to-all | bytes 262144 | tf_op jit(solution)/shard_map/all_to_all | solution.py:177
  75.1 0.7 shard_map.71
  (4 shorter events, 0.1 us)
Async XLA Ops:
  1.6 8.3 %copy-start.2 = (bf16[64,4,256]{2,1,0:T(4,128)(2,1)S(1)}, bf16[64,4,256]{2,1,0:T(4,128)(2,1)}, u32[]{:S(2)}) copy-start(bf16[64,4,256]{2,1,0:T(4,128)(2,1)} %param.6) | copy-start | bytes 393220
  1.6 13.7 %all-to-all-start = ((bf16[8,80,128]{2,1,0:T(8,128)(2,1)}), bf16[8,80,128]{2,1,0:T(8,128)(2,1)S(1)}, u32[]{:S(2)}, u32[]{:S(2)}) async-start(bf16[8,80,128]{2,1,0:T(8,128)(2,1)} %shard_map.64), calls=%async_computation | async-start | bytes 327680 | tf_op jit(solution)/shard_map/all_to_all | solution.py:200
  9.0 0.7 copy-start.3
  10.2 21.7 %collective-permute-start = (bf16[64,1024]{1,0:T(8,128)(2,1)S(1)}, bf16[64,1024]{1,0:T(8,128)(2,1)S(1)}, u32[]{:S(2)}, u32[]{:S(2)}) collective-permute-start(bf16[64,1024]{1,0:T(8,128)(2,1)S(1)} %reshape.31.refs_0_), channel_id=1, source_target_pairs={{0,256},{64,320},{128,384},{192,448},{256,0},{320,64},{384,128},{4... | collective-permute-start | bytes 393224 | tf_op jit(solution)/shard_map/ppermute | solution.py:225
  16.1 24.8 %all-to-all-start.1 = ((bf16[64,24,128]{2,1,0:T(8,128)(2,1)}), bf16[64,24,128]{2,1,0:T(8,128)(2,1)S(1)}, u32[]{:S(2)}, u32[]{:S(2)}) async-start(bf16[64,24,128]{2,1,0:T(8,128)(2,1)} %shard_map.65), calls=%async_computation.1 | async-start | bytes 786432 | tf_op jit(solution)/shard_map/all_to_all | solution.py:177
  31.9 9.0 %copy-start = (bf16[512,512]{1,0:T(8,128)(2,1)S(1)}, bf16[512,512]{1,0:T(8,128)(2,1)}, u32[]{:S(2)}) copy-start(bf16[512,512]{1,0:T(8,128)(2,1)} %constant.47.clone.nu_ref) | copy-start | bytes 1572868
  31.9 9.0 %copy-start.1 = (bf16[256,256]{1,0:T(8,128)(2,1)S(1)}, bf16[256,256]{1,0:T(8,128)(2,1)}, u32[]{:S(2)}) copy-start(bf16[256,256]{1,0:T(8,128)(2,1)} %constant.51.l_ref) | copy-start | bytes 393220
  31.9 3.6 %collective-permute-start.1 = (bf16[128,1024]{1,0:T(8,128)(2,1)S(1)}, bf16[128,1024]{1,0:T(8,128)(2,1)S(1)}, u32[]{:S(2)}, u32[]{:S(2)}) collective-permute-start(bf16[128,1024]{1,0:T(8,128)(2,1)S(1)} %shard_map.67.refs_0_), channel_id=1, source_target_pairs={{0,64},{64,0},{128,192},{192,128},{256,320},{320,256},{384,448},{4... | collective-permute-start | bytes 786440 | tf_op jit(solution)/shard_map/ppermute | solution.py:225
  35.5 22.8 %collective-permute-start.2 = (bf16[256,1024]{1,0:T(8,128)(2,1)S(1)}, bf16[256,1024]{1,0:T(8,128)(2,1)S(1)}, u32[]{:S(2)}, u32[]{:S(2)}) collective-permute-start(bf16[256,1024]{1,0:T(8,128)(2,1)S(1)} %shard_map.68.near_ref), channel_id=1, source_target_pairs={{0,128},{64,192},{128,0},{192,64},{256,384},{320,448},{384,256},{4... | collective-permute-start | bytes 1572872 | tf_op jit(solution)/shard_map/ppermute | solution.py:225
